TPU v7x, 256 devices: a whole 4x4x8 slice. The times are simulated.
256 devices in a mesh: blk: 32 (over x_lo, z, core), sub: 8 (over x_hi, y).
Axes of the slice: x: 4 (x_hi: 2, x_lo: 2; x = x_hi * 2 + x_lo), y: 4, z: 8, core: 2. Of those that a mesh axis runs over, the one named last changes fastest.
Arguments:
- queries: bfloat16 [8, 1024, 768], P('sub', 'blk'), may hold values from -16 to 16
- codes: int32 [8, 96, 32768], P('sub', None, 'blk'), may hold values from 0 to 255
- positives: int32 [8, 1024], P('sub', 'blk'), may hold values from 0 to 32767
- codebook: bfloat16 [96, 8, 256], P('sub'), may hold values from -4 to 4
Outputs:
- query_grad: bfloat16 [8, 1024, 768], P('sub', 'blk')
- codeword_grad: float32 [96, 8, 256], P('sub')
All inputs are finite; a program needn't handle non-finite values.
Results may differ from a plain program's by a relative error of at most 0.0029.
Values may be sent and summed in bfloat16 or wider, within the bound.
No kernel may reach another device: no remote copies, remote signals or barrier semaphores. Data moves between devices by JAX's collectives and lax.ppermute only.
A program may use at most 64 MiB of HBM per device.

v0:
```python
import jax
import jax.numpy as jnp
from jax import lax
from jax.sharding import PartitionSpec as P


def block_size(row_count, limit):
    block_rows = 1
    while block_rows * 2 <= limit and row_count % (block_rows * 2) == 0:
        block_rows = block_rows * 2
    return block_rows


def decode_rows(book, code_rows):
    sub_count = code_rows.shape[0]
    row_count = code_rows.shape[1]
    code_count = book.shape[2]
    block_rows = block_size(row_count, 128)
    block_count = row_count // block_rows
    code_blocks = jnp.transpose(code_rows.reshape(sub_count, block_count, block_rows), (1, 0, 2))

    def decode_block(carry, code_block):
        onehot = (
            code_block[:, :, None] == jnp.arange(code_count, dtype=jnp.int32)[None, None, :]
        ).astype(jnp.bfloat16)
        part_rows = jnp.einsum("mpk,mwk->pmw", onehot, book, preferred_element_type=jnp.float32)
        return (carry, part_rows.reshape(block_rows, -1).astype(jnp.bfloat16))

    _, decoded = lax.scan(decode_block, None, code_blocks)
    return decoded.reshape(row_count, -1)


def codeword_sums(code_rows, grad_cols, code_count):
    sub_count = code_rows.shape[0]
    row_count = code_rows.shape[1]
    sub_width = grad_cols.shape[1] // sub_count
    block_rows = block_size(row_count, max(12288 // sub_count, 1))
    block_count = row_count // block_rows
    code_blocks = jnp.transpose(code_rows.reshape(sub_count, block_count, block_rows), (1, 0, 2))
    grad_blocks = grad_cols.reshape(block_count, block_rows, sub_count, sub_width)

    def add_block(running, pieces):
        code_block, grad_block = pieces
        onehot = (
            code_block[:, :, None] == jnp.arange(code_count, dtype=jnp.int32)[None, None, :]
        ).astype(jnp.bfloat16)
        running = running + jnp.einsum(
            "mpk,pmw->mwk", onehot, grad_block, preferred_element_type=jnp.float32
        )
        return (running, None)

    start_sums = jnp.zeros((sub_count, sub_width, code_count), jnp.float32)
    running, _ = lax.scan(add_block, start_sums, (code_blocks, grad_blocks))
    return running


def per_device(queries, codes, positives, codebook):
    own_queries = queries[0]
    own_codes = codes[0]
    passage_rows = own_codes.shape[1]
    book = lax.all_gather(codebook, "sub", axis=0, tiled=True)
    code_count = book.shape[2]
    passages = decode_rows(book, own_codes)
    wide_passages = passages.astype(jnp.float32)
    piece = lax.all_gather(own_queries, "blk", axis=0, tiled=True)
    tile = lax.dot_general(
        piece, passages, (((1,), (1,)), ((), ())), preferred_element_type=jnp.float32
    )
    peak_piece = jnp.max(tile, axis=1)
    total_piece = jnp.sum(jnp.exp(tile - peak_piece[:, None]), axis=1)
    peaks = peak_piece
    totals = total_piece
    gathered, scores, peaks, totals = (piece, tile, peaks, totals)
    targets = lax.all_gather(positives[0], "blk", axis=0, tiled=True)
    peak_all = lax.pmax(peaks, "blk")
    total_all = lax.psum(totals * jnp.exp(peaks - peak_all), "blk")
    log_total = peak_all + jnp.log(total_all)
    offset = lax.axis_index("blk") * passage_rows
    local_hits = (
        (targets - offset)[:, None] == jnp.arange(passage_rows, dtype=jnp.int32)[None, :]
    ).astype(jnp.float32)
    weights = jnp.exp(scores - log_total[:, None]) - local_hits
    passage_grad = lax.dot_general(
        weights,
        gathered.astype(jnp.float32),
        (((0,), (0,)), ((), ())),
        precision=lax.Precision.HIGHEST,
        preferred_element_type=jnp.float32,
    ).astype(jnp.bfloat16)
    query_sums = lax.psum_scatter(
        jnp.dot(
            weights,
            wide_passages,
            precision=lax.Precision.HIGHEST,
            preferred_element_type=jnp.float32,
        ),
        "blk",
        scatter_dimension=0,
        tiled=True,
    )
    sub_share = own_codes.shape[0] // lax.axis_size("sub")
    local_sums = codeword_sums(own_codes, passage_grad, code_count)
    whole_sums = lax.psum(local_sums, ("blk", "sub"))
    codeword_grad = lax.dynamic_slice_in_dim(
        whole_sums, lax.axis_index("sub") * sub_share, sub_share, 0
    )
    return (query_sums.astype(jnp.bfloat16)[None], codeword_grad)


def solution(mesh):
    placed = (P("sub", "blk", None), P("sub", None, "blk"), P("sub", "blk"), P("sub", None, None))
    return jax.shard_map(
        per_device,
        mesh=mesh,
        in_specs=placed,
        out_specs=(P("sub", "blk", None), P("sub", None, None)),
        check_vma=False,
    )
```

profile of v0, /device:TPU:1, one launch (start us, length us, event | category | flops | bytes accessed | tf_op | source)
XLA Modules:
  0.0 637.6 jit_solution(2935178170909586919)
XLA Ops:
  7.2 0.0 all-gather.4.cloned.1.call-start
  7.2 0.7 all-gather.4.cloned.1.call-update
  7.9 0.0 all-reduce.3.cloned.1.call-start
  8.0 1.1 copy.19
  9.0 0.1 copy.12
  9.1 30.2 %all_gather.9 = bf16[96,8,256]{2,1,0:T(8,128)(2,1)S(1)} all-gather(bf16[12,8,256]{2,1,0:T(8,128)(2,1)} %param.11), channel_id=1, replica_groups=mesh['blk'=32,'sub'=8] {'sub'}, dimensions={0}, use_global_device_ids=true | all-gather | bytes 442368 | tf_op jit(solution)/shard_map/all_gather | solution.py:61
  39.3 1.3 dynamic-slice
  41.2 0.8 bitcast_dynamic-update-slice_fusion
  42.0 23.0 %all-reduce = s32[1024]{0:T(1024)S(1)} all-reduce(s32[1024]{0:T(1024)S(1)} %bitcast_dynamic-update-slice_fusion), channel_id=3, replica_groups=mesh['blk'=32,'sub'=8] {'blk'}, use_global_device_ids=true, to_apply=%add | all-reduce | flops 1024 | bytes 8192
  65.0 28.9 %while.21 = (s32[]{:T(128)}, bf16[8,128,768]{2,1,0:T(8,128)(2,1)S(1)}, s32[8,96,128]{2,1,0:T(8,128)S(1)}, bf16[96,8,256]{2,1,0:T(8,128)(2,1)S(1)}, s32[]{:T(128)}) while((s32[]{:T(128)}, bf16[8,128,768]{2,1,0:T(8,128)(2,1)S(1)}, s32[8,96,128]{2,1,0:T(8,128)S(1)}, bf16[96,8,256]{2,1,0:T(8,128)(2,1)S(1)}, s32[]{:T(128)}) %tuple.45), condition=%wide.region_1.2_spmd, body=%wide.region_0.1_spmd.sunk | while | flops 53575680 | bytes 1523781 | solution.py:29
  65.0 3.4 fusion.29
  68.4 0.2 copy.24
  68.6 3.4 fusion.29
  72.0 0.2 copy.24
  72.3 3.4 fusion.29
  75.7 0.2 copy.24
  75.9 3.4 fusion.29
  79.3 0.2 copy.24
  79.5 3.4 fusion.29
  82.9 0.2 copy.24
  83.1 3.4 fusion.29
  86.5 0.2 copy.24
  86.7 3.4 fusion.29
  90.1 0.2 copy.24
  90.4 3.4 fusion.29
  93.8 0.2 copy.24
  93.9 0.0 copy-start.2
  94.0 0.0 all-gather.4.cloned.1.call-done
  94.0 5.7 fusion.20
  99.7 0.0 copy-done.2
  99.7 55.1 %pmax.7 = f32[1024]{0:T(1024)S(1)} all-reduce(f32[1024]{0:T(1024)S(1)} %get-tuple-element.99), channel_id=1, replica_groups=mesh['blk'=32,'sub'=8] {'blk'}, use_global_device_ids=true, to_apply=%region_3.4 | all-reduce | flops 1024 | bytes 8192 | tf_op jit(solution)/shard_map/pmax | solution.py:75
  154.8 2.8 exponential_reduce_fusion
  157.6 53.0 %psum.14 = f32[1024]{0:T(1024)S(1)} all-reduce(f32[1024]{0:T(1024)S(1)} %exponential_multiply_fusion), channel_id=1, replica_groups=mesh['blk'=32,'sub'=8] {'blk'}, use_global_device_ids=true, to_apply=%region_5.6 | all-reduce | flops 1024 | bytes 8192 | tf_op jit(solution)/shard_map/psum | solution.py:76
  210.6 8.3 %fusion.16 = bf16[1024,768]{1,0:T(8,128)(2,1)S(1)} fusion(f32[1024,1024]{1,0:T(8,128)} %get-tuple-element.100, s32[1024]{0:T(1024)S(1)} %broadcast_subtract_fusion, f32[1024]{0:T(1024)S(1)} %log_add_fusion, bf16[1,1024,768]{2,1,0:T(8,128)(2,1)} %all-gather.4.cloned.1.call-done), kind=kOutput, calls=%fused_computation.24 | convolution fusion | flops 9668657152 | bytes 7348224 | tf_op jit(solution)/shard_map/dot_general | solution.py:83
  219.0 0.8 copy.14
  219.7 0.0 copy-start
  219.7 0.4 copy.22
  220.2 0.2 copy.15
  220.4 0.5 copy-done
  220.9 39.9 %while.22 = (s32[]{:T(128)}, f32[96,8,256]{2,1,0:T(8,128)S(1)}, bf16[8,128,96,8]{1,3,2,0:T(8,128)(2,1)S(1)}, s32[8,96,128]{2,1,0:T(8,128)S(1)}, s32[]{:T(128)}, /*index=5*/s32[]{:T(128)}) while((s32[]{:T(128)}, f32[96,8,256]{2,1,0:T(8,128)S(1)}, bf16[8,128,96,8]{1,3,2,0:T(8,128)(2,1)S(1)}, s32[8,96,128]{2,1,0:T(8,128)S(1)}, ...), condition=%wide.region_8.9_spmd.clone, body=%wide.region_7.8_spmd.clone.sunk | while | flops 53870592 | bytes 1917015 | solution.py:53
  220.9 4.9 fusion.31
  225.8 4.9 fusion.31
  230.8 4.9 fusion.31
  235.8 4.9 fusion.31
  240.8 4.9 fusion.31
  245.8 4.9 fusion.31
  250.8 4.9 fusion.31
  255.8 4.9 fusion.31
  260.7 0.0 copy-start.1
  260.7 0.9 copy-done.1
  261.6 0.0 all-reduce.3.cloned.1.call-update
  261.6 0.0 reduce-scatter.2.cloned.1.call-start
  261.7 9.4 %fusion.11 = f32[1024,768]{1,0:T(8,128)} fusion(bf16[1024,768]{1,0:T(8,128)(2,1)} %bitcast.60, f32[1024,1024]{1,0:T(8,128)} %get-tuple-element.100, s32[1024]{0:T(1024)S(1)} %broadcast_subtract_fusion, f32[1024]{0:T(1024)S(1)} %log_add_fusion), kind=kOutput, calls=%fused_computation.19 | convolution fusion | flops 9667870720 | bytes 8921088 | tf_op jit(solution)/shard_map/dot_general | solution.py:91
  271.1 0.0 reduce-scatter.2.cloned.1.call-update
  271.2 239.4 %all-reduce.3.cloned.1.call-done = f32[96,8,256]{2,1,0:T(8,128)} async-done(((f32[96,8,256]{2,1,0:T(8,128)}), f32[96,8,256]{2,1,0:T(8,128)}) %all-reduce.3.cloned.1.call-update) | async-done | bytes 786448 | tf_op jit(solution)/shard_map/psum | solution.py:103
  510.5 1.5 constant_dynamic-slice_fusion
  512.0 117.5 %reduce-scatter.2.cloned.1.call-done = f32[32,768]{1,0:T(8,128)} async-done(((f32[1024,768]{1,0:T(8,128)}), f32[32,768]{1,0:T(8,128)}) %reduce-scatter.2.cloned.1.call-update) | async-done | bytes 98320 | tf_op jit(solution)/shard_map/reduce_scatter | solution.py:90
  629.6 1.5 convert_bitcast_fusion
  (30 shorter events, 0.3 us)
Async XLA Ops:
  7.2 86.8 %all-gather.4.cloned.1.call-start = ((), (), s32[]{:S(2)}) async-start(), calls=%async_computation.3 | async-start | bytes 1622016 | tf_op jit(solution)/shard_map/all_gather | solution.py:65
  7.9 502.6 %all-reduce.3.cloned.1.call-start = ((), (), s32[]{:S(2)}) async-start(), calls=%async_computation.2 | async-start | bytes 1572864 | tf_op jit(solution)/shard_map/psum | solution.py:103
  93.9 5.7 copy-start.2
  219.7 1.1 copy-start
  260.7 0.9 copy-start.1
  261.6 367.9 %reduce-scatter.2.cloned.1.call-start = ((), (), s32[]{:S(2)}) async-start(), calls=%async_computation.1 | async-start | bytes 3244032 | tf_op jit(solution)/shard_map/reduce_scatter | solution.py:90
Sparse Core Ops, SparseCore 0:
  9.9 68.5 all-gather.3
  261.8 248.6 all-reduce.2
  513.2 116.3 reduce-scatter.1
where the time goes:
time: 641 us; the launch traced here: 638 us
  waiting for transfers between devices  358 us (56%)
  blocking collectives  161 us (25%)
  matrix products  90.2 us (14%)
  between operations  14.5 us (2%)
  local copies, waits for them, and re-layouts  9.02 us (1%)
    psum x1, waiting for transfers between devices, per_device(): whole_sums = lax.psum(local_sums, ('blk', 'sub'))  239 us
    reduce_scatter x1, waiting for transfers between devices, per_device(): lax.psum_scatter(jnp.dot(weights, wide_passages, precision=lax.Precision....  118 us
    pmax x1, blocking collectives, per_device(): peak_all = lax.pmax(peaks, 'blk')  55.1 us
    psum x1, blocking collectives, per_device(): total_all = lax.psum(totals * jnp.exp(peaks - peak_all), 'blk')  53 us
    dot_general x8, matrix products, add_block(): jnp.einsum('mpk,pmw->mwk', onehot, grad_block, preferred_element_type=jnp...  39.5 us
    all_gather x1, blocking collectives, per_device(): book = lax.all_gather(codebook, 'sub', axis=0, tiled=True)  30.2 us
    dot_general x8, matrix products, decode_block(): jnp.einsum('mpk,mwk->pmw', onehot, book, preferred_element_type=jnp.float32)  27.2 us
    unnamed x1, blocking collectives  23 us
  transfers between devices with their start and end apart: 3, of which 2 were waited for; matrix products, arithmetic and copies ran while one was open for 7% of the time, Pallas kernels for 0%

commit v1 on v0

v1 whole, which is shorter than its diff:
```python
import functools

import jax
import jax.numpy as jnp
from jax import lax
from jax.experimental import pallas as pl
from jax.experimental.pallas import tpu as pltpu
from jax.sharding import Mesh, PartitionSpec as P

f32 = jnp.float32
bf16 = jnp.bfloat16
LANES = 128


def decode_kernel(codes_ref, book_ref, out_ref):
    def pair(j, carry):
        rows = []
        for h in range(2):
            m = 2 * j + h
            table = book_ref[m].astype(f32)
            low, high = table[:, :LANES], table[:, LANES:]
            row = codes_ref[pl.ds(m, 1), :]
            parts = []
            for t in range(row.shape[1] // LANES):
                code = jnp.broadcast_to(row[:, t * LANES : (t + 1) * LANES], (8, LANES))
                index = code & (LANES - 1)
                parts.append(
                    jnp.where(
                        code < LANES,
                        jnp.take_along_axis(low, index, axis=1, mode="promise_in_bounds"),
                        jnp.take_along_axis(high, index, axis=1, mode="promise_in_bounds"),
                    )
                )
            rows.append(jnp.concatenate(parts, axis=1))
        out_ref[pl.ds(pl.multiple_of(16 * j, 16), 16), :] = jnp.concatenate(rows, axis=0).astype(bf16)
        return carry

    lax.fori_loop(0, codes_ref.shape[0] // 2, pair, 0, unroll=4)


def as_row(column):
    return jnp.transpose(jnp.broadcast_to(column, (column.shape[0], LANES)))[:1]


def as_column(row):
    return jnp.transpose(jnp.broadcast_to(row, (LANES, row.shape[1])))[:, :1]


def scores_kernel(own_ref, other_ref, passages_ref, positives_ref, scores_ref, stats_ref):
    half = own_ref.shape[0]
    peers = stats_ref.shape[0]
    block = 256
    for b in range(2 * half // block):
        source = own_ref if b * block < half else other_ref
        start = b * block % half
        tile = jnp.dot(source[start : start + block], passages_ref[...], preferred_element_type=f32)
        scores_ref[b * block : (b + 1) * block] = tile
        peak = jnp.max(tile, axis=1, keepdims=True)
        total = jnp.sum(jnp.exp(tile - peak), axis=1, keepdims=True)
        row = as_row(peak + jnp.log(total))
        stats_ref[:, b * block : (b + 1) * block] = jnp.broadcast_to(row, (peers, block))
    stats_ref[:, 2 * half :] = jnp.broadcast_to(positives_ref[...], (peers, LANES))


def transpose_kernel(own_ref, other_ref, out_ref):
    half = own_ref.shape[0]
    out_ref[:, :half] = jnp.transpose(own_ref[...])
    out_ref[:, half:] = jnp.transpose(other_ref[...])


def weights_kernel(
    place_ref, scores_ref, stats_ref, turned_ref, codes_ref, high_ref, low_ref, sums_ref, grads_ref
):
    core, offset = place_ref[0], place_ref[1]
    query_count, passage_count = scores_ref.shape
    half = query_count // 2
    peers = stats_ref.shape[0]
    chips = peers // 2
    size = half // chips
    first, second = stats_ref[:, :half], stats_ref[:, half : 2 * half]
    same = (lax.broadcasted_iota(jnp.int32, (peers, half), 0) & 1) == core
    targets = jnp.concatenate([stats_ref[:, 2 * half :], jnp.zeros((LANES - peers, LANES), f32)], axis=0)
    targets = jnp.transpose(targets)[:size].astype(jnp.int32)
    spot = lax.broadcasted_iota(jnp.int32, (size, passage_count), 1) + offset
    for h in range(2):
        logs = jnp.where(same, first, second) if h == 0 else jnp.where(same, second, first)
        peak = jnp.max(logs, axis=0, keepdims=True)
        log_total = as_column(peak + jnp.log(jnp.sum(jnp.exp(logs - peak), axis=0, keepdims=True)))
        for c in range(chips):
            rows = slice(h * half + c * size, h * half + (c + 1) * size)
            target = jnp.where(core == h, targets[:, 2 * c : 2 * c + 1], targets[:, 2 * c + 1 : 2 * c + 2])
            weight = jnp.exp(scores_ref[rows] - log_total[c * size : (c + 1) * size])
            weight = weight - jnp.where(target == spot, 1.0, 0.0)
            high = weight.astype(bf16)
            high_ref[rows] = high
            low_ref[rows] = (weight - high.astype(f32)).astype(bf16)
    block = 256
    for b in range(turned_ref.shape[0] // block):
        part = turned_ref[b * block : (b + 1) * block]
        grads_ref[b * block : (b + 1) * block] = jnp.dot(
            part, high_ref[...], preferred_element_type=f32
        ) + jnp.dot(part, low_ref[...], preferred_element_type=f32)

    word = lax.broadcasted_iota(jnp.int32, (LANES, passage_count), 0)

    def subspace(m, carry):
        grad = grads_ref[pl.ds(pl.multiple_of(8 * m, 8), 8), :]
        code = codes_ref[pl.ds(m, 1), :]
        split = code < LANES
        both = jnp.concatenate([jnp.where(split, grad, 0.0), jnp.where(split, 0.0, grad)], axis=0).astype(bf16)
        onehot = jnp.where((code & (LANES - 1)) == word, 1.0, 0.0).astype(bf16)
        sums = lax.dot_general(both, onehot, (((1,), (1,)), ((), ())), preferred_element_type=f32)
        sums_ref[m, :, :LANES] = sums[:8]
        sums_ref[m, :, LANES:] = sums[8:]
        return carry

    lax.fori_loop(0, codes_ref.shape[0], subspace, 0, unroll=2)


def query_kernel(high_ref, low_ref, passages_ref, own_ref, other_ref):
    half = own_ref.shape[0]
    block = 256
    dims = (((1,), (1,)), ((), ()))
    for b in range(2 * half // block):
        rows = slice(b * block, (b + 1) * block)
        part = lax.dot_general(
            high_ref[rows], passages_ref[...], dims, preferred_element_type=f32
        ) + lax.dot_general(low_ref[rows], passages_ref[...], dims, preferred_element_type=f32)
        start = b * block % half
        if b * block < half:
            own_ref[start : start + block] = part
        else:
            other_ref[start : start + block] = part


def call(kernel, shapes, args, flops, scratch=(), scalars=False, vmem=40):
    specs = [pl.BlockSpec(memory_space=pltpu.VMEM)] * len(args)
    if scalars:
        specs[0] = pl.BlockSpec(memory_space=pltpu.SMEM)
    many = isinstance(shapes, list)
    return pl.pallas_call(
        kernel,
        out_shape=shapes,
        in_specs=specs,
        out_specs=[pl.BlockSpec(memory_space=pltpu.VMEM)] * len(shapes) if many else pl.BlockSpec(memory_space=pltpu.VMEM),
        scratch_shapes=scratch,
        compiler_params=pltpu.CompilerParams(vmem_limit_bytes=vmem * 2**20),
        cost_estimate=pl.CostEstimate(flops=flops, bytes_accessed=4 * 2**20, transcendentals=0),
    )(*args)


CHIP = ("xl", "z")
SUB = ("xh", "y")


def spread(value, axes):
    peers = lax.axis_size(axes)
    copies = jnp.broadcast_to(value[None], (peers, *value.shape))
    return lax.all_to_all(copies, axes, 0, 0)


def per_device(queries, codes, positives, codebook):
    swap = functools.partial(lax.ppermute, axis_name="core", perm=[(0, 1), (1, 0)])
    shape = jax.ShapeDtypeStruct
    own_codes = codes[0]
    subspaces, passage_count = own_codes.shape
    width = queries.shape[2]
    core = lax.axis_index("core")
    offset = lax.axis_index(("xl", "z", "core")) * passage_count
    place = jnp.stack([core, offset]).astype(jnp.int32)
    book = spread(codebook, SUB).reshape(subspaces, *codebook.shape[1:])
    own = spread(queries[0], CHIP).reshape(-1, width)
    passages = call(decode_kernel, shape((width, passage_count), bf16), (own_codes, book), 10**9)
    other = swap(own)
    half = own.shape[0]
    targets = jnp.pad(positives.astype(f32), ((0, 0), (0, LANES - positives.shape[1])))
    scores, stats = call(
        scores_kernel,
        [shape((2 * half, passage_count), f32), shape((32, 2 * half + LANES), f32)],
        (own, other, passages, targets),
        2 * 10**9,
    )
    stats = lax.all_to_all(stats, CHIP + ("core",), 0, 0, tiled=True)
    turned = call(transpose_kernel, shape((width, 2 * half), bf16), (own, other), 10**9)
    high, low, sums = call(
        weights_kernel,
        [
            shape((2 * half, passage_count), bf16),
            shape((2 * half, passage_count), bf16),
            shape((subspaces, 8, 256), f32),
        ],
        (place, scores, stats, turned, own_codes),
        8 * 10**9,
        scratch=[pltpu.VMEM((width, passage_count), f32)],
        scalars=True,
    )
    parts = sums.reshape(8, 2, subspaces // 16, 8, 256)
    parts = jnp.swapaxes(parts, 0, 1).reshape(16, subspaces // 16, 8, 256)
    parts = jnp.sum(lax.all_to_all(parts, ("core",) + SUB, 0, 0), axis=0)
    query_own, query_other = call(
        query_kernel,
        [shape((half, width), f32), shape((half, width), f32)],
        (high, low, passages),
        4 * 10**9,
    )
    query_sums = query_own + swap(query_other)
    query_sums = lax.all_to_all(query_sums.reshape(16, half // 16, width), CHIP, 0, 0)
    query_grad = jnp.sum(query_sums, axis=0).astype(bf16)
    parts = jnp.sum(spread(parts, CHIP), axis=0)
    cross = swap(parts)
    codeword_grad = jnp.concatenate(
        [jnp.where(core == 0, parts, cross), jnp.where(core == 0, cross, parts)], axis=0
    )
    return query_grad[None], codeword_grad


def solution(mesh):
    split = Mesh(mesh.devices.reshape(2, 8, 2, 2, 4), ("xl", "z", "core", "xh", "y"))
    blk = ("xl", "z", "core")
    return jax.shard_map(
        per_device,
        mesh=split,
        in_specs=(P(SUB, blk, None), P(SUB, None, blk), P(SUB, blk), P(SUB, None, None)),
        out_specs=(P(SUB, blk, None), P(SUB, None, None)),
        check_vma=False,
    )
```

time: 641 us -> 190 us (0.30)
  waiting for transfers between devices: 358 us -> 73.7 us
  blocking collectives: 161 us -> 30.1 us
  matrix products: 90.2 us -> 0 us
  starting transfers between devices: 0.12 us -> 32.1 us
  Pallas kernels: 0 us -> 27.1 us
  between operations: 14.5 us -> 0.8 us
  local copies, waits for them, and re-layouts: 9.02 us -> 18.4 us
    psum x1 -> x0, waiting for transfers between devices: 239 us -> none  [per_device(): whole_sums = lax.psum(local_sums, ('blk', 'sub'))]
    reduce_scatter x1 -> x0, waiting for transfers between devices: 118 us -> none  [per_device(): lax.psum_scatter(jnp.dot(weights, wide_passages, precision=lax.Precision....]
    dot_general x19 -> x0, matrix products: 90.2 us -> none  [the longest x8 39.5 us: add_block(): jnp.einsum('mpk,pmw->mwk', onehot, grad_block, preferred_element_type=jnp...]
    all_to_all x0 -> x5, waiting for transfers between devices: none -> 72.8 us  [the longest x1 32.7 us: per_device(): lax.all_to_all(query_sums.reshape(16, half // 16, width), CHIP, 0, 0)]
    pmax x1 -> x0, blocking collectives: 55.1 us -> none  [per_device(): peak_all = lax.pmax(peaks, 'blk')]
    psum x1 -> x0, blocking collectives: 53 us -> none  [per_device(): total_all = lax.psum(totals * jnp.exp(peaks - peak_all), 'blk')]
    all_gather x1 -> x0, blocking collectives: 30.2 us -> none  [per_device(): book = lax.all_gather(codebook, 'sub', axis=0, tiled=True)]
    all_to_all x0 -> x1, blocking collectives: none -> 30.1 us  [spread(): return lax.all_to_all(copies, axes, 0, 0)]
  transfers between devices with their start and end apart: 3 -> 8, of which waited for: 2 -> 6; matrix products, arithmetic and copies ran while one was open for 7% -> 4% of each run, Pallas kernels for 0% -> 4%
where the time goes in v1:
time: 190 us; the launch traced here: 189 us
  waiting for transfers between devices  73.7 us (39%)
  starting transfers between devices  32.1 us (17%)
  blocking collectives  30.1 us (16%)
  Pallas kernels  27.1 us (14%)
  local copies, waits for them, and re-layouts  18.4 us (10%)
  other arithmetic  6.54 us (3%)
    all_to_all x1, waiting for transfers between devices, per_device(): lax.all_to_all(query_sums.reshape(16, half // 16, width), CHIP, 0, 0)  32.7 us
    all_to_all x1, blocking collectives, spread(): return lax.all_to_all(copies, axes, 0, 0)  30.1 us
    pallas_call x5, Pallas kernels, call(): pl.pallas_call(kernel, out_shape=shapes, in_specs=specs, out_specs=[pl.Bl...  27.1 us
    all_to_all x2, waiting for transfers between devices, spread(): return lax.all_to_all(copies, axes, 0, 0)  26 us
    unnamed x27, local copies, waits for them, and re-layouts  14 us
    all_to_all x2, starting transfers between devices, spread(): return lax.all_to_all(copies, axes, 0, 0)  10.6 us
    all_to_all x1, waiting for transfers between devices, per_device(): stats = lax.all_to_all(stats, CHIP + ('core',), 0, 0, tiled=True)  7.54 us
    all_to_all x1, waiting for transfers between devices, per_device(): parts = jnp.sum(lax.all_to_all(parts, ('core',) + SUB, 0, 0), axis=0)  6.62 us
  transfers between devices with their start and end apart: 8, of which 6 were waited for; matrix products, arithmetic and copies ran while one was open for 4% of the time, Pallas kernels for 4%

profile of v1, /device:TPU:1, one launch (start us, length us, event | category | flops | bytes accessed | tf_op | source)
XLA Modules:
  0.0 188.7 jit_solution(3508933886590235381)
XLA Ops:
  0.6 0.0 copy-start.11
  0.6 0.9 broadcast_in_dim.9
  1.5 0.0 copy-start.12
  1.5 0.0 copy-start
  1.6 30.1 %all_to_all.36 = bf16[16,32,768]{2,1,0:T(8,128)(2,1)S(1)} all-to-all(bf16[16,32,768]{2,1,0:T(8,128)(2,1)S(1)} %broadcast_in_dim.9), channel_id=1, replica_groups=mesh['xl'=2,'z'=8,'core'=2,'xh'=2,'y'=4] {'xl','z'}, dimensions={0} | all-to-all | bytes 1572864 | tf_op jit(solution)/shard_map/all_to_all | solution.py:159
  31.6 2.2 %collective-permute-start = (bf16[512,768]{1,0:T(8,128)(2,1)S(1)}, bf16[512,768]{1,0:T(8,128)(2,1)S(1)}, u32[]{:S(2)}, u32[]{:S(2)}) collective-permute-start(bf16[512,768]{1,0:T(8,128)(2,1)S(1)} %bitcast.18), channel_id=1, source_target_pairs={{0,8},{8,0},{1,9},{9,1},{2,10},{10,2},{3,11},{11,3},{4,12},{12,4},... | collective-permute-start | bytes 2359304 | tf_op jit(solution)/shard_map/ppermute | solution.py:174
  33.9 0.0 copy-done.11
  33.9 0.8 broadcast_in_dim.10
  34.6 6.4 %all-to-all-start.1 = ((bf16[8,12,8,256]{3,2,1,0:T(8,128)(2,1)}), bf16[8,12,8,256]{3,2,1,0:T(8,128)(2,1)S(1)}, u32[]{:S(2)}, u32[]{:S(2)}) async-start(bf16[8,12,8,256]{3,2,1,0:T(8,128)(2,1)} %broadcast_in_dim.10), calls=%async_computation.1 | async-start | bytes 786432 | tf_op jit(solution)/shard_map/all_to_all | solution.py:159
  41.0 0.0 copy-done.12
  41.0 9.0 %all-to-all-done.1 = bf16[8,12,8,256]{3,2,1,0:T(8,128)(2,1)S(1)} async-done(((bf16[8,12,8,256]{3,2,1,0:T(8,128)(2,1)}), bf16[8,12,8,256]{3,2,1,0:T(8,128)(2,1)S(1)}, u32[]{:S(2)}, u32[]{:S(2)}) %all-to-all-start.1) | async-done | bytes 393248 | tf_op jit(solution)/shard_map/all_to_all | solution.py:159
  50.0 0.0 copy-done
  50.0 3.0 %shard_map.59.passages_ref = bf16[768,1024]{1,0:T(8,128)(2,1)S(1)} custom-call(s32[96,1024]{1,0:T(8,128)S(1)} %bitcast.25, bf16[96,8,256]{2,1,0:T(8,128)(2,1)S(1)} %bitcast.22), custom_call_target="tpu_custom_call" | custom-call | flops 1000000000 | bytes 4194304 | tf_op jit(solution)/shard_map/pallas_call | solution.py:141
  53.0 0.0 copy-start.3
  53.0 0.0 collective-permute-done.other_ref
  53.0 2.3 %shard_map.60 = (f32[1024,1024]{1,0:T(8,128)S(1)}, f32[32,1152]{1,0:T(8,128)S(1)}) custom-call(bf16[512,768]{1,0:T(8,128)(2,1)S(1)} %bitcast.19, bf16[512,768]{1,0:T(8,128)(2,1)S(1)} %collective-permute-done.other_ref, bf16[768,1024]{1,0:T(8,128)(2,1)S(1)} %shard_map.59.passages_ref, f32[1,128]{1,0:T(1,128)S(1)} %pad.4.positives_ref), custom_call_target="tpu_custom_call" | custom-call | flops 2000000000 | bytes 4194304 | tf_op jit(solution)/shard_map/pallas_call | solution.py:141
  55.3 0.0 copy-done.3
  55.3 0.0 copy-start.5
  55.3 1.9 %copy-done.5 = f32[1024,1024]{1,0:T(8,128)} copy-done((f32[1024,1024]{1,0:T(8,128)}, f32[1024,1024]{1,0:T(8,128)S(1)}, u32[]{:S(2)}) %copy-start.5) | copy-done | bytes 4194328
  57.3 0.8 copy.9
  58.1 6.0 %all-to-all-start.2 = ((f32[32,1,1152]{2,1,0:T(1,128)}), f32[32,1,1152]{2,1,0:T(1,128)S(1)}, u32[]{:S(2)}, u32[]{:S(2)}) async-start(f32[32,1,1152]{2,1,0:T(1,128)} %copy.9), calls=%async_computation.2 | async-start | bytes 294912 | tf_op jit(solution)/shard_map/all_to_all | solution.py:183
  64.1 0.1 pad_add_fusion.place_ref
  64.2 0.5 shard_map.61.turned_ref
  64.7 0.0 copy-start.1
  64.7 1.2 copy-done.1
  65.9 7.5 %all-to-all-done.2 = f32[32,1,1152]{2,1,0:T(1,128)S(1)} async-done(((f32[32,1,1152]{2,1,0:T(1,128)}), f32[32,1,1152]{2,1,0:T(1,128)S(1)}, u32[]{:S(2)}, u32[]{:S(2)}) %all-to-all-start.2) | async-done | bytes 147488 | tf_op jit(solution)/shard_map/all_to_all | solution.py:183
  73.4 0.0 copy-start.2
  73.4 1.4 copy-done.2
  74.8 0.0 copy-start.6
  74.8 2.2 %copy-done.6 = f32[1024,1024]{1,0:T(8,128)S(1)} copy-done((f32[1024,1024]{1,0:T(8,128)S(1)}, f32[1024,1024]{1,0:T(8,128)}, u32[]{:S(2)}) %copy-start.6) | copy-done | bytes 4194328
  77.0 17.8 %shard_map.62 = (bf16[1024,1024]{1,0:T(8,128)(2,1)S(1)}, bf16[1024,1024]{1,0:T(8,128)(2,1)S(1)}, f32[96,8,256]{2,1,0:T(8,128)S(1)}) custom-call(s32[2]{0:T(128)S(1)} %pad_add_fusion.place_ref, f32[1024,1024]{1,0:T(8,128)S(1)} %copy-done.6, f32[32,1152]{1,0:T(8,128)S(1)} %bitcast.23, bf16[768,1024]{1,0:T(8,128)(2,1)S(1)} %copy-done.2, s32[96,1024]{1,0:T(8,128)S(1)} %bitcast.26), custom_call_target="tpu_custom_call" | custom-call | flops 8000000000 | bytes 4194304 | tf_op jit(solution)/shard_map/pallas_call | solution.py:141
  94.8 0.0 copy-start.7
  94.9 1.3 copy-done.7
  96.2 0.0 copy-start.9
  96.2 1.3 copy-done.9
  97.5 0.9 copy.10
  98.4 5.8 %all-to-all-start.4 = ((f32[16,6,8,256]{3,2,1,0:T(8,128)}), f32[16,6,8,256]{3,2,1,0:T(8,128)}, u32[]{:S(2)}, u32[]{:S(2)}) async-start(f32[16,6,8,256]{3,2,1,0:T(8,128)} %bitcast.11), calls=%async_computation.4 | async-start | bytes 1572864 | tf_op jit(solution)/shard_map/all_to_all | solution.py:199
  104.2 0.0 copy-start.4
  104.2 1.4 copy-done.4
  105.6 0.0 copy-start.8
  105.7 1.6 copy-done.8
  107.2 0.0 copy-start.10
  107.2 1.6 copy-done.10
  108.8 3.4 %shard_map.63 = (f32[512,768]{1,0:T(8,128)S(1)}, f32[512,768]{1,0:T(8,128)S(1)}) custom-call(bf16[1024,1024]{1,0:T(8,128)(2,1)S(1)} %copy-done.8, bf16[1024,1024]{1,0:T(8,128)(2,1)S(1)} %copy-done.10, bf16[768,1024]{1,0:T(8,128)(2,1)S(1)} %copy-done.4), custom_call_target="tpu_custom_call" | custom-call | flops 4000000000 | bytes 4194304 | tf_op jit(solution)/shard_map/pallas_call | solution.py:141
  112.3 0.3 collective-permute-start.1
  112.6 6.6 %all-to-all-done.4 = f32[16,6,8,256]{3,2,1,0:T(8,128)} async-done(((f32[16,6,8,256]{3,2,1,0:T(8,128)}), f32[16,6,8,256]{3,2,1,0:T(8,128)}, u32[]{:S(2)}, u32[]{:S(2)}) %all-to-all-start.4) | async-done | bytes 786464 | tf_op jit(solution)/shard_map/all_to_all | solution.py:199
  119.2 1.2 reduce_sum.28
  120.4 1.0 broadcast_in_dim.11
  121.4 4.3 %all-to-all-start.5 = ((f32[16,6,8,256]{3,2,1,0:T(8,128)}), f32[16,6,8,256]{3,2,1,0:T(8,128)}, u32[]{:S(2)}, u32[]{:S(2)}) async-start(f32[16,6,8,256]{3,2,1,0:T(8,128)} %broadcast_in_dim.11), calls=%async_computation.5 | async-start | bytes 1572864 | tf_op jit(solution)/shard_map/all_to_all | solution.py:159
  125.7 0.0 collective-permute-done.1
  125.7 2.7 %add.13 = f32[512,768]{1,0:T(8,128)} add(f32[512,768]{1,0:T(8,128)S(1)} %get-tuple-element.13, f32[512,768]{1,0:T(8,128)} %collective-permute-done.1) | non-fusion elementwise | flops 393216 | bytes 4718592 | tf_op jit(solution)/shard_map/add | solution.py:206
  128.4 17.0 %all-to-all-done.5 = f32[16,6,8,256]{3,2,1,0:T(8,128)} async-done(((f32[16,6,8,256]{3,2,1,0:T(8,128)}), f32[16,6,8,256]{3,2,1,0:T(8,128)}, u32[]{:S(2)}, u32[]{:S(2)}) %all-to-all-start.5) | async-done | bytes 786464 | tf_op jit(solution)/shard_map/all_to_all | solution.py:159
  145.4 6.3 %all-to-all-start.3 = ((f32[16,32,768]{2,1,0:T(8,128)}), f32[16,32,768]{2,1,0:T(8,128)S(1)}, u32[]{:S(2)}, u32[]{:S(2)}) async-start(f32[16,32,768]{2,1,0:T(8,128)} %bitcast.7), calls=%async_computation.3 | async-start | bytes 3145728 | tf_op jit(solution)/shard_map/all_to_all | solution.py:207
  151.7 1.2 reduce_sum.29
  152.9 0.9 collective-permute-start.2
  153.8 0.9 collective-permute-done.2
  154.7 0.6 pad_maximum_fusion
  155.3 32.7 %all-to-all-done.3 = f32[16,32,768]{2,1,0:T(8,128)S(1)} async-done(((f32[16,32,768]{2,1,0:T(8,128)}), f32[16,32,768]{2,1,0:T(8,128)S(1)}, u32[]{:S(2)}, u32[]{:S(2)}) %all-to-all-start.3) | async-done | bytes 1572896 | tf_op jit(solution)/shard_map/all_to_all | solution.py:207
  188.0 0.7 reduce_sum.27
  (4 shorter events, 0.0 us)
Async XLA Ops:
  0.6 33.2 %copy-start.11 = (bf16[12,8,256]{2,1,0:T(8,128)(2,1)S(1)}, bf16[12,8,256]{2,1,0:T(8,128)(2,1)}, u32[]{:S(2)}) copy-start(bf16[12,8,256]{2,1,0:T(8,128)(2,1)} %param.7) | copy-start | bytes 147460
  1.5 39.5 %copy-start.12 = (s32[1,32]{1,0:T(1,128)S(1)}, s32[1,32]{1,0:T(1,128)}, u32[]{:S(2)}) copy-start(s32[1,32]{1,0:T(1,128)} %param.6) | copy-start | bytes 388
  1.5 48.4 %copy-start = (s32[1,96,1024]{2,1,0:T(8,128)S(1)}, s32[1,96,1024]{2,1,0:T(8,128)}, u32[]{:S(2)}) copy-start(s32[1,96,1024]{2,1,0:T(8,128)} %param.5) | copy-start | bytes 1179652
  31.6 21.4 %collective-permute-start = (bf16[512,768]{1,0:T(8,128)(2,1)S(1)}, bf16[512,768]{1,0:T(8,128)(2,1)S(1)}, u32[]{:S(2)}, u32[]{:S(2)}) collective-permute-start(bf16[512,768]{1,0:T(8,128)(2,1)S(1)} %bitcast.18), channel_id=1, source_target_pairs={{0,8},{8,0},{1,9},{9,1},{2,10},{10,2},{3,11},{11,3},{4,12},{12,4},... | collective-permute-start | bytes 2359304 | tf_op jit(solution)/shard_map/ppermute | solution.py:174
  34.6 15.3 %all-to-all-start.1 = ((bf16[8,12,8,256]{3,2,1,0:T(8,128)(2,1)}), bf16[8,12,8,256]{3,2,1,0:T(8,128)(2,1)S(1)}, u32[]{:S(2)}, u32[]{:S(2)}) async-start(bf16[8,12,8,256]{3,2,1,0:T(8,128)(2,1)} %broadcast_in_dim.10), calls=%async_computation.1 | async-start | bytes 786432 | tf_op jit(solution)/shard_map/all_to_all | solution.py:159
  53.0 2.3 %copy-start.3 = (bf16[768,1024]{1,0:T(8,128)(2,1)}, bf16[768,1024]{1,0:T(8,128)(2,1)S(1)}, u32[]{:S(2)}) copy-start(bf16[768,1024]{1,0:T(8,128)(2,1)S(1)} %shard_map.59.passages_ref) | copy-start | bytes 4718596
  55.3 1.9 %copy-start.5 = (f32[1024,1024]{1,0:T(8,128)}, f32[1024,1024]{1,0:T(8,128)S(1)}, u32[]{:S(2)}) copy-start(f32[1024,1024]{1,0:T(8,128)S(1)} %get-tuple-element.9.scores_ref) | copy-start | bytes 12582916
  58.1 15.3 %all-to-all-start.2 = ((f32[32,1,1152]{2,1,0:T(1,128)}), f32[32,1,1152]{2,1,0:T(1,128)S(1)}, u32[]{:S(2)}, u32[]{:S(2)}) async-start(f32[32,1,1152]{2,1,0:T(1,128)} %copy.9), calls=%async_computation.2 | async-start | bytes 294912 | tf_op jit(solution)/shard_map/all_to_all | solution.py:183
  64.7 1.2 copy-start.1
  73.4 1.4 copy-start.2
  74.8 2.2 %copy-start.6 = (f32[1024,1024]{1,0:T(8,128)S(1)}, f32[1024,1024]{1,0:T(8,128)}, u32[]{:S(2)}) copy-start(f32[1024,1024]{1,0:T(8,128)} %copy-done.5) | copy-start | bytes 12582916
  94.8 1.3 copy-start.7
  96.2 1.3 copy-start.9
  98.4 20.8 %all-to-all-start.4 = ((f32[16,6,8,256]{3,2,1,0:T(8,128)}), f32[16,6,8,256]{3,2,1,0:T(8,128)}, u32[]{:S(2)}, u32[]{:S(2)}) async-start(f32[16,6,8,256]{3,2,1,0:T(8,128)} %bitcast.11), calls=%async_computation.4 | async-start | bytes 1572864 | tf_op jit(solution)/shard_map/all_to_all | solution.py:199
  104.2 1.4 copy-start.4
  105.6 1.6 copy-start.8
  107.2 1.6 copy-start.10
  112.3 13.4 %collective-permute-start.1 = (f32[512,768]{1,0:T(8,128)S(1)}, f32[512,768]{1,0:T(8,128)}, u32[]{:S(2)}, u32[]{:S(2)}) collective-permute-start(f32[512,768]{1,0:T(8,128)S(1)} %get-tuple-element.14), channel_id=1, source_target_pairs={{0,8},{8,0},{1,9},{9,1},{2,10},{10,2},{3,11},{11,3},{4,12},{12,4},... | collective-permute-start | bytes 4718600 | tf_op jit(solution)/shard_map/ppermute | solution.py:206
  121.4 24.0 %all-to-all-start.5 = ((f32[16,6,8,256]{3,2,1,0:T(8,128)}), f32[16,6,8,256]{3,2,1,0:T(8,128)}, u32[]{:S(2)}, u32[]{:S(2)}) async-start(f32[16,6,8,256]{3,2,1,0:T(8,128)} %broadcast_in_dim.11), calls=%async_computation.5 | async-start | bytes 1572864 | tf_op jit(solution)/shard_map/all_to_all | solution.py:159
  145.4 42.6 %all-to-all-start.3 = ((f32[16,32,768]{2,1,0:T(8,128)}), f32[16,32,768]{2,1,0:T(8,128)S(1)}, u32[]{:S(2)}, u32[]{:S(2)}) async-start(f32[16,32,768]{2,1,0:T(8,128)} %bitcast.7), calls=%async_computation.3 | async-start | bytes 3145728 | tf_op jit(solution)/shard_map/all_to_all | solution.py:207
  152.9 1.8 collective-permute-start.2

commit v2 on v0

v2 whole, which is shorter than its diff:
```python
import functools

import jax
import jax.numpy as jnp
from jax import lax
from jax.experimental import pallas as pl
from jax.experimental.pallas import tpu as pltpu
from jax.sharding import Mesh, PartitionSpec as P

f32 = jnp.float32
bf16 = jnp.bfloat16
i32 = jnp.int32
i16 = jnp.int16
LANES = 128
BLOCK = 256
CHIP = ("xl", "z")
SUB = ("xh", "y")
ROWS_BY_ROWS = (((1,), (1,)), ((), ()))


def as_column(row):
    return jnp.transpose(jnp.broadcast_to(row, (LANES, row.shape[1])))[:, :1]


def as_row(column):
    return jnp.transpose(jnp.broadcast_to(column, (column.shape[0], LANES)))[:1]


def exponents(rows):
    peak = jnp.maximum(jnp.max(jnp.abs(rows), axis=1, keepdims=True), 2.0**-100)
    return jnp.ceil(jnp.log2(peak * (1.0 / 32767.0)))


def as_words(rows, exponent):
    scaled = jnp.round(rows * jnp.exp2(-exponent))
    return jnp.clip(scaled, -32767.0, 32767.0).astype(i32).astype(i16)


def exponent_rows(exponent):
    column = jnp.concatenate([exponent, jnp.zeros((LANES - exponent.shape[0], 1), f32)], axis=0)
    return jnp.transpose(jnp.broadcast_to(column, (LANES, LANES)))[:16].astype(i32).astype(i16)


def scale_column(rows, count):
    row = rows.astype(i32).astype(f32)[:1]
    return jnp.exp2(jnp.transpose(jnp.broadcast_to(row, (LANES, LANES)))[:count])


def spread_kernel(queries_ref, positives_ref, out_ref):
    size, width = queries_ref.shape
    target = positives_ref[...]
    tail = jnp.concatenate([target // LANES, target % LANES, jnp.zeros((14, LANES), i32)], axis=0)
    tail = tail.astype(f32).astype(bf16)
    for c in range(out_ref.shape[0]):
        for t in range(width // LANES):
            out_ref[c, t * size : (t + 1) * size] = queries_ref[:, t * LANES : (t + 1) * LANES]
        out_ref[c, width // LANES * size :] = tail


def query_columns(pack_ref, t, first, count):
    size = (pack_ref.shape[1] - 16) // 6
    return pack_ref[first : first + count, t * size : (t + 1) * size, :].reshape(count * size, LANES)


def query_rows(pack_ref, first, count):
    return jnp.concatenate([query_columns(pack_ref, t, first, count) for t in range(6)], axis=1)


def target_columns(pack_ref):
    chips, length, _ = pack_ref.shape
    tail = pack_ref[:, length - 16 :, :].astype(f32)
    target = tail[:, 0, :] * LANES + tail[:, 1, :]
    target = jnp.concatenate([target, jnp.zeros((LANES - chips, LANES), f32)], axis=0)
    return jnp.transpose(target)


def decode_kernel(place_ref, codes_ref, near_ref, far_ref, out_ref):
    share = near_ref.shape[1]
    far, along = place_ref[2], place_ref[3]

    def table_of(group, member):
        piece = (along + 4 - group % 4) % 4
        near, other = near_ref[piece, member], far_ref[piece, member]
        return jnp.where(group // 4 == far, near, other).astype(f32)

    for group in range(8):

        def pair(j, carry, group=group):
            rows = []
            for h in range(2):
                table = table_of(group, 2 * j + h)
                low, high = table[:, :LANES], table[:, LANES:]
                row = codes_ref[pl.ds(group * share + 2 * j + h, 1), :]
                parts = []
                for t in range(row.shape[1] // LANES):
                    code = jnp.broadcast_to(row[:, t * LANES : (t + 1) * LANES], (8, LANES))
                    index = code & (LANES - 1)
                    parts.append(
                        jnp.where(
                            code < LANES,
                            jnp.take_along_axis(low, index, axis=1, mode="promise_in_bounds"),
                            jnp.take_along_axis(high, index, axis=1, mode="promise_in_bounds"),
                        )
                    )
                rows.append(jnp.concatenate(parts, axis=1))
            start = pl.multiple_of(16 * (group * share // 2 + j), 16)
            out_ref[pl.ds(start, 16), :] = jnp.concatenate(rows, axis=0).astype(bf16)
            return carry

        lax.fori_loop(0, share // 2, pair, 0, unroll=2)


def scores_kernel(own_ref, other_ref, passages_ref, stats_ref):
    for b in range(4):
        rows = query_rows(own_ref if b < 2 else other_ref, b % 2 * 8, 8)
        tile = jnp.dot(rows, passages_ref[...], preferred_element_type=f32)
        peak = jnp.max(tile, axis=1, keepdims=True)
        total = jnp.sum(jnp.exp(tile - peak), axis=1, keepdims=True)
        row = as_row(peak + jnp.log(total))
        for j in range(2):
            piece = row[:, j * LANES : (j + 1) * LANES]
            stats_ref[:, 2 * b + j : 2 * b + j + 1, :] = jnp.broadcast_to(piece[None], (stats_ref.shape[0], 1, LANES))


def log_totals(core, stats_ref, h):
    peers = stats_ref.shape[0]
    same = (lax.broadcasted_iota(i32, (peers, LANES), 0) & 1) == core
    out = []
    for j in range(4):
        logs = jnp.where(same, stats_ref[:, 4 * h + j, :], stats_ref[:, 4 - 4 * h + j, :])
        peak = jnp.max(logs, axis=0, keepdims=True)
        out.append(peak + jnp.log(jnp.sum(jnp.exp(logs - peak), axis=0, keepdims=True)))
    return out


def weights_kernel(
    place_ref, stats_ref, own_ref, other_ref, passages_ref, other_sums_ref, own_sums_ref, grads_ref, high_ref, low_ref
):
    core, offset = place_ref[0], place_ref[1]
    half, passage_count = own_sums_ref.shape[0], passages_ref.shape[1]
    size = half // own_ref.shape[0]
    passages = passages_ref[...]
    spot = lax.broadcasted_iota(i32, (size, passage_count), 1) + offset
    for h, pack_ref, sums_ref in ((1, other_ref, other_sums_ref), (0, own_ref, own_sums_ref)):
        totals = [as_column(row) for row in log_totals(core, stats_ref, h)]
        targets = target_columns(pack_ref)[:size].astype(i32)
        for b in range(half // BLOCK):
            tile = jnp.dot(query_rows(pack_ref, b * 8, 8), passages, preferred_element_type=f32)
            tile = jnp.exp(tile - jnp.concatenate(totals[2 * b : 2 * b + 2], axis=0))
            rows = slice(h * half + b * BLOCK, h * half + (b + 1) * BLOCK)
            pieces = []
            for c in range(BLOCK // size):
                place = b * BLOCK // size + c
                hits = jnp.where(targets[:, place : place + 1] == spot, 1.0, 0.0)
                pieces.append(tile[c * size : (c + 1) * size] - hits)
            weight = jnp.concatenate(pieces, axis=0)
            high = weight.astype(bf16)
            low = (weight - high.astype(f32)).astype(bf16)
            high_ref[rows] = high
            low_ref[rows] = low
            sums_ref[b * BLOCK : (b + 1) * BLOCK] = lax.dot_general(
                high, passages, ROWS_BY_ROWS, preferred_element_type=f32
            ) + lax.dot_general(low, passages, ROWS_BY_ROWS, preferred_element_type=f32)
    chips = own_ref.shape[0]
    for t in range(3):
        turned = jnp.concatenate(
            [
                jnp.concatenate(
                    [jnp.transpose(query_columns(pack_ref, 2 * t + k, 0, chips)) for pack_ref in (own_ref, other_ref)],
                    axis=1,
                )
                for k in range(2)
            ],
            axis=0,
        )
        grad = jnp.dot(turned, high_ref[...], preferred_element_type=f32) + jnp.dot(
            turned, low_ref[...], preferred_element_type=f32
        )
        grads_ref[t * BLOCK : (t + 1) * BLOCK] = grad.astype(bf16)


def codeword_kernel(mine, place_ref, grads_ref, codes_ref, out_ref):
    core = place_ref[0] if mine else 1 - place_ref[0]
    word = lax.broadcasted_iota(i32, (32, codes_ref.shape[1]), 0)

    def four(j, carry):
        sums = []
        for m in range(4):
            grad = grads_ref[pl.ds(pl.multiple_of(32 * j + 16 * (m // 2), 16), 16), :].astype(f32)
            grad = grad[m % 2 * 8 : m % 2 * 8 + 8]
            code = codes_ref[pl.ds(4 * j + m, 1), :]
            high = (code >> 5) - 4 * core
            parts = jnp.concatenate([jnp.where(high == t, grad, 0.0) for t in range(4)], axis=0).astype(bf16)
            onehot = jnp.where((code & 31) == word, 1.0, 0.0).astype(bf16)
            sums.append(lax.dot_general(parts, onehot, ROWS_BY_ROWS, preferred_element_type=f32))
        sums = jnp.concatenate(sums, axis=1)
        for k in range(2):
            out_ref[j // 3, k, j % 3] = sums[16 * k : 16 * k + 16]
        return carry

    lax.fori_loop(0, codes_ref.shape[0] // 4, four, 0, unroll=4)


def put_query_words(chunk, out_ref, c):
    size, width = chunk.shape
    exponent = exponents(chunk)
    words = as_words(chunk, exponent)
    for t in range(width // LANES):
        out_ref[c, t * size : (t + 1) * size] = words[:, t * LANES : (t + 1) * LANES]
    return exponent


def take_query_words(words_ref, c, scale, width):
    size = scale.shape[0]
    words = [words_ref[c, t * size : (t + 1) * size] for t in range(width // LANES)]
    return jnp.concatenate([word.astype(i32).astype(f32) * scale for word in words], axis=1)


def send_kernel(place_ref, sums_ref, cross_ref, out_ref):
    peers = out_ref.shape[0]
    half, width = sums_ref.shape
    size = half // (2 * peers)
    for c in range(peers):
        rows = pl.ds(pl.multiple_of((1 - place_ref[4]) * (half // 2) + c * size, size), size)
        exponent = put_query_words(sums_ref[rows] + cross_ref[rows], out_ref, c)
        out_ref[c, width // LANES * size :] = exponent_rows(exponent)


def pack_kernel(place_ref, sums_ref, cross_ref, words_ref, parts_ref, out_ref):
    peers = out_ref.shape[0]
    half, width = sums_ref.shape
    size = half // (2 * peers)
    base = width // LANES * size
    totals = parts_ref[0]
    for c in range(1, parts_ref.shape[0]):
        totals = totals + parts_ref[c]
    totals = totals.reshape(-1, LANES)
    totals_exponent = exponents(totals)
    totals = as_words(totals, totals_exponent)
    for c in range(peers):
        rows = pl.ds(pl.multiple_of(place_ref[4] * (half // 2) + c * size, size), size)
        received = take_query_words(words_ref, c, scale_column(words_ref[c, base:], size), width)
        exponent = put_query_words(sums_ref[rows] + cross_ref[rows] + received, out_ref, c)
        out_ref[c, base : base + totals.shape[0]] = totals
        out_ref[c, base + totals.shape[0] :] = exponent_rows(jnp.concatenate([exponent, totals_exponent], axis=0))


def unpack_kernel(words_ref, query_ref, sums_ref):
    peers = words_ref.shape[0]
    size, width = query_ref.shape
    base = width // LANES * size
    count = sums_ref.shape[0]
    query, sums = 0.0, 0.0
    for c in range(peers):
        scale = scale_column(words_ref[c, base + count :], size + count)
        query = query + take_query_words(words_ref, c, scale[:size], width)
        sums = sums + words_ref[c, base : base + count].astype(i32).astype(f32) * scale[size:]
    query_ref[...] = query.astype(bf16)
    sums_ref[...] = sums


def join_kernel(place_ref, own_ref, beside_ref, cross_ref, out_ref, all_ref):
    core, side = place_ref[0], place_ref[4]
    count = own_ref.shape[0]
    all_ref[2 * core + side] = own_ref[...]
    all_ref[2 * core + 1 - side] = beside_ref[...]
    all_ref[2 - 2 * core + side] = cross_ref[:count]
    all_ref[2 - 2 * core + 1 - side] = cross_ref[count:]
    for j in range(3):
        rows = [all_ref[t // 2, 16 * j + t % 2 * 8 : 16 * j + t % 2 * 8 + 8] for t in range(8)]
        for m in range(4):
            out_ref[4 * j + m] = jnp.concatenate([row[:, 32 * m : 32 * m + 32] for row in rows], axis=1)


IN_VMEM = pl.BlockSpec(memory_space=pltpu.VMEM)
IN_SMEM = pl.BlockSpec(memory_space=pltpu.SMEM)


def call(kernel, shapes, args, flops, scratch=(), special=None, out_special=None, vmem=12):
    specs = [IN_VMEM] * len(args)
    for place, spec in (special or {}).items():
        specs[place] = spec
    many = isinstance(shapes, list)
    outs = [IN_VMEM] * (len(shapes) if many else 1)
    for place, spec in (out_special or {}).items():
        outs[place] = spec
    return pl.pallas_call(
        kernel,
        out_shape=shapes,
        in_specs=specs,
        out_specs=outs if many else outs[0],
        scratch_shapes=scratch,
        compiler_params=pltpu.CompilerParams(vmem_limit_bytes=vmem * 2**20),
        cost_estimate=pl.CostEstimate(flops=flops, bytes_accessed=2**16, transcendentals=0),
    )(*args)


def per_device(queries, codes, positives, codebook):
    swap = functools.partial(lax.ppermute, axis_name="core", perm=[(0, 1), (1, 0)])
    swap_x = functools.partial(lax.ppermute, axis_name="xl", perm=[(0, 1), (1, 0)])
    shape = jax.ShapeDtypeStruct
    own_codes = codes[0]
    subspaces, passage_count = own_codes.shape
    size, width = queries.shape[1:]
    chips = 16
    half = chips * size
    offset = lax.axis_index(("xl", "z", "core")) * passage_count
    axes = [lax.axis_index(name) for name in ("core", "xh", "y", "xl")]
    place = jnp.stack([axes[0], offset, *axes[1:]]).astype(i32)
    scalar = {0: IN_SMEM}
    length = width // LANES * size + 16
    near = [codebook] + [lax.ppermute(codebook, "y", [(i, (i + k) % 4) for i in range(4)]) for k in range(1, 4)]
    near = jnp.stack(near)
    far = lax.ppermute(near, "xh", [(0, 1), (1, 0)])
    targets = jnp.pad(positives, ((0, 0), (0, LANES - size)))
    own = call(spread_kernel, shape((chips, length, LANES), bf16), (queries[0], targets), 10**6)
    own = lax.all_to_all(own, CHIP, 0, 0)
    passages = call(
        decode_kernel, shape((width, passage_count), bf16), (place, own_codes, near, far), 10**6, special=scalar
    )
    own, passages = lax.optimization_barrier((own, passages))
    other = swap(own)
    stats = call(scores_kernel, shape((32, 8, LANES), f32), (own, other, passages), 10**6)
    stats = lax.all_to_all(stats, CHIP + ("core",), 0, 0, tiled=True)
    query_other, query_own, grads = call(
        weights_kernel,
        [shape((half, width), f32), shape((half, width), f32), shape((width, passage_count), bf16)],
        (place, stats, own, other, passages),
        10**6,
        scratch=[pltpu.VMEM((2 * half, passage_count), bf16), pltpu.VMEM((2 * half, passage_count), bf16)],
        special=scalar,
        vmem=20,
    )
    query_cross = swap(query_other)

    def codeword_sums(mine):
        return call(
            functools.partial(codeword_kernel, mine),
            shape((8, 2, subspaces // 32, 16, LANES), f32),
            (place, grads, own_codes),
            10**6,
            special=scalar,
        )

    sums_cross = swap(codeword_sums(False))
    parts = codeword_sums(True) + sums_cross
    words = call(
        send_kernel, shape((chips // 2, length, LANES), i16), (place, query_own, query_cross), 10**6, special=scalar
    )
    parts, words = lax.optimization_barrier((parts, words))
    words = swap_x(words)
    parts = lax.all_to_all(parts.reshape(16, subspaces // 32, 16, LANES), SUB + ("xl",), 0, 0)
    count = subspaces // 32 * 16
    words = call(
        pack_kernel,
        shape((chips // 2, length + count, LANES), i16),
        (place, query_own, query_cross, words, parts),
        10**6,
        special=scalar,
    )
    words = lax.all_to_all(words, "z", 0, 0)
    query_grad, sums = call(unpack_kernel, [shape((size, width), bf16), shape((count, LANES), f32)], (words,), 10**6)
    beside = swap_x(sums)
    cross = swap(jnp.concatenate([sums, beside]))
    codeword_grad = call(
        join_kernel,
        shape((subspaces // 8, 8, 2 * LANES), f32),
        (place, sums, beside, cross),
        10**6,
        scratch=[pltpu.VMEM((4, count, LANES), f32)],
        special=scalar,
    )
    return query_grad[None], codeword_grad


def solution(mesh):
    split = Mesh(mesh.devices.reshape(2, 8, 2, 2, 4), ("xl", "z", "core", "xh", "y"))
    blk = ("xl", "z", "core")
    return jax.shard_map(
        per_device,
        mesh=split,
        in_specs=(P(SUB, blk, None), P(SUB, None, blk), P(SUB, blk), P(SUB, None, None)),
        out_specs=(P(SUB, blk, None), P(SUB, None, None)),
        check_vma=False,
    )
```

time: 641 us -> 128 us (0.20)
  waiting for transfers between devices: 358 us -> 14.3 us
  blocking collectives: 161 us -> 53.8 us
  matrix products: 90.2 us -> 0 us
  Pallas kernels: 0 us -> 29.7 us
  starting transfers between devices: 0.12 us -> 27.4 us
  between operations: 14.5 us -> 0.73 us
  local copies, waits for them, and re-layouts: 9.02 us -> 1.6 us
    psum x1 -> x0, waiting for transfers between devices: 239 us -> none  [per_device(): whole_sums = lax.psum(local_sums, ('blk', 'sub'))]
    reduce_scatter x1 -> x0, waiting for transfers between devices: 118 us -> none  [per_device(): lax.psum_scatter(jnp.dot(weights, wide_passages, precision=lax.Precision....]
    dot_general x19 -> x0, matrix products: 90.2 us -> none  [the longest x8 39.5 us: add_block(): jnp.einsum('mpk,pmw->mwk', onehot, grad_block, preferred_element_type=jnp...]
    pmax x1 -> x0, blocking collectives: 55.1 us -> none  [per_device(): peak_all = lax.pmax(peaks, 'blk')]
    all_to_all x0 -> x3, blocking collectives: none -> 53.8 us  [the longest x1 19.1 us: per_device(): stats = lax.all_to_all(stats, CHIP + ('core',), 0, 0, tiled=True)]
    psum x1 -> x0, blocking collectives: 53 us -> none  [per_device(): total_all = lax.psum(totals * jnp.exp(peaks - peak_all), 'blk')]
    all_gather x1 -> x0, blocking collectives: 30.2 us -> none  [per_device(): book = lax.all_gather(codebook, 'sub', axis=0, tiled=True)]
    pallas_call x0 -> x10, Pallas kernels: none -> 29.7 us  [call(): pl.pallas_call(kernel, out_shape=shapes, in_specs=specs, out_specs=outs i...]
  transfers between devices with their start and end apart: 3 -> 11, of which waited for: 2 -> 6; matrix products, arithmetic and copies ran while one was open for 7% -> 0% of each run, Pallas kernels for 0% -> 10%
where the time goes in v2:
time: 128 us
  blocking collectives  53.8 us (42%)
  Pallas kernels  29.7 us (23%)
  starting transfers between devices  27.4 us (21%)
  waiting for transfers between devices  14.3 us (11%)
  local copies, waits for them, and re-layouts  1.6 us (1%)
    pallas_call x10, Pallas kernels, call(): pl.pallas_call(kernel, out_shape=shapes, in_specs=specs, out_specs=outs i...  29.7 us
    all_to_all x1, blocking collectives, per_device(): stats = lax.all_to_all(stats, CHIP + ('core',), 0, 0, tiled=True)  19.1 us
    all_to_all x1, blocking collectives, per_device(): words = lax.all_to_all(words, 'z', 0, 0)  17.6 us
    all_to_all x1, blocking collectives, per_device(): lax.all_to_all(parts.reshape(16, subspaces // 32, 16, LANES), SUB + ('xl'...  17.1 us
    all_to_all x1, starting transfers between devices, per_device(): own = lax.all_to_all(own, CHIP, 0, 0)  10 us
    ppermute x1, waiting for transfers between devices, per_device(): far = lax.ppermute(near, 'xh', [(0, 1), (1, 0)])  6.46 us
    ppermute x3, starting transfers between devices, per_device(): lax.ppermute(codebook, 'y', [(i, (i + k) % 4) for i in range(4)])  4.46 us
    ppermute x1, starting transfers between devices, per_device(): cross = swap(jnp.concatenate([sums, beside]))  4.46 us
  transfers between devices with their start and end apart: 11, of which 6 were waited for; matrix products, arithmetic and copies ran while one was open for 0% of the time, Pallas kernels for 10%

profile of v2, /device:TPU:1, one launch (start us, length us, event | category | flops | bytes accessed | tf_op | source)
XLA Modules:
  0.0 127.6 jit_solution(10539320552560240139)
XLA Ops:
  0.6 0.0 copy-start
  0.6 0.7 pad.4.positives_ref
  1.4 0.0 copy-start.1
  1.4 0.8 copy-done.1
  2.1 0.0 copy-start.2
  2.2 1.0 shard_map.59
  3.2 10.0 %all-to-all-start = ((bf16[16,208,128]{2,1,0:T(8,128)(2,1)}), bf16[16,208,128]{2,1,0:T(8,128)(2,1)S(1)}, u32[]{:S(2)}, u32[]{:S(2)}) async-start(bf16[16,208,128]{2,1,0:T(8,128)(2,1)} %shard_map.59), calls=%async_computation | async-start | bytes 1703936 | tf_op jit(solution)/shard_map/all_to_all | solution.py:317
  13.2 0.0 copy-done.2
  13.2 1.4 %collective-permute-start = (bf16[12,8,256]{2,1,0:T(8,128)(2,1)S(1)}, bf16[12,8,256]{2,1,0:T(8,128)(2,1)S(1)}, u32[]{:S(2)}, u32[]{:S(2)}) collective-permute-start(bf16[12,8,256]{2,1,0:T(8,128)(2,1)S(1)} %copy-done.2), channel_id=1, source_target_pairs={{0,1},{1,2},{2,3},{3,0},{4,5},{5,6},{6,7},{7,4},{8,9},{9,10},{10,1... | collective-permute-start | bytes 147464 | tf_op jit(solution)/shard_map/ppermute | solution.py:312
  14.6 1.5 %collective-permute-start.2 = (bf16[12,8,256]{2,1,0:T(8,128)(2,1)S(1)}, bf16[12,8,256]{2,1,0:T(8,128)(2,1)S(1)}, u32[]{:S(2)}, u32[]{:S(2)}) collective-permute-start(bf16[12,8,256]{2,1,0:T(8,128)(2,1)S(1)} %copy-done.2), channel_id=1, source_target_pairs={{0,3},{1,0},{2,1},{3,2},{4,7},{5,4},{6,5},{7,6},{8,11},{9,8},{10,9... | collective-permute-start | bytes 147464 | tf_op jit(solution)/shard_map/ppermute | solution.py:312
  16.1 1.6 %collective-permute-start.1 = (bf16[12,8,256]{2,1,0:T(8,128)(2,1)S(1)}, bf16[12,8,256]{2,1,0:T(8,128)(2,1)S(1)}, u32[]{:S(2)}, u32[]{:S(2)}) collective-permute-start(bf16[12,8,256]{2,1,0:T(8,128)(2,1)S(1)} %copy-done.2), channel_id=1, source_target_pairs={{0,2},{1,3},{2,0},{3,1},{4,6},{5,7},{6,4},{7,5},{8,10},{9,11},{10,... | collective-permute-start | bytes 147464 | tf_op jit(solution)/shard_map/ppermute | solution.py:312
  17.7 0.0 collective-permute-done
  17.7 0.1 collective-permute-done.2
  17.8 2.8 %collective-permute-done.1 = bf16[12,8,256]{2,1,0:T(8,128)(2,1)S(1)} collective-permute-done((bf16[12,8,256]{2,1,0:T(8,128)(2,1)S(1)}, bf16[12,8,256]{2,1,0:T(8,128)(2,1)S(1)}, u32[]{:S(2)}, u32[]{:S(2)}) %collective-permute-start.1) | collective-permute-done | bytes 49184 | tf_op jit(solution)/shard_map/ppermute | solution.py:312
  20.7 2.5 %collective-permute-start.3 = (bf16[4,12,8,256]{3,2,1,0:T(8,128)(2,1)S(1)}, bf16[4,12,8,256]{3,2,1,0:T(8,128)(2,1)S(1)}, u32[]{:S(2)}, u32[]{:S(2)}) collective-permute-start(bf16[4,12,8,256]{3,2,1,0:T(8,128)(2,1)S(1)} %pad_maximum_fusion.near_ref), channel_id=1, source_target_pairs={{0,4},{4,0},{1,5},{5,1},{2,6},{6,2},{3,7},{7,3},{8,12},{12,8},{9,1... | collective-permute-start | bytes 589832 | tf_op jit(solution)/shard_map/ppermute | solution.py:314
  23.2 0.1 stack.38.place_ref
  23.3 6.5 %collective-permute-done.3.far_ref = bf16[4,12,8,256]{3,2,1,0:T(8,128)(2,1)S(1)} collective-permute-done((bf16[4,12,8,256]{3,2,1,0:T(8,128)(2,1)S(1)}, bf16[4,12,8,256]{3,2,1,0:T(8,128)(2,1)S(1)}, u32[]{:S(2)}, u32[]{:S(2)}) %collective-permute-start.3) | collective-permute-done | bytes 196640 | tf_op jit(solution)/shard_map/ppermute | solution.py:314
  29.8 0.0 copy-done
  29.8 4.5 %shard_map.60.passages_ref = bf16[768,1024]{1,0:T(8,128)(2,1)S(1)} custom-call(s32[5]{0:T(128)S(1)} %stack.38.place_ref, s32[96,1024]{1,0:T(8,128)S(1)} %bitcast.13, bf16[4,12,8,256]{3,2,1,0:T(8,128)(2,1)S(1)} %pad_maximum_fusion.near_ref, bf16[4,12,8,256]{3,2,1,0:T(8,128)(2,1)S(1)} %collective-permute-done.3.far_ref), custom_call_target="tpu_custom_call" | custom-call | flops 1000000 | bytes 65536 | tf_op jit(solution)/shard_map/pallas_call | solution.py:287
  34.2 0.0 all-to-all-done.own_ref
  34.2 3.1 %collective-permute-start.4 = (bf16[16,208,128]{2,1,0:T(8,128)(2,1)S(1)}, bf16[16,208,128]{2,1,0:T(8,128)(2,1)S(1)}, u32[]{:S(2)}, u32[]{:S(2)}) collective-permute-start(bf16[16,208,128]{2,1,0:T(8,128)(2,1)S(1)} %all-to-all-done.own_ref), channel_id=1, source_target_pairs={{0,8},{8,0},{1,9},{9,1},{2,10},{10,2},{3,11},{11,3},{4,12},{12,4},... | collective-permute-start | bytes 2555912 | tf_op jit(solution)/shard_map/ppermute | solution.py:322
  37.3 2.0 %collective-permute-done.4.other_ref = bf16[16,208,128]{2,1,0:T(8,128)(2,1)S(1)} collective-permute-done((bf16[16,208,128]{2,1,0:T(8,128)(2,1)S(1)}, bf16[16,208,128]{2,1,0:T(8,128)(2,1)S(1)}, u32[]{:S(2)}, u32[]{:S(2)}) %collective-permute-start.4) | collective-permute-done | bytes 852000 | tf_op jit(solution)/shard_map/ppermute | solution.py:322
  39.3 2.4 %shard_map.61 = f32[32,8,128]{2,1,0:T(8,128)S(1)} custom-call(bf16[16,208,128]{2,1,0:T(8,128)(2,1)S(1)} %all-to-all-done.own_ref, bf16[16,208,128]{2,1,0:T(8,128)(2,1)S(1)} %collective-permute-done.4.other_ref, bf16[768,1024]{1,0:T(8,128)(2,1)S(1)} %shard_map.60.passages_ref), custom_call_target="tpu_custom_call" | custom-call | flops 1000000 | bytes 65536 | tf_op jit(solution)/shard_map/pallas_call | solution.py:287
  41.7 19.1 %all_to_all.20.stats_ref = f32[32,8,128]{2,1,0:T(8,128)S(1)} all-to-all(f32[32,8,128]{2,1,0:T(8,128)S(1)} %shard_map.61), channel_id=1, replica_groups=mesh['xl'=2,'z'=8,'core'=2,'xh'=2,'y'=4] {'xl','z','core'}, dimensions={0} | all-to-all | bytes 262144 | tf_op jit(solution)/shard_map/all_to_all | solution.py:324
  60.8 9.5 %shard_map.62 = (f32[512,768]{1,0:T(8,128)S(1)}, f32[512,768]{1,0:T(8,128)S(1)}, bf16[768,1024]{1,0:T(8,128)(2,1)S(1)}) custom-call(s32[5]{0:T(128)S(1)} %stack.38.place_ref, f32[32,8,128]{2,1,0:T(8,128)S(1)} %all_to_all.20.stats_ref, bf16[16,208,128]{2,1,0:T(8,128)(2,1)S(1)} %all-to-all-done.own_ref, ...), custom_call_target="tpu_custom_call" | custom-call | flops 1000000 | bytes 65536 | tf_op jit(solution)/shard_map/pallas_call | solution.py:287
  70.3 1.7 %collective-permute-start.5 = (f32[512,768]{1,0:T(8,128)S(1)}, f32[512,768]{1,0:T(8,128)S(1)}, u32[]{:S(2)}, u32[]{:S(2)}) collective-permute-start(f32[512,768]{1,0:T(8,128)S(1)} %get-tuple-element.14), channel_id=1, source_target_pairs={{0,8},{8,0},{1,9},{9,1},{2,10},{10,2},{3,11},{11,3},{4,12},{12,4},... | collective-permute-start | bytes 4718600 | tf_op jit(solution)/shard_map/ppermute | solution.py:334
  72.0 3.9 %shard_map.64 = f32[8,2,3,16,128]{4,3,2,1,0:T(8,128)S(1)} custom-call(s32[5]{0:T(128)S(1)} %stack.38.place_ref, bf16[768,1024]{1,0:T(8,128)(2,1)S(1)} %get-tuple-element.15.grads_ref, s32[96,1024]{1,0:T(8,128)S(1)} %bitcast.14), custom_call_target="tpu_custom_call" | custom-call | flops 1000000 | bytes 65536 | tf_op jit(solution)/shard_map/pallas_call | solution.py:287
  75.9 0.1 collective-permute-start.6
  76.0 3.9 %shard_map.63 = f32[8,2,3,16,128]{4,3,2,1,0:T(8,128)S(1)} custom-call(s32[5]{0:T(128)S(1)} %stack.38.place_ref, bf16[768,1024]{1,0:T(8,128)(2,1)S(1)} %get-tuple-element.15.grads_ref, s32[96,1024]{1,0:T(8,128)S(1)} %bitcast.15), custom_call_target="tpu_custom_call" | custom-call | flops 1000000 | bytes 65536 | tf_op jit(solution)/shard_map/pallas_call | solution.py:287
  79.9 0.0 collective-permute-done.6
  79.9 0.1 add.13
  80.0 0.0 collective-permute-done.5.cross_ref
  80.0 0.9 shard_map.65
  80.9 0.3 collective-permute-start.7
  81.2 17.1 %all_to_all.21.parts_ref = f32[16,3,16,128]{3,2,1,0:T(8,128)S(1)} all-to-all(f32[16,3,16,128]{3,2,1,0:T(8,128)S(1)} %bitcast.17), channel_id=1, replica_groups=mesh['xl'=2,'z'=8,'core'=2,'xh'=2,'y'=4] {'xh','y','xl'}, dimensions={0} | all-to-all | bytes 786432 | tf_op jit(solution)/shard_map/all_to_all | solution.py:352
  98.3 0.0 collective-permute-done.7.words_ref
  98.3 1.5 %shard_map.66 = s16[8,256,128]{2,1,0:T(8,128)(2,1)S(1)} custom-call(s32[5]{0:T(128)S(1)} %stack.38.place_ref, f32[512,768]{1,0:T(8,128)S(1)} %get-tuple-element.13.sums_ref, f32[512,768]{1,0:T(8,128)S(1)} %collective-permute-done.5.cross_ref, s16[8,208,128]{2,1,0:T(8,128)(2,1)S(1)} %collective-permute-done.7.words_ref, ...), custom_call_target="tpu_custom_call" | custom-call | flops 1000000 | bytes 65536 | tf_op jit(solution)/shard_map/pallas_call | solution.py:287
  99.8 17.6 %all_to_all.22.words_ref = s16[8,256,128]{2,1,0:T(8,128)(2,1)S(1)} all-to-all(s16[8,256,128]{2,1,0:T(8,128)(2,1)S(1)} %shard_map.66), channel_id=1, replica_groups=mesh['xl'=2,'z'=8,'core'=2,'xh'=2,'y'=4] {'z'}, dimensions={0} | all-to-all | bytes 1048576 | tf_op jit(solution)/shard_map/all_to_all | solution.py:361
  117.4 0.8 shard_map.67
  118.2 0.7 collective-permute-start.8
  118.9 2.0 %collective-permute-done.8.beside_ref = f32[48,128]{1,0:T(8,128)S(1)} collective-permute-done((f32[48,128]{1,0:T(8,128)S(1)}, f32[48,128]{1,0:T(8,128)S(1)}, u32[]{:S(2)}, u32[]{:S(2)}) %collective-permute-start.8) | collective-permute-done | bytes 24608 | tf_op jit(solution)/shard_map/ppermute | solution.py:363
  120.9 4.5 %collective-permute-start.9 = (f32[96,128]{1,0:T(8,128)S(1)}, f32[96,128]{1,0:T(8,128)S(1)}, u32[]{:S(2)}, u32[]{:S(2)}) collective-permute-start(f32[96,128]{1,0:T(8,128)S(1)} %pad_maximum_fusion.1), channel_id=1, source_target_pairs={{0,8},{8,0},{1,9},{9,1},{2,10},{10,2},{3,11},{11,3},{4,12},{12,4},... | collective-permute-start | bytes 147464 | tf_op jit(solution)/shard_map/ppermute | solution.py:364
  125.3 0.9 collective-permute-done.9.cross_ref
  126.2 1.3 %shard_map.68 = f32[12,8,256]{2,1,0:T(8,128)} custom-call(s32[5]{0:T(128)S(1)} %stack.38.place_ref, f32[48,128]{1,0:T(8,128)S(1)} %get-tuple-element.19.own_ref, f32[48,128]{1,0:T(8,128)S(1)} %collective-permute-done.8.beside_ref, f32[96,128]{1,0:T(8,128)S(1)} %collective-permute-done.9.cross_ref), custom_call_target="tpu_custom_call" | custom-call | flops 1000000 | bytes 65536 | tf_op jit(solution)/shard_map/pallas_call | solution.py:287
  (2 shorter events, 0.0 us)
Async XLA Ops:
  0.6 29.1 %copy-start = (s32[1,96,1024]{2,1,0:T(8,128)S(1)}, s32[1,96,1024]{2,1,0:T(8,128)}, u32[]{:S(2)}) copy-start(s32[1,96,1024]{2,1,0:T(8,128)} %param.5) | copy-start | bytes 1179652
  1.4 0.8 copy-start.1
  2.1 11.1 %copy-start.2 = (bf16[12,8,256]{2,1,0:T(8,128)(2,1)S(1)}, bf16[12,8,256]{2,1,0:T(8,128)(2,1)}, u32[]{:S(2)}) copy-start(bf16[12,8,256]{2,1,0:T(8,128)(2,1)} %param.7) | copy-start | bytes 147460
  3.2 31.1 %all-to-all-start = ((bf16[16,208,128]{2,1,0:T(8,128)(2,1)}), bf16[16,208,128]{2,1,0:T(8,128)(2,1)S(1)}, u32[]{:S(2)}, u32[]{:S(2)}) async-start(bf16[16,208,128]{2,1,0:T(8,128)(2,1)} %shard_map.59), calls=%async_computation | async-start | bytes 1703936 | tf_op jit(solution)/shard_map/all_to_all | solution.py:317
  13.2 4.5 %collective-permute-start = (bf16[12,8,256]{2,1,0:T(8,128)(2,1)S(1)}, bf16[12,8,256]{2,1,0:T(8,128)(2,1)S(1)}, u32[]{:S(2)}, u32[]{:S(2)}) collective-permute-start(bf16[12,8,256]{2,1,0:T(8,128)(2,1)S(1)} %copy-done.2), channel_id=1, source_target_pairs={{0,1},{1,2},{2,3},{3,0},{4,5},{5,6},{6,7},{7,4},{8,9},{9,10},{10,1... | collective-permute-start | bytes 147464 | tf_op jit(solution)/shard_map/ppermute | solution.py:312
  14.6 3.2 %collective-permute-start.2 = (bf16[12,8,256]{2,1,0:T(8,128)(2,1)S(1)}, bf16[12,8,256]{2,1,0:T(8,128)(2,1)S(1)}, u32[]{:S(2)}, u32[]{:S(2)}) collective-permute-start(bf16[12,8,256]{2,1,0:T(8,128)(2,1)S(1)} %copy-done.2), channel_id=1, source_target_pairs={{0,3},{1,0},{2,1},{3,2},{4,7},{5,4},{6,5},{7,6},{8,11},{9,8},{10,9... | collective-permute-start | bytes 147464 | tf_op jit(solution)/shard_map/ppermute | solution.py:312
  16.1 4.5 %collective-permute-start.1 = (bf16[12,8,256]{2,1,0:T(8,128)(2,1)S(1)}, bf16[12,8,256]{2,1,0:T(8,128)(2,1)S(1)}, u32[]{:S(2)}, u32[]{:S(2)}) collective-permute-start(bf16[12,8,256]{2,1,0:T(8,128)(2,1)S(1)} %copy-done.2), channel_id=1, source_target_pairs={{0,2},{1,3},{2,0},{3,1},{4,6},{5,7},{6,4},{7,5},{8,10},{9,11},{10,... | collective-permute-start | bytes 147464 | tf_op jit(solution)/shard_map/ppermute | solution.py:312
  20.7 9.1 %collective-permute-start.3 = (bf16[4,12,8,256]{3,2,1,0:T(8,128)(2,1)S(1)}, bf16[4,12,8,256]{3,2,1,0:T(8,128)(2,1)S(1)}, u32[]{:S(2)}, u32[]{:S(2)}) collective-permute-start(bf16[4,12,8,256]{3,2,1,0:T(8,128)(2,1)S(1)} %pad_maximum_fusion.near_ref), channel_id=1, source_target_pairs={{0,4},{4,0},{1,5},{5,1},{2,6},{6,2},{3,7},{7,3},{8,12},{12,8},{9,1... | collective-permute-start | bytes 589832 | tf_op jit(solution)/shard_map/ppermute | solution.py:314
  34.2 5.1 %collective-permute-start.4 = (bf16[16,208,128]{2,1,0:T(8,128)(2,1)S(1)}, bf16[16,208,128]{2,1,0:T(8,128)(2,1)S(1)}, u32[]{:S(2)}, u32[]{:S(2)}) collective-permute-start(bf16[16,208,128]{2,1,0:T(8,128)(2,1)S(1)} %all-to-all-done.own_ref), channel_id=1, source_target_pairs={{0,8},{8,0},{1,9},{9,1},{2,10},{10,2},{3,11},{11,3},{4,12},{12,4},... | collective-permute-start | bytes 2555912 | tf_op jit(solution)/shard_map/ppermute | solution.py:322
  70.3 9.7 %collective-permute-start.5 = (f32[512,768]{1,0:T(8,128)S(1)}, f32[512,768]{1,0:T(8,128)S(1)}, u32[]{:S(2)}, u32[]{:S(2)}) collective-permute-start(f32[512,768]{1,0:T(8,128)S(1)} %get-tuple-element.14), channel_id=1, source_target_pairs={{0,8},{8,0},{1,9},{9,1},{2,10},{10,2},{3,11},{11,3},{4,12},{12,4},... | collective-permute-start | bytes 4718600 | tf_op jit(solution)/shard_map/ppermute | solution.py:334
  75.9 4.0 %collective-permute-start.6 = (f32[8,2,3,16,128]{4,3,2,1,0:T(8,128)S(1)}, f32[8,2,3,16,128]{4,3,2,1,0:T(8,128)S(1)}, u32[]{:S(2)}, u32[]{:S(2)}) collective-permute-start(f32[8,2,3,16,128]{4,3,2,1,0:T(8,128)S(1)} %shard_map.64), channel_id=1, source_target_pairs={{0,8},{8,0},{1,9},{9,1},{2,10},{10,2},{3,11},{11,3},{4,12},{12,4},... | collective-permute-start | bytes 1179656 | tf_op jit(solution)/shard_map/ppermute | solution.py:345
  80.9 17.4 %collective-permute-start.7 = (s16[8,208,128]{2,1,0:T(8,128)(2,1)S(1)}, s16[8,208,128]{2,1,0:T(8,128)(2,1)S(1)}, u32[]{:S(2)}, u32[]{:S(2)}) collective-permute-start(s16[8,208,128]{2,1,0:T(8,128)(2,1)S(1)} %shard_map.65), channel_id=1, source_target_pairs={{0,128},{128,0},{1,129},{129,1},{2,130},{130,2},{3,131},{131,3},{4... | collective-permute-start | bytes 1277960 | tf_op jit(solution)/shard_map/ppermute | solution.py:351
  118.2 2.7 %collective-permute-start.8 = (f32[48,128]{1,0:T(8,128)S(1)}, f32[48,128]{1,0:T(8,128)S(1)}, u32[]{:S(2)}, u32[]{:S(2)}) collective-permute-start(f32[48,128]{1,0:T(8,128)S(1)} %get-tuple-element.19.own_ref), channel_id=1, source_target_pairs={{0,128},{128,0},{1,129},{129,1},{2,130},{130,2},{3,131},{131,3},{4... | collective-permute-start | bytes 73736 | tf_op jit(solution)/shard_map/ppermute | solution.py:363
  120.9 5.3 %collective-permute-start.9 = (f32[96,128]{1,0:T(8,128)S(1)}, f32[96,128]{1,0:T(8,128)S(1)}, u32[]{:S(2)}, u32[]{:S(2)}) collective-permute-start(f32[96,128]{1,0:T(8,128)S(1)} %pad_maximum_fusion.1), channel_id=1, source_target_pairs={{0,8},{8,0},{1,9},{9,1},{2,10},{10,2},{3,11},{11,3},{4,12},{12,4},... | collective-permute-start | bytes 147464 | tf_op jit(solution)/shard_map/ppermute | solution.py:364

commit v3 on v2

--- a/solution.py
+++ b/solution.py
@@ -46,15 +46,17 @@
     return jnp.exp2(jnp.transpose(jnp.broadcast_to(row, (LANES, LANES)))[:count])
 
 
-def spread_kernel(queries_ref, positives_ref, out_ref):
+def spread_kernel(place_ref, queries_ref, positives_ref, book_ref, out_ref, share_ref):
     size, width = queries_ref.shape
-    target = positives_ref[...]
+    target = jnp.concatenate([positives_ref[...], jnp.zeros((1, LANES - size), i32)], axis=1)
     tail = jnp.concatenate([target // LANES, target % LANES, jnp.zeros((14, LANES), i32)], axis=0)
     tail = tail.astype(f32).astype(bf16)
     for c in range(out_ref.shape[0]):
         for t in range(width // LANES):
             out_ref[c, t * size : (t + 1) * size] = queries_ref[:, t * LANES : (t + 1) * LANES]
         out_ref[c, width // LANES * size :] = tail
+    count = share_ref.shape[0]
+    share_ref[...] = book_ref[pl.ds(place_ref[0] * count, count)]
 
 
 def query_columns(pack_ref, t, first, count):
@@ -74,40 +76,36 @@
     return jnp.transpose(target)
 
 
-def decode_kernel(place_ref, codes_ref, near_ref, far_ref, out_ref):
+def decode_kernel(place_ref, codes_ref, near_ref, near_cross_ref, far_ref, far_cross_ref, out_ref):
+    core, far_side, along = place_ref[0], 1 - place_ref[2], place_ref[3]
     share = near_ref.shape[1]
-    far, along = place_ref[2], place_ref[3]
-
-    def table_of(group, member):
-        piece = (along + 4 - group % 4) % 4
-        near, other = near_ref[piece, member], far_ref[piece, member]
-        return jnp.where(group // 4 == far, near, other).astype(f32)
-
-    for group in range(8):
-
-        def pair(j, carry, group=group):
-            rows = []
-            for h in range(2):
-                table = table_of(group, 2 * j + h)
-                low, high = table[:, :LANES], table[:, LANES:]
-                row = codes_ref[pl.ds(group * share + 2 * j + h, 1), :]
-                parts = []
-                for t in range(row.shape[1] // LANES):
-                    code = jnp.broadcast_to(row[:, t * LANES : (t + 1) * LANES], (8, LANES))
-                    index = code & (LANES - 1)
-                    parts.append(
-                        jnp.where(
-                            code < LANES,
-                            jnp.take_along_axis(low, index, axis=1, mode="promise_in_bounds"),
-                            jnp.take_along_axis(high, index, axis=1, mode="promise_in_bounds"),
-                        )
+
+    def pair(j, carry):
+        side, group, c, k = j // (4 * share), j // share % 4, j // (share // 2) % 2, j % (share // 2) * 2
+        piece = (along + 4 - group) % 4
+        rows = []
+        for h in range(2):
+            near = jnp.where(core == c, near_ref[piece, k + h].astype(f32), near_cross_ref[piece, k + h].astype(f32))
+            far = jnp.where(core == c, far_ref[piece, k + h].astype(f32), far_cross_ref[piece, k + h].astype(f32))
+            table = jnp.where(side == far_side, far, near)
+            low, high = table[:, :LANES], table[:, LANES:]
+            row = codes_ref[pl.ds(2 * j + h, 1), :]
+            parts = []
+            for t in range(row.shape[1] // LANES):
+                code = jnp.broadcast_to(row[:, t * LANES : (t + 1) * LANES], (8, LANES))
+                index = code & (LANES - 1)
+                parts.append(
+                    jnp.where(
+                        code < LANES,
+                        jnp.take_along_axis(low, index, axis=1, mode="promise_in_bounds"),
+                        jnp.take_along_axis(high, index, axis=1, mode="promise_in_bounds"),
                     )
-                rows.append(jnp.concatenate(parts, axis=1))
-            start = pl.multiple_of(16 * (group * share // 2 + j), 16)
-            out_ref[pl.ds(start, 16), :] = jnp.concatenate(rows, axis=0).astype(bf16)
-            return carry
-
-        lax.fori_loop(0, share // 2, pair, 0, unroll=2)
+                )
+            rows.append(jnp.concatenate(parts, axis=1))
+        out_ref[pl.ds(pl.multiple_of(16 * j, 16), 16), :] = jnp.concatenate(rows, axis=0).astype(bf16)
+        return carry
+
+    lax.fori_loop(0, codes_ref.shape[0] // 2, pair, 0, unroll=8)
 
 
 def scores_kernel(own_ref, other_ref, passages_ref, stats_ref):
@@ -198,7 +196,7 @@
             out_ref[j // 3, k, j % 3] = sums[16 * k : 16 * k + 16]
         return carry
 
-    lax.fori_loop(0, codes_ref.shape[0] // 4, four, 0, unroll=4)
+    lax.fori_loop(0, codes_ref.shape[0] // 4, four, 0, unroll=8)
 
 
 def put_query_words(chunk, out_ref, c):
@@ -259,13 +257,12 @@
     sums_ref[...] = sums
 
 
-def join_kernel(place_ref, own_ref, beside_ref, cross_ref, out_ref, all_ref):
+def join_kernel(place_ref, own_ref, beside_ref, cross_ref, corner_ref, out_ref, all_ref):
     core, side = place_ref[0], place_ref[4]
-    count = own_ref.shape[0]
     all_ref[2 * core + side] = own_ref[...]
     all_ref[2 * core + 1 - side] = beside_ref[...]
-    all_ref[2 - 2 * core + side] = cross_ref[:count]
-    all_ref[2 - 2 * core + 1 - side] = cross_ref[count:]
+    all_ref[2 - 2 * core + side] = cross_ref[...]
+    all_ref[2 - 2 * core + 1 - side] = corner_ref[...]
     for j in range(3):
         rows = [all_ref[t // 2, 16 * j + t % 2 * 8 : 16 * j + t % 2 * 8 + 8] for t in range(8)]
         for m in range(4):
@@ -309,17 +306,27 @@
     place = jnp.stack([axes[0], offset, *axes[1:]]).astype(i32)
     scalar = {0: IN_SMEM}
     length = width // LANES * size + 16
-    near = [codebook] + [lax.ppermute(codebook, "y", [(i, (i + k) % 4) for i in range(4)]) for k in range(1, 4)]
+    own, share = call(
+        spread_kernel,
+        [shape((chips, length, LANES), bf16), shape((codebook.shape[0] // 2, *codebook.shape[1:]), bf16)],
+        (place, queries[0], positives, codebook),
+        10**6,
+        special=scalar,
+        vmem=60,
+    )
+    near = [share] + [lax.ppermute(share, "y", [(i, (i + k) % 4) for i in range(4)]) for k in range(1, 4)]
     near = jnp.stack(near)
     far = lax.ppermute(near, "xh", [(0, 1), (1, 0)])
-    targets = jnp.pad(positives, ((0, 0), (0, LANES - size)))
-    own = call(spread_kernel, shape((chips, length, LANES), bf16), (queries[0], targets), 10**6)
     own = lax.all_to_all(own, CHIP, 0, 0)
+    own, *books = lax.optimization_barrier((own, near, swap(near), far, swap(far)))
+    other = swap(own)
     passages = call(
-        decode_kernel, shape((width, passage_count), bf16), (place, own_codes, near, far), 10**6, special=scalar
-    )
-    own, passages = lax.optimization_barrier((own, passages))
-    other = swap(own)
+        decode_kernel,
+        shape((width, passage_count), bf16),
+        (place, own_codes, *books),
+        10**6,
+        special=scalar,
+    )
     stats = call(scores_kernel, shape((32, 8, LANES), f32), (own, other, passages), 10**6)
     stats = lax.all_to_all(stats, CHIP + ("core",), 0, 0, tiled=True)
     query_other, query_own, grads = call(
@@ -361,11 +368,12 @@
     words = lax.all_to_all(words, "z", 0, 0)
     query_grad, sums = call(unpack_kernel, [shape((size, width), bf16), shape((count, LANES), f32)], (words,), 10**6)
     beside = swap_x(sums)
-    cross = swap(jnp.concatenate([sums, beside]))
+    corner = lax.ppermute(sums, ("xl", "core"), [(i, 3 - i) for i in range(4)])
+    cross = swap(sums)
     codeword_grad = call(
         join_kernel,
         shape((subspaces // 8, 8, 2 * LANES), f32),
-        (place, sums, beside, cross),
+        (place, sums, beside, cross, corner),
         10**6,
         scratch=[pltpu.VMEM((4, count, LANES), f32)],
         special=scalar,

time: 128 us -> 122 us (0.953)
  starting transfers between devices: 27.4 us -> 31.8 us
  blocking collectives: 53.8 us -> 49.6 us
  waiting for transfers between devices: 14.3 us -> 10.4 us
  Pallas kernels: 29.7 us -> 28.4 us
    all_to_all x1, blocking collectives: 19.1 us -> 13.8 us  [per_device(): stats = lax.all_to_all(stats, CHIP + ('core',), 0, 0, tiled=True)]
    ppermute x1, waiting for transfers between devices: 6.46 us -> 1.22 us  [per_device(): far = lax.ppermute(near, 'xh', [(0, 1), (1, 0)])]
    ppermute x4 -> x7, starting transfers between devices: 8.91 us -> 13.7 us  [the longest x1 3.86 us: per_device(): corner = lax.ppermute(sums, ('xl', 'core'), [(i, 3 - i) for i in range(4)])]
    all_to_all x1, waiting for transfers between devices: 0.01 us -> 2.98 us  [per_device(): own = lax.all_to_all(own, CHIP, 0, 0)]
    ppermute x1, waiting for transfers between devices: 2.01 us -> 0.01 us  [per_device(): other = swap(own)]
    pallas_call x10, Pallas kernels: 29.7 us -> 28.4 us  [call(): pl.pallas_call(kernel, out_shape=shapes, in_specs=specs, out_specs=outs i...]
    ppermute x4 -> x7, waiting for transfers between devices: 3.83 us -> 5.06 us  [the longest x3 3.4 us: per_device(): lax.ppermute(share, 'y', [(i, (i + k) % 4) for i in range(4)])]
  transfers between devices with their start and end apart: 11 -> 14, of which waited for: 6 -> 7; matrix products, arithmetic and copies ran while one was open for 0% -> 0% of each run, Pallas kernels for 10% -> 8%
where the time goes in v3:
time: 122 us
  blocking collectives  49.6 us (41%)
  starting transfers between devices  31.8 us (26%)
  Pallas kernels  28.4 us (23%)
  waiting for transfers between devices  10.4 us (9%)
    pallas_call x10, Pallas kernels, call(): pl.pallas_call(kernel, out_shape=shapes, in_specs=specs, out_specs=outs i...  28.4 us
    all_to_all x1, blocking collectives, per_device(): lax.all_to_all(parts.reshape(16, subspaces // 32, 16, LANES), SUB + ('xl'...  18.2 us
    all_to_all x1, blocking collectives, per_device(): words = lax.all_to_all(words, 'z', 0, 0)  17.6 us
    all_to_all x1, blocking collectives, per_device(): stats = lax.all_to_all(stats, CHIP + ('core',), 0, 0, tiled=True)  13.8 us
    all_to_all x1, starting transfers between devices, per_device(): own = lax.all_to_all(own, CHIP, 0, 0)  10.2 us
    ppermute x1, starting transfers between devices, per_device(): corner = lax.ppermute(sums, ('xl', 'core'), [(i, 3 - i) for i in range(4)])  3.86 us
    ppermute x3, starting transfers between devices, per_device(): lax.ppermute(share, 'y', [(i, (i + k) % 4) for i in range(4)])  3.85 us
    ppermute x3, waiting for transfers between devices, per_device(): lax.ppermute(share, 'y', [(i, (i + k) % 4) for i in range(4)])  3.4 us
  transfers between devices with their start and end apart: 14, of which 7 were waited for; matrix products, arithmetic and copies ran while one was open for 0% of the time, Pallas kernels for 8%

profile of v3, /device:TPU:1, one launch (start us, length us, event | category | flops | bytes accessed | tf_op | source)
XLA Modules:
  0.0 121.7 jit_solution(3859850985896272349)
XLA Ops:
  0.6 0.0 copy-start
  0.7 0.6 stack.38.place_ref
  1.3 0.0 copy-start.1
  1.3 1.9 %shard_map.59 = (bf16[16,208,128]{2,1,0:T(8,128)(2,1)}, bf16[6,8,256]{2,1,0:T(8,128)(2,1)}) custom-call(s32[5]{0:T(128)} %stack.38.place_ref, bf16[32,768]{1,0:T(8,128)(2,1)} %bitcast.17, s32[1,32]{1,0:T(1,128)} %positives_ref.1, bf16[12,8,256]{2,1,0:T(8,128)(2,1)} %book_ref.1), custom_call_target="tpu_custom_call" | custom-call | flops 1000000 | bytes 65536 | tf_op jit(solution)/shard_map/pallas_call | solution.py:284
  3.1 0.0 copy-start.2
  3.1 10.2 %all-to-all-start = ((bf16[16,208,128]{2,1,0:T(8,128)(2,1)}), bf16[16,208,128]{2,1,0:T(8,128)(2,1)S(1)}, u32[]{:S(2)}, u32[]{:S(2)}) async-start(bf16[16,208,128]{2,1,0:T(8,128)(2,1)} %get-tuple-element.16), calls=%async_computation | async-start | bytes 1703936 | tf_op jit(solution)/shard_map/all_to_all | solution.py:320
  13.3 0.0 copy-done.2
  13.3 2.8 %collective-permute-start.2 = (bf16[6,8,256]{2,1,0:T(8,128)(2,1)S(1)}, bf16[6,8,256]{2,1,0:T(8,128)(2,1)S(1)}, u32[]{:S(2)}, u32[]{:S(2)}) collective-permute-start(bf16[6,8,256]{2,1,0:T(8,128)(2,1)S(1)} %copy-done.2), channel_id=1, source_target_pairs={{0,3},{1,0},{2,1},{3,2},{4,7},{5,4},{6,5},{7,6},{8,11},{9,8},{10,9... | collective-permute-start | bytes 73736 | tf_op jit(solution)/shard_map/ppermute | solution.py:317
  16.1 0.3 collective-permute-start.1
  16.5 0.7 collective-permute-start
  17.2 0.0 collective-permute-done.2
  17.2 3.2 %collective-permute-done.1 = bf16[6,8,256]{2,1,0:T(8,128)(2,1)S(1)} collective-permute-done((bf16[6,8,256]{2,1,0:T(8,128)(2,1)S(1)}, bf16[6,8,256]{2,1,0:T(8,128)(2,1)S(1)}, u32[]{:S(2)}, u32[]{:S(2)}) %collective-permute-start.1) | collective-permute-done | bytes 24608 | tf_op jit(solution)/shard_map/ppermute | solution.py:317
  20.3 0.2 collective-permute-done
  20.6 2.5 %collective-permute-start.4 = (bf16[4,6,8,256]{3,2,1,0:T(8,128)(2,1)S(1)}, bf16[4,6,8,256]{3,2,1,0:T(8,128)(2,1)S(1)}, u32[]{:S(2)}, u32[]{:S(2)}) collective-permute-start(bf16[4,6,8,256]{3,2,1,0:T(8,128)(2,1)S(1)} %pad_maximum_fusion.near_ref), channel_id=1, source_target_pairs={{0,4},{4,0},{1,5},{5,1},{2,6},{6,2},{3,7},{7,3},{8,12},{12,8},{9,1... | collective-permute-start | bytes 294920 | tf_op jit(solution)/shard_map/ppermute | solution.py:319
  23.1 2.7 %collective-permute-start.3 = (bf16[4,6,8,256]{3,2,1,0:T(8,128)(2,1)S(1)}, bf16[4,6,8,256]{3,2,1,0:T(8,128)(2,1)S(1)}, u32[]{:S(2)}, u32[]{:S(2)}) collective-permute-start(bf16[4,6,8,256]{3,2,1,0:T(8,128)(2,1)S(1)} %pad_maximum_fusion.near_ref), channel_id=1, source_target_pairs={{0,8},{8,0},{1,9},{9,1},{2,10},{10,2},{3,11},{11,3},{4,12},{12,4},... | collective-permute-start | bytes 294920 | tf_op jit(solution)/shard_map/ppermute | solution.py:321
  25.9 1.2 %collective-permute-done.4.far_ref = bf16[4,6,8,256]{3,2,1,0:T(8,128)(2,1)S(1)} collective-permute-done((bf16[4,6,8,256]{3,2,1,0:T(8,128)(2,1)S(1)}, bf16[4,6,8,256]{3,2,1,0:T(8,128)(2,1)S(1)}, u32[]{:S(2)}, u32[]{:S(2)}) %collective-permute-start.4) | collective-permute-done | bytes 98336 | tf_op jit(solution)/shard_map/ppermute | solution.py:319
  27.1 3.3 %collective-permute-start.5 = (bf16[4,6,8,256]{3,2,1,0:T(8,128)(2,1)S(1)}, bf16[4,6,8,256]{3,2,1,0:T(8,128)(2,1)S(1)}, u32[]{:S(2)}, u32[]{:S(2)}) collective-permute-start(bf16[4,6,8,256]{3,2,1,0:T(8,128)(2,1)S(1)} %collective-permute-done.4.far_ref), channel_id=1, source_target_pairs={{0,8},{8,0},{1,9},{9,1},{2,10},{10,2},{3,11},{11,3},{4,12},{12,4},... | collective-permute-start | bytes 294920 | tf_op jit(solution)/shard_map/ppermute | solution.py:321
  30.4 0.0 collective-permute-done.3.near_cross_ref
  30.4 0.9 collective-permute-done.5.far_cross_ref
  31.3 3.0 %all-to-all-done.own_ref = bf16[16,208,128]{2,1,0:T(8,128)(2,1)S(1)} async-done(((bf16[16,208,128]{2,1,0:T(8,128)(2,1)}), bf16[16,208,128]{2,1,0:T(8,128)(2,1)S(1)}, u32[]{:S(2)}, u32[]{:S(2)}) %all-to-all-start) | async-done | bytes 852000 | tf_op jit(solution)/shard_map/all_to_all | solution.py:320
  34.3 2.5 %collective-permute-start.6 = (bf16[16,208,128]{2,1,0:T(8,128)(2,1)S(1)}, bf16[16,208,128]{2,1,0:T(8,128)(2,1)S(1)}, u32[]{:S(2)}, u32[]{:S(2)}) collective-permute-start(bf16[16,208,128]{2,1,0:T(8,128)(2,1)S(1)} %all-to-all-done.own_ref), channel_id=1, source_target_pairs={{0,8},{8,0},{1,9},{9,1},{2,10},{10,2},{3,11},{11,3},{4,12},{12,4},... | collective-permute-start | bytes 2555912 | tf_op jit(solution)/shard_map/ppermute | solution.py:322
  36.8 0.0 copy-done
  36.8 0.0 copy-done.1
  36.8 3.2 %shard_map.60.passages_ref = bf16[768,1024]{1,0:T(8,128)(2,1)S(1)} custom-call(s32[5]{0:T(128)S(1)} %copy-done.1, s32[96,1024]{1,0:T(8,128)S(1)} %bitcast.13, bf16[4,6,8,256]{3,2,1,0:T(8,128)(2,1)S(1)} %pad_maximum_fusion.near_ref, bf16[4,6,8,256]{3,2,1,0:T(8,128)(2,1)S(1)} %collective-permute-done.3.near_cross_ref, ...), custom_call_target="tpu_custom_call" | custom-call | flops 1000000 | bytes 65536 | tf_op jit(solution)/shard_map/pallas_call | solution.py:284
  40.0 0.0 collective-permute-done.6.other_ref
  40.0 2.4 %shard_map.61 = f32[32,8,128]{2,1,0:T(8,128)S(1)} custom-call(bf16[16,208,128]{2,1,0:T(8,128)(2,1)S(1)} %all-to-all-done.own_ref, bf16[16,208,128]{2,1,0:T(8,128)(2,1)S(1)} %collective-permute-done.6.other_ref, bf16[768,1024]{1,0:T(8,128)(2,1)S(1)} %shard_map.60.passages_ref), custom_call_target="tpu_custom_call" | custom-call | flops 1000000 | bytes 65536 | tf_op jit(solution)/shard_map/pallas_call | solution.py:284
  42.4 13.8 %all_to_all.20.stats_ref = f32[32,8,128]{2,1,0:T(8,128)S(1)} all-to-all(f32[32,8,128]{2,1,0:T(8,128)S(1)} %shard_map.61), channel_id=1, replica_groups=mesh['xl'=2,'z'=8,'core'=2,'xh'=2,'y'=4] {'xl','z','core'}, dimensions={0} | all-to-all | bytes 262144 | tf_op jit(solution)/shard_map/all_to_all | solution.py:331
  56.2 9.5 %shard_map.62 = (f32[512,768]{1,0:T(8,128)S(1)}, f32[512,768]{1,0:T(8,128)S(1)}, bf16[768,1024]{1,0:T(8,128)(2,1)S(1)}) custom-call(s32[5]{0:T(128)S(1)} %copy-done.1, f32[32,8,128]{2,1,0:T(8,128)S(1)} %all_to_all.20.stats_ref, bf16[16,208,128]{2,1,0:T(8,128)(2,1)S(1)} %all-to-all-done.own_ref, bf16[16,208,128]{2,1,0:T(8,128)(2,1)S(1)} %collective-permute-done.6.other_ref, ...), custom_call_target="tpu_custom_call" | custom-call | flops 1000000 | bytes 65536 | tf_op jit(solution)/shard_map/pallas_call | solution.py:284
  65.7 1.7 %collective-permute-start.7 = (f32[512,768]{1,0:T(8,128)S(1)}, f32[512,768]{1,0:T(8,128)S(1)}, u32[]{:S(2)}, u32[]{:S(2)}) collective-permute-start(f32[512,768]{1,0:T(8,128)S(1)} %get-tuple-element.24), channel_id=1, source_target_pairs={{0,8},{8,0},{1,9},{9,1},{2,10},{10,2},{3,11},{11,3},{4,12},{12,4},... | collective-permute-start | bytes 4718600 | tf_op jit(solution)/shard_map/ppermute | solution.py:341
  67.4 3.4 %shard_map.64 = f32[8,2,3,16,128]{4,3,2,1,0:T(8,128)S(1)} custom-call(s32[5]{0:T(128)S(1)} %copy-done.1, bf16[768,1024]{1,0:T(8,128)(2,1)S(1)} %get-tuple-element.25.grads_ref, s32[96,1024]{1,0:T(8,128)S(1)} %bitcast.14), custom_call_target="tpu_custom_call" | custom-call | flops 1000000 | bytes 65536 | tf_op jit(solution)/shard_map/pallas_call | solution.py:284
  70.8 0.1 collective-permute-start.8
  70.9 3.4 %shard_map.63 = f32[8,2,3,16,128]{4,3,2,1,0:T(8,128)S(1)} custom-call(s32[5]{0:T(128)S(1)} %copy-done.1, bf16[768,1024]{1,0:T(8,128)(2,1)S(1)} %get-tuple-element.25.grads_ref, s32[96,1024]{1,0:T(8,128)S(1)} %bitcast.15), custom_call_target="tpu_custom_call" | custom-call | flops 1000000 | bytes 65536 | tf_op jit(solution)/shard_map/pallas_call | solution.py:284
  74.3 0.0 collective-permute-done.8
  74.3 0.1 add.11
  74.4 0.0 collective-permute-done.7.cross_ref
  74.4 0.9 shard_map.65
  75.3 0.3 collective-permute-start.9
  75.6 18.2 %all_to_all.21.parts_ref = f32[16,3,16,128]{3,2,1,0:T(8,128)S(1)} all-to-all(f32[16,3,16,128]{3,2,1,0:T(8,128)S(1)} %bitcast.16), channel_id=1, replica_groups=mesh['xl'=2,'z'=8,'core'=2,'xh'=2,'y'=4] {'xh','y','xl'}, dimensions={0} | all-to-all | bytes 786432 | tf_op jit(solution)/shard_map/all_to_all | solution.py:359
  93.8 0.0 collective-permute-done.9.words_ref
  93.8 1.6 %shard_map.66 = s16[8,256,128]{2,1,0:T(8,128)(2,1)S(1)} custom-call(s32[5]{0:T(128)S(1)} %copy-done.1, f32[512,768]{1,0:T(8,128)S(1)} %get-tuple-element.23.sums_ref, f32[512,768]{1,0:T(8,128)S(1)} %collective-permute-done.7.cross_ref, s16[8,208,128]{2,1,0:T(8,128)(2,1)S(1)} %collective-permute-done.9.words_ref, f32[16,3,16,128]{3,2,1,0:T(8,128)S(1)} %all_to_all.21.parts_ref), custom_call_target="tpu_custom_call" | custom-call | flops 1000000 | bytes 65536 | tf_op jit(solution)/shard_map/pallas_call | solution.py:284
  95.4 17.6 %all_to_all.22.words_ref = s16[8,256,128]{2,1,0:T(8,128)(2,1)S(1)} all-to-all(s16[8,256,128]{2,1,0:T(8,128)(2,1)S(1)} %shard_map.66), channel_id=1, replica_groups=mesh['xl'=2,'z'=8,'core'=2,'xh'=2,'y'=4] {'z'}, dimensions={0} | all-to-all | bytes 1048576 | tf_op jit(solution)/shard_map/all_to_all | solution.py:368
  112.9 0.8 shard_map.67
  113.8 3.9 %collective-permute-start.12 = (f32[48,128]{1,0:T(8,128)S(1)}, f32[48,128]{1,0:T(8,128)S(1)}, u32[]{:S(2)}, u32[]{:S(2)}) collective-permute-start(f32[48,128]{1,0:T(8,128)S(1)} %get-tuple-element.29.own_ref), channel_id=1, source_target_pairs={{0,136},{8,128},{128,8},{136,0},{1,137},{9,129},{129,9},{137,1},{2... | collective-permute-start | bytes 73736 | tf_op jit(solution)/shard_map/ppermute | solution.py:371
  117.6 0.0 collective-permute-start.11
  117.6 0.8 collective-permute-start.10
  118.4 0.7 collective-permute-done.12.corner_ref
  119.1 0.0 collective-permute-done.11.cross_ref
  119.2 1.2 collective-permute-done.10.beside_ref
  120.3 1.3 %shard_map.68 = f32[12,8,256]{2,1,0:T(8,128)} custom-call(s32[5]{0:T(128)S(1)} %copy-done.1, f32[48,128]{1,0:T(8,128)S(1)} %get-tuple-element.29.own_ref, f32[48,128]{1,0:T(8,128)S(1)} %collective-permute-done.10.beside_ref, f32[48,128]{1,0:T(8,128)S(1)} %collective-permute-done.11.cross_ref, f32[48,128]{1,0:T(8,128)S(1)} %collective-permute-done.12.corner_ref), custom_call_target="tpu_custom_call" | custom-call | flops 1000000 | bytes 65536 | tf_op jit(solution)/shard_map/pallas_call | solution.py:284
  (1 shorter events, 0.0 us)
Async XLA Ops:
  0.6 36.1 %copy-start = (s32[1,96,1024]{2,1,0:T(8,128)S(1)}, s32[1,96,1024]{2,1,0:T(8,128)}, u32[]{:S(2)}) copy-start(s32[1,96,1024]{2,1,0:T(8,128)} %param.5) | copy-start | bytes 1179652
  1.3 35.5 %copy-start.1 = (s32[5]{0:T(128)S(1)}, s32[5]{0:T(128)}, u32[]{:S(2)}) copy-start(s32[5]{0:T(128)} %stack.38.place_ref) | copy-start | bytes 64
  3.1 10.2 %copy-start.2 = (bf16[6,8,256]{2,1,0:T(8,128)(2,1)S(1)}, bf16[6,8,256]{2,1,0:T(8,128)(2,1)}, u32[]{:S(2)}) copy-start(bf16[6,8,256]{2,1,0:T(8,128)(2,1)} %get-tuple-element.17) | copy-start | bytes 73732
  3.1 31.2 %all-to-all-start = ((bf16[16,208,128]{2,1,0:T(8,128)(2,1)}), bf16[16,208,128]{2,1,0:T(8,128)(2,1)S(1)}, u32[]{:S(2)}, u32[]{:S(2)}) async-start(bf16[16,208,128]{2,1,0:T(8,128)(2,1)} %get-tuple-element.16), calls=%async_computation | async-start | bytes 1703936 | tf_op jit(solution)/shard_map/all_to_all | solution.py:320
  13.3 3.9 %collective-permute-start.2 = (bf16[6,8,256]{2,1,0:T(8,128)(2,1)S(1)}, bf16[6,8,256]{2,1,0:T(8,128)(2,1)S(1)}, u32[]{:S(2)}, u32[]{:S(2)}) collective-permute-start(bf16[6,8,256]{2,1,0:T(8,128)(2,1)S(1)} %copy-done.2), channel_id=1, source_target_pairs={{0,3},{1,0},{2,1},{3,2},{4,7},{5,4},{6,5},{7,6},{8,11},{9,8},{10,9... | collective-permute-start | bytes 73736 | tf_op jit(solution)/shard_map/ppermute | solution.py:317
  16.1 4.2 %collective-permute-start.1 = (bf16[6,8,256]{2,1,0:T(8,128)(2,1)S(1)}, bf16[6,8,256]{2,1,0:T(8,128)(2,1)S(1)}, u32[]{:S(2)}, u32[]{:S(2)}) collective-permute-start(bf16[6,8,256]{2,1,0:T(8,128)(2,1)S(1)} %copy-done.2), channel_id=1, source_target_pairs={{0,2},{1,3},{2,0},{3,1},{4,6},{5,7},{6,4},{7,5},{8,10},{9,11},{10,... | collective-permute-start | bytes 73736 | tf_op jit(solution)/shard_map/ppermute | solution.py:317
  16.5 4.1 %collective-permute-start = (bf16[6,8,256]{2,1,0:T(8,128)(2,1)S(1)}, bf16[6,8,256]{2,1,0:T(8,128)(2,1)S(1)}, u32[]{:S(2)}, u32[]{:S(2)}) collective-permute-start(bf16[6,8,256]{2,1,0:T(8,128)(2,1)S(1)} %copy-done.2), channel_id=1, source_target_pairs={{0,1},{1,2},{2,3},{3,0},{4,5},{5,6},{6,7},{7,4},{8,9},{9,10},{10,1... | collective-permute-start | bytes 73736 | tf_op jit(solution)/shard_map/ppermute | solution.py:317
  20.6 6.5 %collective-permute-start.4 = (bf16[4,6,8,256]{3,2,1,0:T(8,128)(2,1)S(1)}, bf16[4,6,8,256]{3,2,1,0:T(8,128)(2,1)S(1)}, u32[]{:S(2)}, u32[]{:S(2)}) collective-permute-start(bf16[4,6,8,256]{3,2,1,0:T(8,128)(2,1)S(1)} %pad_maximum_fusion.near_ref), channel_id=1, source_target_pairs={{0,4},{4,0},{1,5},{5,1},{2,6},{6,2},{3,7},{7,3},{8,12},{12,8},{9,1... | collective-permute-start | bytes 294920 | tf_op jit(solution)/shard_map/ppermute | solution.py:319
  23.1 7.2 %collective-permute-start.3 = (bf16[4,6,8,256]{3,2,1,0:T(8,128)(2,1)S(1)}, bf16[4,6,8,256]{3,2,1,0:T(8,128)(2,1)S(1)}, u32[]{:S(2)}, u32[]{:S(2)}) collective-permute-start(bf16[4,6,8,256]{3,2,1,0:T(8,128)(2,1)S(1)} %pad_maximum_fusion.near_ref), channel_id=1, source_target_pairs={{0,8},{8,0},{1,9},{9,1},{2,10},{10,2},{3,11},{11,3},{4,12},{12,4},... | collective-permute-start | bytes 294920 | tf_op jit(solution)/shard_map/ppermute | solution.py:321
  27.1 4.2 %collective-permute-start.5 = (bf16[4,6,8,256]{3,2,1,0:T(8,128)(2,1)S(1)}, bf16[4,6,8,256]{3,2,1,0:T(8,128)(2,1)S(1)}, u32[]{:S(2)}, u32[]{:S(2)}) collective-permute-start(bf16[4,6,8,256]{3,2,1,0:T(8,128)(2,1)S(1)} %collective-permute-done.4.far_ref), channel_id=1, source_target_pairs={{0,8},{8,0},{1,9},{9,1},{2,10},{10,2},{3,11},{11,3},{4,12},{12,4},... | collective-permute-start | bytes 294920 | tf_op jit(solution)/shard_map/ppermute | solution.py:321
  34.3 5.7 %collective-permute-start.6 = (bf16[16,208,128]{2,1,0:T(8,128)(2,1)S(1)}, bf16[16,208,128]{2,1,0:T(8,128)(2,1)S(1)}, u32[]{:S(2)}, u32[]{:S(2)}) collective-permute-start(bf16[16,208,128]{2,1,0:T(8,128)(2,1)S(1)} %all-to-all-done.own_ref), channel_id=1, source_target_pairs={{0,8},{8,0},{1,9},{9,1},{2,10},{10,2},{3,11},{11,3},{4,12},{12,4},... | collective-permute-start | bytes 2555912 | tf_op jit(solution)/shard_map/ppermute | solution.py:322
  65.7 8.6 %collective-permute-start.7 = (f32[512,768]{1,0:T(8,128)S(1)}, f32[512,768]{1,0:T(8,128)S(1)}, u32[]{:S(2)}, u32[]{:S(2)}) collective-permute-start(f32[512,768]{1,0:T(8,128)S(1)} %get-tuple-element.24), channel_id=1, source_target_pairs={{0,8},{8,0},{1,9},{9,1},{2,10},{10,2},{3,11},{11,3},{4,12},{12,4},... | collective-permute-start | bytes 4718600 | tf_op jit(solution)/shard_map/ppermute | solution.py:341
  70.8 3.5 %collective-permute-start.8 = (f32[8,2,3,16,128]{4,3,2,1,0:T(8,128)S(1)}, f32[8,2,3,16,128]{4,3,2,1,0:T(8,128)S(1)}, u32[]{:S(2)}, u32[]{:S(2)}) collective-permute-start(f32[8,2,3,16,128]{4,3,2,1,0:T(8,128)S(1)} %shard_map.64), channel_id=1, source_target_pairs={{0,8},{8,0},{1,9},{9,1},{2,10},{10,2},{3,11},{11,3},{4,12},{12,4},... | collective-permute-start | bytes 1179656 | tf_op jit(solution)/shard_map/ppermute | solution.py:352
  75.3 18.5 %collective-permute-start.9 = (s16[8,208,128]{2,1,0:T(8,128)(2,1)S(1)}, s16[8,208,128]{2,1,0:T(8,128)(2,1)S(1)}, u32[]{:S(2)}, u32[]{:S(2)}) collective-permute-start(s16[8,208,128]{2,1,0:T(8,128)(2,1)S(1)} %shard_map.65), channel_id=1, source_target_pairs={{0,128},{128,0},{1,129},{129,1},{2,130},{130,2},{3,131},{131,3},{4... | collective-permute-start | bytes 1277960 | tf_op jit(solution)/shard_map/ppermute | solution.py:358
  113.8 5.4 %collective-permute-start.12 = (f32[48,128]{1,0:T(8,128)S(1)}, f32[48,128]{1,0:T(8,128)S(1)}, u32[]{:S(2)}, u32[]{:S(2)}) collective-permute-start(f32[48,128]{1,0:T(8,128)S(1)} %get-tuple-element.29.own_ref), channel_id=1, source_target_pairs={{0,136},{8,128},{128,8},{136,0},{1,137},{9,129},{129,9},{137,1},{2... | collective-permute-start | bytes 73736 | tf_op jit(solution)/shard_map/ppermute | solution.py:371
  117.6 1.5 %collective-permute-start.11 = (f32[48,128]{1,0:T(8,128)S(1)}, f32[48,128]{1,0:T(8,128)S(1)}, u32[]{:S(2)}, u32[]{:S(2)}) collective-permute-start(f32[48,128]{1,0:T(8,128)S(1)} %get-tuple-element.29.own_ref), channel_id=1, source_target_pairs={{0,8},{8,0},{1,9},{9,1},{2,10},{10,2},{3,11},{11,3},{4,12},{12,4},... | collective-permute-start | bytes 73736 | tf_op jit(solution)/shard_map/ppermute | solution.py:372
  117.6 2.7 %collective-permute-start.10 = (f32[48,128]{1,0:T(8,128)S(1)}, f32[48,128]{1,0:T(8,128)S(1)}, u32[]{:S(2)}, u32[]{:S(2)}) collective-permute-start(f32[48,128]{1,0:T(8,128)S(1)} %get-tuple-element.29.own_ref), channel_id=1, source_target_pairs={{0,128},{128,0},{1,129},{129,1},{2,130},{130,2},{3,131},{131,3},{4... | collective-permute-start | bytes 73736 | tf_op jit(solution)/shard_map/ppermute | solution.py:370

commit v4 on v3

--- a/solution.py
+++ b/solution.py
@@ -46,7 +46,7 @@
     return jnp.exp2(jnp.transpose(jnp.broadcast_to(row, (LANES, LANES)))[:count])
 
 
-def spread_kernel(place_ref, queries_ref, positives_ref, book_ref, out_ref, share_ref):
+def spread_kernel(queries_ref, positives_ref, out_ref):
     size, width = queries_ref.shape
     target = jnp.concatenate([positives_ref[...], jnp.zeros((1, LANES - size), i32)], axis=1)
     tail = jnp.concatenate([target // LANES, target % LANES, jnp.zeros((14, LANES), i32)], axis=0)
@@ -55,6 +55,9 @@
         for t in range(width // LANES):
             out_ref[c, t * size : (t + 1) * size] = queries_ref[:, t * LANES : (t + 1) * LANES]
         out_ref[c, width // LANES * size :] = tail
+
+
+def share_kernel(place_ref, book_ref, share_ref):
     count = share_ref.shape[0]
     share_ref[...] = book_ref[pl.ds(place_ref[0] * count, count)]
 
@@ -108,16 +111,24 @@
     lax.fori_loop(0, codes_ref.shape[0] // 2, pair, 0, unroll=8)
 
 
-def scores_kernel(own_ref, other_ref, passages_ref, stats_ref):
-    for b in range(4):
-        rows = query_rows(own_ref if b < 2 else other_ref, b % 2 * 8, 8)
-        tile = jnp.dot(rows, passages_ref[...], preferred_element_type=f32)
+def local_logs(pack_ref, passages_ref):
+    rows = []
+    for b in range(2):
+        tile = jnp.dot(query_rows(pack_ref, b * 8, 8), passages_ref[...], preferred_element_type=f32)
         peak = jnp.max(tile, axis=1, keepdims=True)
         total = jnp.sum(jnp.exp(tile - peak), axis=1, keepdims=True)
         row = as_row(peak + jnp.log(total))
-        for j in range(2):
-            piece = row[:, j * LANES : (j + 1) * LANES]
-            stats_ref[:, 2 * b + j : 2 * b + j + 1, :] = jnp.broadcast_to(piece[None], (stats_ref.shape[0], 1, LANES))
+        rows += [row[:, j * LANES : (j + 1) * LANES] for j in range(2)]
+    return jnp.concatenate(rows, axis=0)
+
+
+def own_scores_kernel(pack_ref, passages_ref, logs_ref):
+    logs_ref[...] = local_logs(pack_ref, passages_ref)
+
+
+def other_scores_kernel(pack_ref, passages_ref, own_logs_ref, stats_ref):
+    logs = jnp.concatenate([own_logs_ref[...], local_logs(pack_ref, passages_ref)], axis=0)
+    stats_ref[...] = jnp.broadcast_to(logs[None], stats_ref.shape)
 
 
 def log_totals(core, stats_ref, h):
@@ -132,7 +143,8 @@
 
 
 def weights_kernel(
-    place_ref, stats_ref, own_ref, other_ref, passages_ref, other_sums_ref, own_sums_ref, grads_ref, high_ref, low_ref
+    place_ref, stats_ref, own_ref, other_ref, passages_ref, other_sums_ref, own_sums_ref, grads_ref,
+    high_ref, low_ref, turned_ref
 ):
     core, offset = place_ref[0], place_ref[1]
     half, passage_count = own_sums_ref.shape[0], passages_ref.shape[1]
@@ -140,6 +152,9 @@
     passages = passages_ref[...]
     spot = lax.broadcasted_iota(i32, (size, passage_count), 1) + offset
     for h, pack_ref, sums_ref in ((1, other_ref, other_sums_ref), (0, own_ref, own_sums_ref)):
+        for t in range(turned_ref.shape[0] // LANES):
+            columns = query_columns(pack_ref, t, 0, pack_ref.shape[0])
+            turned_ref[t * LANES : (t + 1) * LANES, h * half : (h + 1) * half] = jnp.transpose(columns)
         totals = [as_column(row) for row in log_totals(core, stats_ref, h)]
         targets = target_columns(pack_ref)[:size].astype(i32)
         for b in range(half // BLOCK):
@@ -159,44 +174,35 @@
             sums_ref[b * BLOCK : (b + 1) * BLOCK] = lax.dot_general(
                 high, passages, ROWS_BY_ROWS, preferred_element_type=f32
             ) + lax.dot_general(low, passages, ROWS_BY_ROWS, preferred_element_type=f32)
-    chips = own_ref.shape[0]
-    for t in range(3):
-        turned = jnp.concatenate(
-            [
-                jnp.concatenate(
-                    [jnp.transpose(query_columns(pack_ref, 2 * t + k, 0, chips)) for pack_ref in (own_ref, other_ref)],
-                    axis=1,
-                )
-                for k in range(2)
-            ],
-            axis=0,
+    for n in range(passage_count // BLOCK):
+        columns = slice(n * BLOCK, (n + 1) * BLOCK)
+        grad = jnp.dot(turned_ref[...], high_ref[:, columns], preferred_element_type=f32) + jnp.dot(
+            turned_ref[...], low_ref[:, columns], preferred_element_type=f32
         )
-        grad = jnp.dot(turned, high_ref[...], preferred_element_type=f32) + jnp.dot(
-            turned, low_ref[...], preferred_element_type=f32
-        )
-        grads_ref[t * BLOCK : (t + 1) * BLOCK] = grad.astype(bf16)
+        grads_ref[:, columns] = grad.astype(bf16)
 
 
 def codeword_kernel(mine, place_ref, grads_ref, codes_ref, out_ref):
     core = place_ref[0] if mine else 1 - place_ref[0]
-    word = lax.broadcasted_iota(i32, (32, codes_ref.shape[1]), 0)
-
-    def four(j, carry):
+    word = lax.broadcasted_iota(i32, (64, codes_ref.shape[1]), 0)
+
+    def two(j, carry):
+        first = j // 3 * 12 + 6 * core + 2 * (j % 3)
+        grads = grads_ref[pl.ds(pl.multiple_of(8 * first, 16), 16), :].astype(f32)
         sums = []
-        for m in range(4):
-            grad = grads_ref[pl.ds(pl.multiple_of(32 * j + 16 * (m // 2), 16), 16), :].astype(f32)
-            grad = grad[m % 2 * 8 : m % 2 * 8 + 8]
-            code = codes_ref[pl.ds(4 * j + m, 1), :]
-            high = (code >> 5) - 4 * core
+        for m in range(2):
+            grad = grads[8 * m : 8 * m + 8]
+            code = codes_ref[pl.ds(first + m, 1), :]
+            high = code >> 6
             parts = jnp.concatenate([jnp.where(high == t, grad, 0.0) for t in range(4)], axis=0).astype(bf16)
-            onehot = jnp.where((code & 31) == word, 1.0, 0.0).astype(bf16)
+            onehot = jnp.where((code & 63) == word, 1.0, 0.0).astype(bf16)
             sums.append(lax.dot_general(parts, onehot, ROWS_BY_ROWS, preferred_element_type=f32))
         sums = jnp.concatenate(sums, axis=1)
         for k in range(2):
             out_ref[j // 3, k, j % 3] = sums[16 * k : 16 * k + 16]
         return carry
 
-    lax.fori_loop(0, codes_ref.shape[0] // 4, four, 0, unroll=8)
+    lax.fori_loop(0, codes_ref.shape[0] // 4, two, 0, unroll=8)
 
 
 def put_query_words(chunk, out_ref, c):
@@ -263,10 +269,11 @@
     all_ref[2 * core + 1 - side] = beside_ref[...]
     all_ref[2 - 2 * core + side] = cross_ref[...]
     all_ref[2 - 2 * core + 1 - side] = corner_ref[...]
-    for j in range(3):
-        rows = [all_ref[t // 2, 16 * j + t % 2 * 8 : 16 * j + t % 2 * 8 + 8] for t in range(8)]
-        for m in range(4):
-            out_ref[4 * j + m] = jnp.concatenate([row[:, 32 * m : 32 * m + 32] for row in rows], axis=1)
+    for c in range(2):
+        for j in range(3):
+            rows = [all_ref[2 * c + t // 2, 16 * j + t % 2 * 8 : 16 * j + t % 2 * 8 + 8] for t in range(4)]
+            for m in range(2):
+                out_ref[6 * c + 2 * j + m] = jnp.concatenate([row[:, 64 * m : 64 * m + 64] for row in rows], axis=1)
 
 
 IN_VMEM = pl.BlockSpec(memory_space=pltpu.VMEM)
@@ -306,35 +313,40 @@
     place = jnp.stack([axes[0], offset, *axes[1:]]).astype(i32)
     scalar = {0: IN_SMEM}
     length = width // LANES * size + 16
-    own, share = call(
-        spread_kernel,
-        [shape((chips, length, LANES), bf16), shape((codebook.shape[0] // 2, *codebook.shape[1:]), bf16)],
-        (place, queries[0], positives, codebook),
+    own = call(spread_kernel, shape((chips, length, LANES), bf16), (queries[0], positives), 10**6, vmem=60)
+    share = call(
+        share_kernel,
+        shape((codebook.shape[0] // 2, *codebook.shape[1:]), bf16),
+        (place, codebook),
         10**6,
         special=scalar,
-        vmem=60,
     )
     near = [share] + [lax.ppermute(share, "y", [(i, (i + k) % 4) for i in range(4)]) for k in range(1, 4)]
     near = jnp.stack(near)
     far = lax.ppermute(near, "xh", [(0, 1), (1, 0)])
     own = lax.all_to_all(own, CHIP, 0, 0)
-    own, *books = lax.optimization_barrier((own, near, swap(near), far, swap(far)))
-    other = swap(own)
     passages = call(
         decode_kernel,
         shape((width, passage_count), bf16),
-        (place, own_codes, *books),
+        (place, own_codes, near, swap(near), far, swap(far)),
         10**6,
         special=scalar,
     )
-    stats = call(scores_kernel, shape((32, 8, LANES), f32), (own, other, passages), 10**6)
+    own, passages = lax.optimization_barrier((own, passages))
+    other = swap(own)
+    own_logs = call(own_scores_kernel, shape((4, LANES), f32), (own, passages), 10**6)
+    stats = call(other_scores_kernel, shape((32, 8, LANES), f32), (other, passages, own_logs), 10**6)
     stats = lax.all_to_all(stats, CHIP + ("core",), 0, 0, tiled=True)
     query_other, query_own, grads = call(
         weights_kernel,
         [shape((half, width), f32), shape((half, width), f32), shape((width, passage_count), bf16)],
         (place, stats, own, other, passages),
         10**6,
-        scratch=[pltpu.VMEM((2 * half, passage_count), bf16), pltpu.VMEM((2 * half, passage_count), bf16)],
+        scratch=[
+            pltpu.VMEM((2 * half, passage_count), bf16),
+            pltpu.VMEM((2 * half, passage_count), bf16),
+            pltpu.VMEM((width, 2 * half), bf16),
+        ],
         special=scalar,
         vmem=20,
     )

time: 122 us -> 120 us (0.984)
  blocking collectives: 49.6 us -> 52.2 us
  waiting for transfers between devices: 10.4 us -> 8.79 us
  starting transfers between devices: 31.8 us -> 30.4 us
    all_to_all x1, blocking collectives: 13.8 us -> 17.4 us  [per_device(): stats = lax.all_to_all(stats, CHIP + ('core',), 0, 0, tiled=True)]
    all_to_all x1, waiting for transfers between devices: 2.98 us -> 0.01 us  [per_device(): own = lax.all_to_all(own, CHIP, 0, 0)]
    pallas_call x10 -> x12, Pallas kernels: 28.4 us -> 27.3 us  [call(): pl.pallas_call(kernel, out_shape=shapes, in_specs=specs, out_specs=outs i...]
  transfers between devices with their start and end apart: 14 -> 14, of which waited for: 7 -> 7; matrix products, arithmetic and copies ran while one was open for 0% -> 0% of each run, Pallas kernels for 8% -> 9%
where the time goes in v4:
time: 120 us
  blocking collectives  52.2 us (44%)
  starting transfers between devices  30.4 us (25%)
  Pallas kernels  27.3 us (23%)
  waiting for transfers between devices  8.79 us (7%)
    pallas_call x12, Pallas kernels, call(): pl.pallas_call(kernel, out_shape=shapes, in_specs=specs, out_specs=outs i...  27.3 us
    all_to_all x1, blocking collectives, per_device(): words = lax.all_to_all(words, 'z', 0, 0)  17.6 us
    all_to_all x1, blocking collectives, per_device(): stats = lax.all_to_all(stats, CHIP + ('core',), 0, 0, tiled=True)  17.4 us
    all_to_all x1, blocking collectives, per_device(): lax.all_to_all(parts.reshape(16, subspaces // 32, 16, LANES), SUB + ('xl'...  17.2 us
    all_to_all x1, starting transfers between devices, per_device(): own = lax.all_to_all(own, CHIP, 0, 0)  10 us
    ppermute x1, starting transfers between devices, per_device(): corner = lax.ppermute(sums, ('xl', 'core'), [(i, 3 - i) for i in range(4)])  4.15 us
    ppermute x3, starting transfers between devices, per_device(): lax.ppermute(share, 'y', [(i, (i + k) % 4) for i in range(4)])  3.85 us
    ppermute x3, waiting for transfers between devices, per_device(): lax.ppermute(share, 'y', [(i, (i + k) % 4) for i in range(4)])  3.7 us
  transfers between devices with their start and end apart: 14, of which 7 were waited for; matrix products, arithmetic and copies ran while one was open for 0% of the time, Pallas kernels for 9%

profile of v4, /device:TPU:1, one launch (start us, length us, event | category | flops | bytes accessed | tf_op | source)
XLA Modules:
  0.0 119.6 jit_solution(8024229834653659043)
XLA Ops:
  0.6 0.0 copy-start.1
  0.6 0.0 copy-start
  0.7 1.9 %shard_map.59 = bf16[16,208,128]{2,1,0:T(8,128)(2,1)} custom-call(bf16[32,768]{1,0:T(8,128)(2,1)} %bitcast.18, s32[1,32]{1,0:T(1,128)} %positives_ref.1), custom_call_target="tpu_custom_call" | custom-call | flops 1000000 | bytes 65536 | tf_op jit(solution)/shard_map/pallas_call | solution.py:291
  2.5 10.0 %all-to-all-start = ((bf16[16,208,128]{2,1,0:T(8,128)(2,1)}), bf16[16,208,128]{2,1,0:T(8,128)(2,1)S(1)}, u32[]{:S(2)}, u32[]{:S(2)}) async-start(bf16[16,208,128]{2,1,0:T(8,128)(2,1)} %shard_map.59), calls=%async_computation | async-start | bytes 1703936 | tf_op jit(solution)/shard_map/all_to_all | solution.py:327
  12.6 0.1 stack.38.place_ref
  12.7 0.0 copy-done.1
  12.7 0.5 shard_map.60
  13.2 2.8 %collective-permute-start.2 = (bf16[6,8,256]{2,1,0:T(8,128)(2,1)S(1)}, bf16[6,8,256]{2,1,0:T(8,128)(2,1)S(1)}, u32[]{:S(2)}, u32[]{:S(2)}) collective-permute-start(bf16[6,8,256]{2,1,0:T(8,128)(2,1)S(1)} %shard_map.60), channel_id=1, source_target_pairs={{0,3},{1,0},{2,1},{3,2},{4,7},{5,4},{6,5},{7,6},{8,11},{9,8},{10,9... | collective-permute-start | bytes 73736 | tf_op jit(solution)/shard_map/ppermute | solution.py:324
  16.0 0.3 collective-permute-start.1
  16.4 0.7 collective-permute-start
  17.1 0.0 collective-permute-done.2
  17.1 3.2 %collective-permute-done.1 = bf16[6,8,256]{2,1,0:T(8,128)(2,1)S(1)} collective-permute-done((bf16[6,8,256]{2,1,0:T(8,128)(2,1)S(1)}, bf16[6,8,256]{2,1,0:T(8,128)(2,1)S(1)}, u32[]{:S(2)}, u32[]{:S(2)}) %collective-permute-start.1) | collective-permute-done | bytes 24608 | tf_op jit(solution)/shard_map/ppermute | solution.py:324
  20.2 0.5 collective-permute-done
  20.8 2.5 %collective-permute-start.4 = (bf16[4,6,8,256]{3,2,1,0:T(8,128)(2,1)S(1)}, bf16[4,6,8,256]{3,2,1,0:T(8,128)(2,1)S(1)}, u32[]{:S(2)}, u32[]{:S(2)}) collective-permute-start(bf16[4,6,8,256]{3,2,1,0:T(8,128)(2,1)S(1)} %pad_maximum_fusion.near_ref), channel_id=1, source_target_pairs={{0,4},{4,0},{1,5},{5,1},{2,6},{6,2},{3,7},{7,3},{8,12},{12,8},{9,1... | collective-permute-start | bytes 294920 | tf_op jit(solution)/shard_map/ppermute | solution.py:326
  23.3 2.4 %collective-permute-start.3 = (bf16[4,6,8,256]{3,2,1,0:T(8,128)(2,1)S(1)}, bf16[4,6,8,256]{3,2,1,0:T(8,128)(2,1)S(1)}, u32[]{:S(2)}, u32[]{:S(2)}) collective-permute-start(bf16[4,6,8,256]{3,2,1,0:T(8,128)(2,1)S(1)} %pad_maximum_fusion.near_ref), channel_id=1, source_target_pairs={{0,8},{8,0},{1,9},{9,1},{2,10},{10,2},{3,11},{11,3},{4,12},{12,4},... | collective-permute-start | bytes 294920 | tf_op jit(solution)/shard_map/ppermute | solution.py:331
  25.8 1.2 %collective-permute-done.4.far_ref = bf16[4,6,8,256]{3,2,1,0:T(8,128)(2,1)S(1)} collective-permute-done((bf16[4,6,8,256]{3,2,1,0:T(8,128)(2,1)S(1)}, bf16[4,6,8,256]{3,2,1,0:T(8,128)(2,1)S(1)}, u32[]{:S(2)}, u32[]{:S(2)}) %collective-permute-start.4) | collective-permute-done | bytes 98336 | tf_op jit(solution)/shard_map/ppermute | solution.py:326
  27.0 3.3 %collective-permute-start.5 = (bf16[4,6,8,256]{3,2,1,0:T(8,128)(2,1)S(1)}, bf16[4,6,8,256]{3,2,1,0:T(8,128)(2,1)S(1)}, u32[]{:S(2)}, u32[]{:S(2)}) collective-permute-start(bf16[4,6,8,256]{3,2,1,0:T(8,128)(2,1)S(1)} %collective-permute-done.4.far_ref), channel_id=1, source_target_pairs={{0,8},{8,0},{1,9},{9,1},{2,10},{10,2},{3,11},{11,3},{4,12},{12,4},... | collective-permute-start | bytes 294920 | tf_op jit(solution)/shard_map/ppermute | solution.py:331
  30.3 0.0 collective-permute-done.3.near_cross_ref
  30.3 0.9 collective-permute-done.5.far_cross_ref
  31.3 0.0 copy-done
  31.3 3.2 %shard_map.61.passages_ref = bf16[768,1024]{1,0:T(8,128)(2,1)S(1)} custom-call(s32[5]{0:T(128)S(1)} %stack.38.place_ref, s32[96,1024]{1,0:T(8,128)S(1)} %bitcast.13, bf16[4,6,8,256]{3,2,1,0:T(8,128)(2,1)S(1)} %pad_maximum_fusion.near_ref, bf16[4,6,8,256]{3,2,1,0:T(8,128)(2,1)S(1)} %collective-permute-done.3.near_cross_ref, ...), custom_call_target="tpu_custom_call" | custom-call | flops 1000000 | bytes 65536 | tf_op jit(solution)/shard_map/pallas_call | solution.py:291
  34.5 0.0 all-to-all-done.pack_ref.own_ref
  34.5 1.5 %collective-permute-start.6 = (bf16[16,208,128]{2,1,0:T(8,128)(2,1)S(1)}, bf16[16,208,128]{2,1,0:T(8,128)(2,1)S(1)}, u32[]{:S(2)}, u32[]{:S(2)}) collective-permute-start(bf16[16,208,128]{2,1,0:T(8,128)(2,1)S(1)} %all-to-all-done.pack_ref.own_ref), channel_id=1, source_target_pairs={{0,8},{8,0},{1,9},{9,1},{2,10},{10,2},{3,11},{11,3},{4,12},{12,4},... | collective-permute-start | bytes 2555912 | tf_op jit(solution)/shard_map/ppermute | solution.py:336
  36.0 1.3 %shard_map.62.own_logs_ref = f32[4,128]{1,0:T(4,128)S(1)} custom-call(bf16[16,208,128]{2,1,0:T(8,128)(2,1)S(1)} %all-to-all-done.pack_ref.own_ref, bf16[768,1024]{1,0:T(8,128)(2,1)S(1)} %shard_map.61.passages_ref), custom_call_target="tpu_custom_call" | custom-call | flops 1000000 | bytes 65536 | tf_op jit(solution)/shard_map/pallas_call | solution.py:291
  37.3 0.7 collective-permute-done.6.pack_ref.other_ref
  38.0 1.3 %shard_map.63 = f32[32,8,128]{2,1,0:T(8,128)S(1)} custom-call(bf16[16,208,128]{2,1,0:T(8,128)(2,1)S(1)} %collective-permute-done.6.pack_ref.other_ref, bf16[768,1024]{1,0:T(8,128)(2,1)S(1)} %shard_map.61.passages_ref, f32[4,128]{1,0:T(4,128)S(1)} %shard_map.62.own_logs_ref), custom_call_target="tpu_custom_call" | custom-call | flops 1000000 | bytes 65536 | tf_op jit(solution)/shard_map/pallas_call | solution.py:291
  39.3 17.4 %all_to_all.20.stats_ref = f32[32,8,128]{2,1,0:T(8,128)S(1)} all-to-all(f32[32,8,128]{2,1,0:T(8,128)S(1)} %shard_map.63), channel_id=1, replica_groups=mesh['xl'=2,'z'=8,'core'=2,'xh'=2,'y'=4] {'xl','z','core'}, dimensions={0} | all-to-all | bytes 262144 | tf_op jit(solution)/shard_map/all_to_all | solution.py:339
  56.7 9.0 %shard_map.64 = (f32[512,768]{1,0:T(8,128)S(1)}, f32[512,768]{1,0:T(8,128)S(1)}, bf16[768,1024]{1,0:T(8,128)(2,1)S(1)}) custom-call(s32[5]{0:T(128)S(1)} %stack.38.place_ref, f32[32,8,128]{2,1,0:T(8,128)S(1)} %all_to_all.20.stats_ref, bf16[16,208,128]{2,1,0:T(8,128)(2,1)S(1)} %all-to-all-done.pack_ref.own_ref, ...), custom_call_target="tpu_custom_call" | custom-call | flops 1000000 | bytes 65536 | tf_op jit(solution)/shard_map/pallas_call | solution.py:291
  65.7 1.7 %collective-permute-start.7 = (f32[512,768]{1,0:T(8,128)S(1)}, f32[512,768]{1,0:T(8,128)S(1)}, u32[]{:S(2)}, u32[]{:S(2)}) collective-permute-start(f32[512,768]{1,0:T(8,128)S(1)} %get-tuple-element.14), channel_id=1, source_target_pairs={{0,8},{8,0},{1,9},{9,1},{2,10},{10,2},{3,11},{11,3},{4,12},{12,4},... | collective-permute-start | bytes 4718600 | tf_op jit(solution)/shard_map/ppermute | solution.py:353
  67.4 2.8 %shard_map.66 = f32[8,2,3,16,128]{4,3,2,1,0:T(8,128)S(1)} custom-call(s32[5]{0:T(128)S(1)} %stack.38.place_ref, bf16[768,1024]{1,0:T(8,128)(2,1)S(1)} %get-tuple-element.15.grads_ref, s32[96,1024]{1,0:T(8,128)S(1)} %bitcast.14), custom_call_target="tpu_custom_call" | custom-call | flops 1000000 | bytes 65536 | tf_op jit(solution)/shard_map/pallas_call | solution.py:291
  70.2 0.1 collective-permute-start.8
  70.2 2.8 %shard_map.65 = f32[8,2,3,16,128]{4,3,2,1,0:T(8,128)S(1)} custom-call(s32[5]{0:T(128)S(1)} %stack.38.place_ref, bf16[768,1024]{1,0:T(8,128)(2,1)S(1)} %get-tuple-element.15.grads_ref, s32[96,1024]{1,0:T(8,128)S(1)} %bitcast.15), custom_call_target="tpu_custom_call" | custom-call | flops 1000000 | bytes 65536 | tf_op jit(solution)/shard_map/pallas_call | solution.py:291
  73.0 0.0 collective-permute-done.8
  73.0 0.1 add.11
  73.1 0.0 collective-permute-done.7.cross_ref
  73.1 0.9 shard_map.67
  74.0 0.3 collective-permute-start.9
  74.3 17.2 %all_to_all.21.parts_ref = f32[16,3,16,128]{3,2,1,0:T(8,128)S(1)} all-to-all(f32[16,3,16,128]{3,2,1,0:T(8,128)S(1)} %bitcast.17), channel_id=1, replica_groups=mesh['xl'=2,'z'=8,'core'=2,'xh'=2,'y'=4] {'xh','y','xl'}, dimensions={0} | all-to-all | bytes 786432 | tf_op jit(solution)/shard_map/all_to_all | solution.py:371
  91.5 0.0 collective-permute-done.9.words_ref
  91.5 1.6 %shard_map.68 = s16[8,256,128]{2,1,0:T(8,128)(2,1)S(1)} custom-call(s32[5]{0:T(128)S(1)} %stack.38.place_ref, f32[512,768]{1,0:T(8,128)S(1)} %get-tuple-element.13.sums_ref, f32[512,768]{1,0:T(8,128)S(1)} %collective-permute-done.7.cross_ref, s16[8,208,128]{2,1,0:T(8,128)(2,1)S(1)} %collective-permute-done.9.words_ref, ...), custom_call_target="tpu_custom_call" | custom-call | flops 1000000 | bytes 65536 | tf_op jit(solution)/shard_map/pallas_call | solution.py:291
  93.1 17.6 %all_to_all.22.words_ref = s16[8,256,128]{2,1,0:T(8,128)(2,1)S(1)} all-to-all(s16[8,256,128]{2,1,0:T(8,128)(2,1)S(1)} %shard_map.68), channel_id=1, replica_groups=mesh['xl'=2,'z'=8,'core'=2,'xh'=2,'y'=4] {'z'}, dimensions={0} | all-to-all | bytes 1048576 | tf_op jit(solution)/shard_map/all_to_all | solution.py:380
  110.6 0.8 shard_map.69
  111.5 4.1 %collective-permute-start.12 = (f32[48,128]{1,0:T(8,128)S(1)}, f32[48,128]{1,0:T(8,128)S(1)}, u32[]{:S(2)}, u32[]{:S(2)}) collective-permute-start(f32[48,128]{1,0:T(8,128)S(1)} %get-tuple-element.19.own_ref), channel_id=1, source_target_pairs={{0,136},{8,128},{128,8},{136,0},{1,137},{9,129},{129,9},{137,1},{2... | collective-permute-start | bytes 73736 | tf_op jit(solution)/shard_map/ppermute | solution.py:383
  115.6 0.0 collective-permute-start.11
  115.6 0.5 collective-permute-start.10
  116.1 1.3 %collective-permute-done.12.corner_ref = f32[48,128]{1,0:T(8,128)S(1)} collective-permute-done((f32[48,128]{1,0:T(8,128)S(1)}, f32[48,128]{1,0:T(8,128)S(1)}, u32[]{:S(2)}, u32[]{:S(2)}) %collective-permute-start.12) | collective-permute-done | bytes 24608 | tf_op jit(solution)/shard_map/ppermute | solution.py:383
  117.5 0.0 collective-permute-done.11.cross_ref
  117.5 0.8 collective-permute-done.10.beside_ref
  118.3 1.3 %shard_map.70 = f32[12,8,256]{2,1,0:T(8,128)} custom-call(s32[5]{0:T(128)S(1)} %stack.38.place_ref, f32[48,128]{1,0:T(8,128)S(1)} %get-tuple-element.19.own_ref, f32[48,128]{1,0:T(8,128)S(1)} %collective-permute-done.10.beside_ref, f32[48,128]{1,0:T(8,128)S(1)} %collective-permute-done.11.cross_ref, f32[48,128]{1,0:T(8,128)S(1)} %collective-permute-done.12.corner_ref), custom_call_target="tpu_custom_call" | custom-call | flops 1000000 | bytes 65536 | tf_op jit(solution)/shard_map/pallas_call | solution.py:291
  (1 shorter events, 0.0 us)
Async XLA Ops:
  0.6 12.0 %copy-start.1 = (bf16[12,8,256]{2,1,0:T(8,128)(2,1)S(1)}, bf16[12,8,256]{2,1,0:T(8,128)(2,1)}, u32[]{:S(2)}) copy-start(bf16[12,8,256]{2,1,0:T(8,128)(2,1)} %book_ref.1) | copy-start | bytes 147460
  0.6 30.6 %copy-start = (s32[1,96,1024]{2,1,0:T(8,128)S(1)}, s32[1,96,1024]{2,1,0:T(8,128)}, u32[]{:S(2)}) copy-start(s32[1,96,1024]{2,1,0:T(8,128)} %param.5) | copy-start | bytes 1179652
  2.5 32.0 %all-to-all-start = ((bf16[16,208,128]{2,1,0:T(8,128)(2,1)}), bf16[16,208,128]{2,1,0:T(8,128)(2,1)S(1)}, u32[]{:S(2)}, u32[]{:S(2)}) async-start(bf16[16,208,128]{2,1,0:T(8,128)(2,1)} %shard_map.59), calls=%async_computation | async-start | bytes 1703936 | tf_op jit(solution)/shard_map/all_to_all | solution.py:327
  13.2 3.9 %collective-permute-start.2 = (bf16[6,8,256]{2,1,0:T(8,128)(2,1)S(1)}, bf16[6,8,256]{2,1,0:T(8,128)(2,1)S(1)}, u32[]{:S(2)}, u32[]{:S(2)}) collective-permute-start(bf16[6,8,256]{2,1,0:T(8,128)(2,1)S(1)} %shard_map.60), channel_id=1, source_target_pairs={{0,3},{1,0},{2,1},{3,2},{4,7},{5,4},{6,5},{7,6},{8,11},{9,8},{10,9... | collective-permute-start | bytes 73736 | tf_op jit(solution)/shard_map/ppermute | solution.py:324
  16.0 4.2 %collective-permute-start.1 = (bf16[6,8,256]{2,1,0:T(8,128)(2,1)S(1)}, bf16[6,8,256]{2,1,0:T(8,128)(2,1)S(1)}, u32[]{:S(2)}, u32[]{:S(2)}) collective-permute-start(bf16[6,8,256]{2,1,0:T(8,128)(2,1)S(1)} %shard_map.60), channel_id=1, source_target_pairs={{0,2},{1,3},{2,0},{3,1},{4,6},{5,7},{6,4},{7,5},{8,10},{9,11},{10,... | collective-permute-start | bytes 73736 | tf_op jit(solution)/shard_map/ppermute | solution.py:324
  16.4 4.4 %collective-permute-start = (bf16[6,8,256]{2,1,0:T(8,128)(2,1)S(1)}, bf16[6,8,256]{2,1,0:T(8,128)(2,1)S(1)}, u32[]{:S(2)}, u32[]{:S(2)}) collective-permute-start(bf16[6,8,256]{2,1,0:T(8,128)(2,1)S(1)} %shard_map.60), channel_id=1, source_target_pairs={{0,1},{1,2},{2,3},{3,0},{4,5},{5,6},{6,7},{7,4},{8,9},{9,10},{10,1... | collective-permute-start | bytes 73736 | tf_op jit(solution)/shard_map/ppermute | solution.py:324
  20.8 6.2 %collective-permute-start.4 = (bf16[4,6,8,256]{3,2,1,0:T(8,128)(2,1)S(1)}, bf16[4,6,8,256]{3,2,1,0:T(8,128)(2,1)S(1)}, u32[]{:S(2)}, u32[]{:S(2)}) collective-permute-start(bf16[4,6,8,256]{3,2,1,0:T(8,128)(2,1)S(1)} %pad_maximum_fusion.near_ref), channel_id=1, source_target_pairs={{0,4},{4,0},{1,5},{5,1},{2,6},{6,2},{3,7},{7,3},{8,12},{12,8},{9,1... | collective-permute-start | bytes 294920 | tf_op jit(solution)/shard_map/ppermute | solution.py:326
  23.3 7.0 %collective-permute-start.3 = (bf16[4,6,8,256]{3,2,1,0:T(8,128)(2,1)S(1)}, bf16[4,6,8,256]{3,2,1,0:T(8,128)(2,1)S(1)}, u32[]{:S(2)}, u32[]{:S(2)}) collective-permute-start(bf16[4,6,8,256]{3,2,1,0:T(8,128)(2,1)S(1)} %pad_maximum_fusion.near_ref), channel_id=1, source_target_pairs={{0,8},{8,0},{1,9},{9,1},{2,10},{10,2},{3,11},{11,3},{4,12},{12,4},... | collective-permute-start | bytes 294920 | tf_op jit(solution)/shard_map/ppermute | solution.py:331
  27.0 4.2 %collective-permute-start.5 = (bf16[4,6,8,256]{3,2,1,0:T(8,128)(2,1)S(1)}, bf16[4,6,8,256]{3,2,1,0:T(8,128)(2,1)S(1)}, u32[]{:S(2)}, u32[]{:S(2)}) collective-permute-start(bf16[4,6,8,256]{3,2,1,0:T(8,128)(2,1)S(1)} %collective-permute-done.4.far_ref), channel_id=1, source_target_pairs={{0,8},{8,0},{1,9},{9,1},{2,10},{10,2},{3,11},{11,3},{4,12},{12,4},... | collective-permute-start | bytes 294920 | tf_op jit(solution)/shard_map/ppermute | solution.py:331
  34.5 3.5 %collective-permute-start.6 = (bf16[16,208,128]{2,1,0:T(8,128)(2,1)S(1)}, bf16[16,208,128]{2,1,0:T(8,128)(2,1)S(1)}, u32[]{:S(2)}, u32[]{:S(2)}) collective-permute-start(bf16[16,208,128]{2,1,0:T(8,128)(2,1)S(1)} %all-to-all-done.pack_ref.own_ref), channel_id=1, source_target_pairs={{0,8},{8,0},{1,9},{9,1},{2,10},{10,2},{3,11},{11,3},{4,12},{12,4},... | collective-permute-start | bytes 2555912 | tf_op jit(solution)/shard_map/ppermute | solution.py:336
  65.7 7.4 %collective-permute-start.7 = (f32[512,768]{1,0:T(8,128)S(1)}, f32[512,768]{1,0:T(8,128)S(1)}, u32[]{:S(2)}, u32[]{:S(2)}) collective-permute-start(f32[512,768]{1,0:T(8,128)S(1)} %get-tuple-element.14), channel_id=1, source_target_pairs={{0,8},{8,0},{1,9},{9,1},{2,10},{10,2},{3,11},{11,3},{4,12},{12,4},... | collective-permute-start | bytes 4718600 | tf_op jit(solution)/shard_map/ppermute | solution.py:353
  70.2 2.8 %collective-permute-start.8 = (f32[8,2,3,16,128]{4,3,2,1,0:T(8,128)S(1)}, f32[8,2,3,16,128]{4,3,2,1,0:T(8,128)S(1)}, u32[]{:S(2)}, u32[]{:S(2)}) collective-permute-start(f32[8,2,3,16,128]{4,3,2,1,0:T(8,128)S(1)} %shard_map.66), channel_id=1, source_target_pairs={{0,8},{8,0},{1,9},{9,1},{2,10},{10,2},{3,11},{11,3},{4,12},{12,4},... | collective-permute-start | bytes 1179656 | tf_op jit(solution)/shard_map/ppermute | solution.py:364
  74.0 17.5 %collective-permute-start.9 = (s16[8,208,128]{2,1,0:T(8,128)(2,1)S(1)}, s16[8,208,128]{2,1,0:T(8,128)(2,1)S(1)}, u32[]{:S(2)}, u32[]{:S(2)}) collective-permute-start(s16[8,208,128]{2,1,0:T(8,128)(2,1)S(1)} %shard_map.67), channel_id=1, source_target_pairs={{0,128},{128,0},{1,129},{129,1},{2,130},{130,2},{3,131},{131,3},{4... | collective-permute-start | bytes 1277960 | tf_op jit(solution)/shard_map/ppermute | solution.py:370
  111.5 6.0 %collective-permute-start.12 = (f32[48,128]{1,0:T(8,128)S(1)}, f32[48,128]{1,0:T(8,128)S(1)}, u32[]{:S(2)}, u32[]{:S(2)}) collective-permute-start(f32[48,128]{1,0:T(8,128)S(1)} %get-tuple-element.19.own_ref), channel_id=1, source_target_pairs={{0,136},{8,128},{128,8},{136,0},{1,137},{9,129},{129,9},{137,1},{2... | collective-permute-start | bytes 73736 | tf_op jit(solution)/shard_map/ppermute | solution.py:383
  115.6 1.9 %collective-permute-start.11 = (f32[48,128]{1,0:T(8,128)S(1)}, f32[48,128]{1,0:T(8,128)S(1)}, u32[]{:S(2)}, u32[]{:S(2)}) collective-permute-start(f32[48,128]{1,0:T(8,128)S(1)} %get-tuple-element.19.own_ref), channel_id=1, source_target_pairs={{0,8},{8,0},{1,9},{9,1},{2,10},{10,2},{3,11},{11,3},{4,12},{12,4},... | collective-permute-start | bytes 73736 | tf_op jit(solution)/shard_map/ppermute | solution.py:384
  115.6 2.7 %collective-permute-start.10 = (f32[48,128]{1,0:T(8,128)S(1)}, f32[48,128]{1,0:T(8,128)S(1)}, u32[]{:S(2)}, u32[]{:S(2)}) collective-permute-start(f32[48,128]{1,0:T(8,128)S(1)} %get-tuple-element.19.own_ref), channel_id=1, source_target_pairs={{0,128},{128,0},{1,129},{129,1},{2,130},{130,2},{3,131},{131,3},{4... | collective-permute-start | bytes 73736 | tf_op jit(solution)/shard_map/ppermute | solution.py:382

commit v5 on v4

--- a/solution.py
+++ b/solution.py
@@ -46,15 +46,18 @@
     return jnp.exp2(jnp.transpose(jnp.broadcast_to(row, (LANES, LANES)))[:count])
 
 
-def spread_kernel(queries_ref, positives_ref, out_ref):
+def spread_kernel(queries_ref, positives_ref, out_ref, block_ref, sems):
     size, width = queries_ref.shape
     target = jnp.concatenate([positives_ref[...], jnp.zeros((1, LANES - size), i32)], axis=1)
     tail = jnp.concatenate([target // LANES, target % LANES, jnp.zeros((14, LANES), i32)], axis=0)
-    tail = tail.astype(f32).astype(bf16)
-    for c in range(out_ref.shape[0]):
-        for t in range(width // LANES):
-            out_ref[c, t * size : (t + 1) * size] = queries_ref[:, t * LANES : (t + 1) * LANES]
-        out_ref[c, width // LANES * size :] = tail
+    for t in range(width // LANES):
+        block_ref[t * size : (t + 1) * size] = queries_ref[:, t * LANES : (t + 1) * LANES]
+    block_ref[width // LANES * size :] = tail.astype(f32).astype(bf16)
+    sends = [pltpu.make_async_copy(block_ref, out_ref.at[c], sems.at[c]) for c in range(out_ref.shape[0])]
+    for send in sends:
+        send.start()
+    for send in sends:
+        send.wait()
 
 
 def share_kernel(place_ref, book_ref, share_ref):
@@ -182,8 +185,7 @@
         grads_ref[:, columns] = grad.astype(bf16)
 
 
-def codeword_kernel(mine, place_ref, grads_ref, codes_ref, out_ref):
-    core = place_ref[0] if mine else 1 - place_ref[0]
+def codeword_sums(core, grads_ref, codes_ref, out_ref):
     word = lax.broadcasted_iota(i32, (64, codes_ref.shape[1]), 0)
 
     def two(j, carry):
@@ -205,6 +207,10 @@
     lax.fori_loop(0, codes_ref.shape[0] // 4, two, 0, unroll=8)
 
 
+def codeword_kernel(place_ref, grads_ref, codes_ref, out_ref):
+    codeword_sums(1 - place_ref[0], grads_ref, codes_ref, out_ref)
+
+
 def put_query_words(chunk, out_ref, c):
     size, width = chunk.shape
     exponent = exponents(chunk)
@@ -220,7 +226,7 @@
     return jnp.concatenate([word.astype(i32).astype(f32) * scale for word in words], axis=1)
 
 
-def send_kernel(place_ref, sums_ref, cross_ref, out_ref):
+def send_kernel(place_ref, grads_ref, codes_ref, sums_ref, cross_ref, parts_ref, out_ref):
     peers = out_ref.shape[0]
     half, width = sums_ref.shape
     size = half // (2 * peers)
@@ -228,6 +234,7 @@
         rows = pl.ds(pl.multiple_of((1 - place_ref[4]) * (half // 2) + c * size, size), size)
         exponent = put_query_words(sums_ref[rows] + cross_ref[rows], out_ref, c)
         out_ref[c, width // LANES * size :] = exponent_rows(exponent)
+    codeword_sums(place_ref[0], grads_ref, codes_ref, parts_ref)
 
 
 def pack_kernel(place_ref, sums_ref, cross_ref, words_ref, parts_ref, out_ref):
@@ -249,17 +256,23 @@
         out_ref[c, base + totals.shape[0] :] = exponent_rows(jnp.concatenate([exponent, totals_exponent], axis=0))
 
 
-def unpack_kernel(words_ref, query_ref, sums_ref):
-    peers = words_ref.shape[0]
+def unpack_query_kernel(words_ref, query_ref):
+    peers, length, _ = words_ref.shape
     size, width = query_ref.shape
-    base = width // LANES * size
+    query = 0.0
+    for c in range(peers):
+        query = query + take_query_words(words_ref, c, scale_column(words_ref[c, length - 16 :], size), width)
+    query_ref[...] = query.astype(bf16)
+
+
+def unpack_sums_kernel(size, words_ref, sums_ref):
+    peers, length, _ = words_ref.shape
     count = sums_ref.shape[0]
-    query, sums = 0.0, 0.0
+    start = length - 16 - count
+    sums = 0.0
     for c in range(peers):
-        scale = scale_column(words_ref[c, base + count :], size + count)
-        query = query + take_query_words(words_ref, c, scale[:size], width)
-        sums = sums + words_ref[c, base : base + count].astype(i32).astype(f32) * scale[size:]
-    query_ref[...] = query.astype(bf16)
+        scale = scale_column(words_ref[c, length - 16 :], size + count)[size:]
+        sums = sums + words_ref[c, start : start + count].astype(i32).astype(f32) * scale
     sums_ref[...] = sums
 
 
@@ -277,6 +290,7 @@
 
 
 IN_VMEM = pl.BlockSpec(memory_space=pltpu.VMEM)
+ANYWHERE = pl.BlockSpec(memory_space=pl.ANY)
 IN_SMEM = pl.BlockSpec(memory_space=pltpu.SMEM)
 
 
@@ -313,7 +327,15 @@
     place = jnp.stack([axes[0], offset, *axes[1:]]).astype(i32)
     scalar = {0: IN_SMEM}
     length = width // LANES * size + 16
-    own = call(spread_kernel, shape((chips, length, LANES), bf16), (queries[0], positives), 10**6, vmem=60)
+    own = call(
+        spread_kernel,
+        shape((chips, length, LANES), bf16),
+        (queries[0], positives),
+        10**6,
+        scratch=[pltpu.VMEM((length, LANES), bf16), pltpu.SemaphoreType.DMA((chips,))],
+        out_special={0: ANYWHERE},
+        vmem=60,
+    )
     share = call(
         share_kernel,
         shape((codebook.shape[0] // 2, *codebook.shape[1:]), bf16),
@@ -352,20 +374,16 @@
     )
     query_cross = swap(query_other)
 
-    def codeword_sums(mine):
-        return call(
-            functools.partial(codeword_kernel, mine),
-            shape((8, 2, subspaces // 32, 16, LANES), f32),
-            (place, grads, own_codes),
-            10**6,
-            special=scalar,
-        )
-
-    sums_cross = swap(codeword_sums(False))
-    parts = codeword_sums(True) + sums_cross
-    words = call(
-        send_kernel, shape((chips // 2, length, LANES), i16), (place, query_own, query_cross), 10**6, special=scalar
-    )
+    sums_shape = shape((8, 2, subspaces // 32, 16, LANES), f32)
+    parts_cross = swap(call(codeword_kernel, sums_shape, (place, grads, own_codes), 10**6, special=scalar))
+    parts, words = call(
+        send_kernel,
+        [sums_shape, shape((chips // 2, length, LANES), i16)],
+        (place, grads, own_codes, query_own, query_cross),
+        10**6,
+        special=scalar,
+    )
+    parts = parts + parts_cross
     parts, words = lax.optimization_barrier((parts, words))
     words = swap_x(words)
     parts = lax.all_to_all(parts.reshape(16, subspaces // 32, 16, LANES), SUB + ("xl",), 0, 0)
@@ -378,10 +396,11 @@
         special=scalar,
     )
     words = lax.all_to_all(words, "z", 0, 0)
-    query_grad, sums = call(unpack_kernel, [shape((size, width), bf16), shape((count, LANES), f32)], (words,), 10**6)
+    sums = call(functools.partial(unpack_sums_kernel, size), shape((count, LANES), f32), (words,), 10**6)
     beside = swap_x(sums)
     corner = lax.ppermute(sums, ("xl", "core"), [(i, 3 - i) for i in range(4)])
     cross = swap(sums)
+    query_grad = call(unpack_query_kernel, shape((size, width), bf16), (words,), 10**6)
     codeword_grad = call(
         join_kernel,
         shape((subspaces // 8, 8, 2 * LANES), f32),

time: 120 us -> 119 us (level)
    ppermute x1, waiting for transfers between devices: 1.34 us -> 0.11 us  [per_device(): corner = lax.ppermute(sums, ('xl', 'core'), [(i, 3 - i) for i in range(4)])]
  transfers between devices with their start and end apart: 14 -> 14, of which waited for: 7 -> 8; matrix products, arithmetic and copies ran while one was open for 0% -> 0% of each run, Pallas kernels for 9% -> 10%
where the time goes in v5:
time: 119 us
  blocking collectives  52.6 us (44%)
  starting transfers between devices  30.3 us (25%)
  Pallas kernels  27.1 us (23%)
  waiting for transfers between devices  8.08 us (7%)
    pallas_call x12, Pallas kernels, call(): pl.pallas_call(kernel, out_shape=shapes, in_specs=specs, out_specs=outs i...  27.1 us
    all_to_all x1, blocking collectives, per_device(): words = lax.all_to_all(words, 'z', 0, 0)  17.8 us
    all_to_all x1, blocking collectives, per_device(): lax.all_to_all(parts.reshape(16, subspaces // 32, 16, LANES), SUB + ('xl'...  17.4 us
    all_to_all x1, blocking collectives, per_device(): stats = lax.all_to_all(stats, CHIP + ('core',), 0, 0, tiled=True)  17.4 us
    all_to_all x1, starting transfers between devices, per_device(): own = lax.all_to_all(own, CHIP, 0, 0)  10.1 us
    ppermute x1, starting transfers between devices, per_device(): corner = lax.ppermute(sums, ('xl', 'core'), [(i, 3 - i) for i in range(4)])  3.95 us
    ppermute x3, starting transfers between devices, per_device(): lax.ppermute(share, 'y', [(i, (i + k) % 4) for i in range(4)])  3.85 us
    ppermute x3, waiting for transfers between devices, per_device(): lax.ppermute(share, 'y', [(i, (i + k) % 4) for i in range(4)])  3.7 us
  transfers between devices with their start and end apart: 14, of which 8 were waited for; matrix products, arithmetic and copies ran while one was open for 0% of the time, Pallas kernels for 10%

profile of v5, /device:TPU:1, one launch (start us, length us, event | category | flops | bytes accessed | tf_op | source)
XLA Modules:
  0.0 118.9 jit_solution(16362541275822894594)
XLA Ops:
  0.6 0.0 copy-start.1
  0.6 0.0 copy-start
  0.7 1.9 %shard_map.59 = bf16[16,208,128]{2,1,0:T(8,128)(2,1)} custom-call(bf16[32,768]{1,0:T(8,128)(2,1)} %bitcast.18, s32[1,32]{1,0:T(1,128)} %positives_ref.1), custom_call_target="tpu_custom_call" | custom-call | flops 1000000 | bytes 65536 | tf_op jit(solution)/shard_map/pallas_call | solution.py:305
  2.6 10.1 %all-to-all-start = ((bf16[16,208,128]{2,1,0:T(8,128)(2,1)}), bf16[16,208,128]{2,1,0:T(8,128)(2,1)S(1)}, u32[]{:S(2)}, u32[]{:S(2)}) async-start(bf16[16,208,128]{2,1,0:T(8,128)(2,1)} %shard_map.59), calls=%async_computation | async-start | bytes 1703936 | tf_op jit(solution)/shard_map/all_to_all | solution.py:349
  12.7 0.1 stack.38.place_ref
  12.7 0.0 copy-done.1
  12.7 0.5 shard_map.60
  13.3 2.8 %collective-permute-start.2 = (bf16[6,8,256]{2,1,0:T(8,128)(2,1)S(1)}, bf16[6,8,256]{2,1,0:T(8,128)(2,1)S(1)}, u32[]{:S(2)}, u32[]{:S(2)}) collective-permute-start(bf16[6,8,256]{2,1,0:T(8,128)(2,1)S(1)} %shard_map.60), channel_id=1, source_target_pairs={{0,3},{1,0},{2,1},{3,2},{4,7},{5,4},{6,5},{7,6},{8,11},{9,8},{10,9... | collective-permute-start | bytes 73736 | tf_op jit(solution)/shard_map/ppermute | solution.py:346
  16.1 0.3 collective-permute-start.1
  16.5 0.7 collective-permute-start
  17.2 0.0 collective-permute-done.2
  17.2 3.2 %collective-permute-done.1 = bf16[6,8,256]{2,1,0:T(8,128)(2,1)S(1)} collective-permute-done((bf16[6,8,256]{2,1,0:T(8,128)(2,1)S(1)}, bf16[6,8,256]{2,1,0:T(8,128)(2,1)S(1)}, u32[]{:S(2)}, u32[]{:S(2)}) %collective-permute-start.1) | collective-permute-done | bytes 24608 | tf_op jit(solution)/shard_map/ppermute | solution.py:346
  20.3 0.5 collective-permute-done
  20.9 2.5 %collective-permute-start.4 = (bf16[4,6,8,256]{3,2,1,0:T(8,128)(2,1)S(1)}, bf16[4,6,8,256]{3,2,1,0:T(8,128)(2,1)S(1)}, u32[]{:S(2)}, u32[]{:S(2)}) collective-permute-start(bf16[4,6,8,256]{3,2,1,0:T(8,128)(2,1)S(1)} %pad_maximum_fusion.near_ref), channel_id=1, source_target_pairs={{0,4},{4,0},{1,5},{5,1},{2,6},{6,2},{3,7},{7,3},{8,12},{12,8},{9,1... | collective-permute-start | bytes 294920 | tf_op jit(solution)/shard_map/ppermute | solution.py:348
  23.4 2.4 %collective-permute-start.3 = (bf16[4,6,8,256]{3,2,1,0:T(8,128)(2,1)S(1)}, bf16[4,6,8,256]{3,2,1,0:T(8,128)(2,1)S(1)}, u32[]{:S(2)}, u32[]{:S(2)}) collective-permute-start(bf16[4,6,8,256]{3,2,1,0:T(8,128)(2,1)S(1)} %pad_maximum_fusion.near_ref), channel_id=1, source_target_pairs={{0,8},{8,0},{1,9},{9,1},{2,10},{10,2},{3,11},{11,3},{4,12},{12,4},... | collective-permute-start | bytes 294920 | tf_op jit(solution)/shard_map/ppermute | solution.py:353
  25.9 1.2 %collective-permute-done.4.far_ref = bf16[4,6,8,256]{3,2,1,0:T(8,128)(2,1)S(1)} collective-permute-done((bf16[4,6,8,256]{3,2,1,0:T(8,128)(2,1)S(1)}, bf16[4,6,8,256]{3,2,1,0:T(8,128)(2,1)S(1)}, u32[]{:S(2)}, u32[]{:S(2)}) %collective-permute-start.4) | collective-permute-done | bytes 98336 | tf_op jit(solution)/shard_map/ppermute | solution.py:348
  27.1 3.3 %collective-permute-start.5 = (bf16[4,6,8,256]{3,2,1,0:T(8,128)(2,1)S(1)}, bf16[4,6,8,256]{3,2,1,0:T(8,128)(2,1)S(1)}, u32[]{:S(2)}, u32[]{:S(2)}) collective-permute-start(bf16[4,6,8,256]{3,2,1,0:T(8,128)(2,1)S(1)} %collective-permute-done.4.far_ref), channel_id=1, source_target_pairs={{0,8},{8,0},{1,9},{9,1},{2,10},{10,2},{3,11},{11,3},{4,12},{12,4},... | collective-permute-start | bytes 294920 | tf_op jit(solution)/shard_map/ppermute | solution.py:353
  30.4 0.0 collective-permute-done.3.near_cross_ref
  30.4 0.9 collective-permute-done.5.far_cross_ref
  31.3 0.0 copy-done
  31.3 3.2 %shard_map.61.passages_ref = bf16[768,1024]{1,0:T(8,128)(2,1)S(1)} custom-call(s32[5]{0:T(128)S(1)} %stack.38.place_ref, s32[96,1024]{1,0:T(8,128)S(1)} %bitcast.13, bf16[4,6,8,256]{3,2,1,0:T(8,128)(2,1)S(1)} %pad_maximum_fusion.near_ref, bf16[4,6,8,256]{3,2,1,0:T(8,128)(2,1)S(1)} %collective-permute-done.3.near_cross_ref, ...), custom_call_target="tpu_custom_call" | custom-call | flops 1000000 | bytes 65536 | tf_op jit(solution)/shard_map/pallas_call | solution.py:305
  34.6 0.0 all-to-all-done.pack_ref.own_ref
  34.6 1.5 %collective-permute-start.6 = (bf16[16,208,128]{2,1,0:T(8,128)(2,1)S(1)}, bf16[16,208,128]{2,1,0:T(8,128)(2,1)S(1)}, u32[]{:S(2)}, u32[]{:S(2)}) collective-permute-start(bf16[16,208,128]{2,1,0:T(8,128)(2,1)S(1)} %all-to-all-done.pack_ref.own_ref), channel_id=1, source_target_pairs={{0,8},{8,0},{1,9},{9,1},{2,10},{10,2},{3,11},{11,3},{4,12},{12,4},... | collective-permute-start | bytes 2555912 | tf_op jit(solution)/shard_map/ppermute | solution.py:358
  36.1 1.3 %shard_map.62.own_logs_ref = f32[4,128]{1,0:T(4,128)S(1)} custom-call(bf16[16,208,128]{2,1,0:T(8,128)(2,1)S(1)} %all-to-all-done.pack_ref.own_ref, bf16[768,1024]{1,0:T(8,128)(2,1)S(1)} %shard_map.61.passages_ref), custom_call_target="tpu_custom_call" | custom-call | flops 1000000 | bytes 65536 | tf_op jit(solution)/shard_map/pallas_call | solution.py:305
  37.4 0.7 collective-permute-done.6.pack_ref.other_ref
  38.1 1.3 %shard_map.63 = f32[32,8,128]{2,1,0:T(8,128)S(1)} custom-call(bf16[16,208,128]{2,1,0:T(8,128)(2,1)S(1)} %collective-permute-done.6.pack_ref.other_ref, bf16[768,1024]{1,0:T(8,128)(2,1)S(1)} %shard_map.61.passages_ref, f32[4,128]{1,0:T(4,128)S(1)} %shard_map.62.own_logs_ref), custom_call_target="tpu_custom_call" | custom-call | flops 1000000 | bytes 65536 | tf_op jit(solution)/shard_map/pallas_call | solution.py:305
  39.4 17.4 %all_to_all.20.stats_ref = f32[32,8,128]{2,1,0:T(8,128)S(1)} all-to-all(f32[32,8,128]{2,1,0:T(8,128)S(1)} %shard_map.63), channel_id=1, replica_groups=mesh['xl'=2,'z'=8,'core'=2,'xh'=2,'y'=4] {'xl','z','core'}, dimensions={0} | all-to-all | bytes 262144 | tf_op jit(solution)/shard_map/all_to_all | solution.py:361
  56.8 9.0 %shard_map.64 = (f32[512,768]{1,0:T(8,128)S(1)}, f32[512,768]{1,0:T(8,128)S(1)}, bf16[768,1024]{1,0:T(8,128)(2,1)S(1)}) custom-call(s32[5]{0:T(128)S(1)} %stack.38.place_ref, f32[32,8,128]{2,1,0:T(8,128)S(1)} %all_to_all.20.stats_ref, bf16[16,208,128]{2,1,0:T(8,128)(2,1)S(1)} %all-to-all-done.pack_ref.own_ref, ...), custom_call_target="tpu_custom_call" | custom-call | flops 1000000 | bytes 65536 | tf_op jit(solution)/shard_map/pallas_call | solution.py:305
  65.8 1.7 %collective-permute-start.7 = (f32[512,768]{1,0:T(8,128)S(1)}, f32[512,768]{1,0:T(8,128)S(1)}, u32[]{:S(2)}, u32[]{:S(2)}) collective-permute-start(f32[512,768]{1,0:T(8,128)S(1)} %get-tuple-element.14), channel_id=1, source_target_pairs={{0,8},{8,0},{1,9},{9,1},{2,10},{10,2},{3,11},{11,3},{4,12},{12,4},... | collective-permute-start | bytes 4718600 | tf_op jit(solution)/shard_map/ppermute | solution.py:375
  67.5 2.8 %shard_map.66 = f32[8,2,3,16,128]{4,3,2,1,0:T(8,128)S(1)} custom-call(s32[5]{0:T(128)S(1)} %stack.38.place_ref, bf16[768,1024]{1,0:T(8,128)(2,1)S(1)} %get-tuple-element.15.grads_ref, s32[96,1024]{1,0:T(8,128)S(1)} %bitcast.14), custom_call_target="tpu_custom_call" | custom-call | flops 1000000 | bytes 65536 | tf_op jit(solution)/shard_map/pallas_call | solution.py:305
  70.3 0.1 collective-permute-start.8
  70.3 0.2 collective-permute-done.7.cross_ref
  70.5 3.2 %shard_map.65 = (f32[8,2,3,16,128]{4,3,2,1,0:T(8,128)S(1)}, s16[8,208,128]{2,1,0:T(8,128)(2,1)S(1)}) custom-call(s32[5]{0:T(128)S(1)} %stack.38.place_ref, bf16[768,1024]{1,0:T(8,128)(2,1)S(1)} %get-tuple-element.15.grads_ref, s32[96,1024]{1,0:T(8,128)S(1)} %bitcast.15, f32[512,768]{1,0:T(8,128)S(1)} %get-tuple-element.13.sums_ref, ...), custom_call_target="tpu_custom_call" | custom-call | flops 1000000 | bytes 65536 | tf_op jit(solution)/shard_map/pallas_call | solution.py:305
  73.7 0.0 collective-permute-done.8
  73.7 0.1 add.11
  73.8 0.3 collective-permute-start.9
  74.1 17.4 %all_to_all.21.parts_ref = f32[16,3,16,128]{3,2,1,0:T(8,128)S(1)} all-to-all(f32[16,3,16,128]{3,2,1,0:T(8,128)S(1)} %bitcast.17), channel_id=1, replica_groups=mesh['xl'=2,'z'=8,'core'=2,'xh'=2,'y'=4] {'xh','y','xl'}, dimensions={0} | all-to-all | bytes 786432 | tf_op jit(solution)/shard_map/all_to_all | solution.py:389
  91.5 0.0 collective-permute-done.9.words_ref
  91.5 1.6 %shard_map.67 = s16[8,256,128]{2,1,0:T(8,128)(2,1)S(1)} custom-call(s32[5]{0:T(128)S(1)} %stack.38.place_ref, f32[512,768]{1,0:T(8,128)S(1)} %get-tuple-element.13.sums_ref, f32[512,768]{1,0:T(8,128)S(1)} %collective-permute-done.7.cross_ref, s16[8,208,128]{2,1,0:T(8,128)(2,1)S(1)} %collective-permute-done.9.words_ref, ...), custom_call_target="tpu_custom_call" | custom-call | flops 1000000 | bytes 65536 | tf_op jit(solution)/shard_map/pallas_call | solution.py:305
  93.0 17.8 %all_to_all.22.words_ref = s16[8,256,128]{2,1,0:T(8,128)(2,1)S(1)} all-to-all(s16[8,256,128]{2,1,0:T(8,128)(2,1)S(1)} %shard_map.67), channel_id=1, replica_groups=mesh['xl'=2,'z'=8,'core'=2,'xh'=2,'y'=4] {'z'}, dimensions={0} | all-to-all | bytes 1048576 | tf_op jit(solution)/shard_map/all_to_all | solution.py:398
  110.8 0.2 shard_map.69.own_ref
  111.0 4.0 %collective-permute-start.12 = (f32[48,128]{1,0:T(8,128)S(1)}, f32[48,128]{1,0:T(8,128)S(1)}, u32[]{:S(2)}, u32[]{:S(2)}) collective-permute-start(f32[48,128]{1,0:T(8,128)S(1)} %shard_map.69.own_ref), channel_id=1, source_target_pairs={{0,136},{8,128},{128,8},{136,0},{1,137},{9,129},{129,9},{137,1},{2... | collective-permute-start | bytes 73736 | tf_op jit(solution)/shard_map/ppermute | solution.py:401
  115.0 0.0 collective-permute-start.11
  115.0 0.6 collective-permute-start.10
  115.5 0.8 shard_map.68
  116.4 0.1 collective-permute-done.12.corner_ref
  116.5 0.0 collective-permute-done.11.cross_ref
  116.5 1.2 collective-permute-done.10.beside_ref
  117.6 1.3 %shard_map.70 = f32[12,8,256]{2,1,0:T(8,128)} custom-call(s32[5]{0:T(128)S(1)} %stack.38.place_ref, f32[48,128]{1,0:T(8,128)S(1)} %shard_map.69.own_ref, f32[48,128]{1,0:T(8,128)S(1)} %collective-permute-done.10.beside_ref, f32[48,128]{1,0:T(8,128)S(1)} %collective-permute-done.11.cross_ref, f32[48,128]{1,0:T(8,128)S(1)} %collective-permute-done.12.corner_ref), custom_call_target="tpu_custom_call" | custom-call | flops 1000000 | bytes 65536 | tf_op jit(solution)/shard_map/pallas_call | solution.py:305
  (1 shorter events, 0.0 us)
Async XLA Ops:
  0.6 12.1 %copy-start.1 = (bf16[12,8,256]{2,1,0:T(8,128)(2,1)S(1)}, bf16[12,8,256]{2,1,0:T(8,128)(2,1)}, u32[]{:S(2)}) copy-start(bf16[12,8,256]{2,1,0:T(8,128)(2,1)} %book_ref.1) | copy-start | bytes 147460
  0.6 30.7 %copy-start = (s32[1,96,1024]{2,1,0:T(8,128)S(1)}, s32[1,96,1024]{2,1,0:T(8,128)}, u32[]{:S(2)}) copy-start(s32[1,96,1024]{2,1,0:T(8,128)} %param.5) | copy-start | bytes 1179652
  2.6 32.0 %all-to-all-start = ((bf16[16,208,128]{2,1,0:T(8,128)(2,1)}), bf16[16,208,128]{2,1,0:T(8,128)(2,1)S(1)}, u32[]{:S(2)}, u32[]{:S(2)}) async-start(bf16[16,208,128]{2,1,0:T(8,128)(2,1)} %shard_map.59), calls=%async_computation | async-start | bytes 1703936 | tf_op jit(solution)/shard_map/all_to_all | solution.py:349
  13.3 3.9 %collective-permute-start.2 = (bf16[6,8,256]{2,1,0:T(8,128)(2,1)S(1)}, bf16[6,8,256]{2,1,0:T(8,128)(2,1)S(1)}, u32[]{:S(2)}, u32[]{:S(2)}) collective-permute-start(bf16[6,8,256]{2,1,0:T(8,128)(2,1)S(1)} %shard_map.60), channel_id=1, source_target_pairs={{0,3},{1,0},{2,1},{3,2},{4,7},{5,4},{6,5},{7,6},{8,11},{9,8},{10,9... | collective-permute-start | bytes 73736 | tf_op jit(solution)/shard_map/ppermute | solution.py:346
  16.1 4.2 %collective-permute-start.1 = (bf16[6,8,256]{2,1,0:T(8,128)(2,1)S(1)}, bf16[6,8,256]{2,1,0:T(8,128)(2,1)S(1)}, u32[]{:S(2)}, u32[]{:S(2)}) collective-permute-start(bf16[6,8,256]{2,1,0:T(8,128)(2,1)S(1)} %shard_map.60), channel_id=1, source_target_pairs={{0,2},{1,3},{2,0},{3,1},{4,6},{5,7},{6,4},{7,5},{8,10},{9,11},{10,... | collective-permute-start | bytes 73736 | tf_op jit(solution)/shard_map/ppermute | solution.py:346
  16.5 4.4 %collective-permute-start = (bf16[6,8,256]{2,1,0:T(8,128)(2,1)S(1)}, bf16[6,8,256]{2,1,0:T(8,128)(2,1)S(1)}, u32[]{:S(2)}, u32[]{:S(2)}) collective-permute-start(bf16[6,8,256]{2,1,0:T(8,128)(2,1)S(1)} %shard_map.60), channel_id=1, source_target_pairs={{0,1},{1,2},{2,3},{3,0},{4,5},{5,6},{6,7},{7,4},{8,9},{9,10},{10,1... | collective-permute-start | bytes 73736 | tf_op jit(solution)/shard_map/ppermute | solution.py:346
  20.9 6.2 %collective-permute-start.4 = (bf16[4,6,8,256]{3,2,1,0:T(8,128)(2,1)S(1)}, bf16[4,6,8,256]{3,2,1,0:T(8,128)(2,1)S(1)}, u32[]{:S(2)}, u32[]{:S(2)}) collective-permute-start(bf16[4,6,8,256]{3,2,1,0:T(8,128)(2,1)S(1)} %pad_maximum_fusion.near_ref), channel_id=1, source_target_pairs={{0,4},{4,0},{1,5},{5,1},{2,6},{6,2},{3,7},{7,3},{8,12},{12,8},{9,1... | collective-permute-start | bytes 294920 | tf_op jit(solution)/shard_map/ppermute | solution.py:348
  23.4 7.0 %collective-permute-start.3 = (bf16[4,6,8,256]{3,2,1,0:T(8,128)(2,1)S(1)}, bf16[4,6,8,256]{3,2,1,0:T(8,128)(2,1)S(1)}, u32[]{:S(2)}, u32[]{:S(2)}) collective-permute-start(bf16[4,6,8,256]{3,2,1,0:T(8,128)(2,1)S(1)} %pad_maximum_fusion.near_ref), channel_id=1, source_target_pairs={{0,8},{8,0},{1,9},{9,1},{2,10},{10,2},{3,11},{11,3},{4,12},{12,4},... | collective-permute-start | bytes 294920 | tf_op jit(solution)/shard_map/ppermute | solution.py:353
  27.1 4.2 %collective-permute-start.5 = (bf16[4,6,8,256]{3,2,1,0:T(8,128)(2,1)S(1)}, bf16[4,6,8,256]{3,2,1,0:T(8,128)(2,1)S(1)}, u32[]{:S(2)}, u32[]{:S(2)}) collective-permute-start(bf16[4,6,8,256]{3,2,1,0:T(8,128)(2,1)S(1)} %collective-permute-done.4.far_ref), channel_id=1, source_target_pairs={{0,8},{8,0},{1,9},{9,1},{2,10},{10,2},{3,11},{11,3},{4,12},{12,4},... | collective-permute-start | bytes 294920 | tf_op jit(solution)/shard_map/ppermute | solution.py:353
  34.6 3.5 %collective-permute-start.6 = (bf16[16,208,128]{2,1,0:T(8,128)(2,1)S(1)}, bf16[16,208,128]{2,1,0:T(8,128)(2,1)S(1)}, u32[]{:S(2)}, u32[]{:S(2)}) collective-permute-start(bf16[16,208,128]{2,1,0:T(8,128)(2,1)S(1)} %all-to-all-done.pack_ref.own_ref), channel_id=1, source_target_pairs={{0,8},{8,0},{1,9},{9,1},{2,10},{10,2},{3,11},{11,3},{4,12},{12,4},... | collective-permute-start | bytes 2555912 | tf_op jit(solution)/shard_map/ppermute | solution.py:358
  65.8 4.8 %collective-permute-start.7 = (f32[512,768]{1,0:T(8,128)S(1)}, f32[512,768]{1,0:T(8,128)S(1)}, u32[]{:S(2)}, u32[]{:S(2)}) collective-permute-start(f32[512,768]{1,0:T(8,128)S(1)} %get-tuple-element.14), channel_id=1, source_target_pairs={{0,8},{8,0},{1,9},{9,1},{2,10},{10,2},{3,11},{11,3},{4,12},{12,4},... | collective-permute-start | bytes 4718600 | tf_op jit(solution)/shard_map/ppermute | solution.py:375
  70.3 3.4 %collective-permute-start.8 = (f32[8,2,3,16,128]{4,3,2,1,0:T(8,128)S(1)}, f32[8,2,3,16,128]{4,3,2,1,0:T(8,128)S(1)}, u32[]{:S(2)}, u32[]{:S(2)}) collective-permute-start(f32[8,2,3,16,128]{4,3,2,1,0:T(8,128)S(1)} %shard_map.66), channel_id=1, source_target_pairs={{0,8},{8,0},{1,9},{9,1},{2,10},{10,2},{3,11},{11,3},{4,12},{12,4},... | collective-permute-start | bytes 1179656 | tf_op jit(solution)/shard_map/ppermute | solution.py:378
  73.8 17.7 %collective-permute-start.9 = (s16[8,208,128]{2,1,0:T(8,128)(2,1)S(1)}, s16[8,208,128]{2,1,0:T(8,128)(2,1)S(1)}, u32[]{:S(2)}, u32[]{:S(2)}) collective-permute-start(s16[8,208,128]{2,1,0:T(8,128)(2,1)S(1)} %get-tuple-element.18), channel_id=1, source_target_pairs={{0,128},{128,0},{1,129},{129,1},{2,130},{130,2},{3,131},{131,3},{4... | collective-permute-start | bytes 1277960 | tf_op jit(solution)/shard_map/ppermute | solution.py:388
  111.0 5.5 %collective-permute-start.12 = (f32[48,128]{1,0:T(8,128)S(1)}, f32[48,128]{1,0:T(8,128)S(1)}, u32[]{:S(2)}, u32[]{:S(2)}) collective-permute-start(f32[48,128]{1,0:T(8,128)S(1)} %shard_map.69.own_ref), channel_id=1, source_target_pairs={{0,136},{8,128},{128,8},{136,0},{1,137},{9,129},{129,9},{137,1},{2... | collective-permute-start | bytes 73736 | tf_op jit(solution)/shard_map/ppermute | solution.py:401
  115.0 1.5 %collective-permute-start.11 = (f32[48,128]{1,0:T(8,128)S(1)}, f32[48,128]{1,0:T(8,128)S(1)}, u32[]{:S(2)}, u32[]{:S(2)}) collective-permute-start(f32[48,128]{1,0:T(8,128)S(1)} %shard_map.69.own_ref), channel_id=1, source_target_pairs={{0,8},{8,0},{1,9},{9,1},{2,10},{10,2},{3,11},{11,3},{4,12},{12,4},... | collective-permute-start | bytes 73736 | tf_op jit(solution)/shard_map/ppermute | solution.py:402
  115.0 2.7 %collective-permute-start.10 = (f32[48,128]{1,0:T(8,128)S(1)}, f32[48,128]{1,0:T(8,128)S(1)}, u32[]{:S(2)}, u32[]{:S(2)}) collective-permute-start(f32[48,128]{1,0:T(8,128)S(1)} %shard_map.69.own_ref), channel_id=1, source_target_pairs={{0,128},{128,0},{1,129},{129,1},{2,130},{130,2},{3,131},{131,3},{4... | collective-permute-start | bytes 73736 | tf_op jit(solution)/shard_map/ppermute | solution.py:400

commit v6 on v5

--- a/solution.py
+++ b/solution.py
@@ -204,7 +204,7 @@
             out_ref[j // 3, k, j % 3] = sums[16 * k : 16 * k + 16]
         return carry
 
-    lax.fori_loop(0, codes_ref.shape[0] // 4, two, 0, unroll=8)
+    lax.fori_loop(0, codes_ref.shape[0] // 4, two, 0, unroll=24)
 
 
 def codeword_kernel(place_ref, grads_ref, codes_ref, out_ref):

time: 119 us -> 119 us (level)
  transfers between devices with their start and end apart: 14 -> 14, of which waited for: 8 -> 8; matrix products, arithmetic and copies ran while one was open for 0% -> 0% of each run, Pallas kernels for 10% -> 9%
where the time goes in v6:
time: 119 us
  blocking collectives  52.5 us (44%)
  starting transfers between devices  30.5 us (26%)
  Pallas kernels  26.2 us (22%)
  waiting for transfers between devices  8.47 us (7%)
    pallas_call x12, Pallas kernels, call(): pl.pallas_call(kernel, out_shape=shapes, in_specs=specs, out_specs=outs i...  26.2 us
    all_to_all x1, blocking collectives, per_device(): words = lax.all_to_all(words, 'z', 0, 0)  17.8 us
    all_to_all x1, blocking collectives, per_device(): lax.all_to_all(parts.reshape(16, subspaces // 32, 16, LANES), SUB + ('xl'...  17.4 us
    all_to_all x1, blocking collectives, per_device(): stats = lax.all_to_all(stats, CHIP + ('core',), 0, 0, tiled=True)  17.4 us
    all_to_all x1, starting transfers between devices, per_device(): own = lax.all_to_all(own, CHIP, 0, 0)  10.1 us
    ppermute x1, starting transfers between devices, per_device(): corner = lax.ppermute(sums, ('xl', 'core'), [(i, 3 - i) for i in range(4)])  3.96 us
    ppermute x3, starting transfers between devices, per_device(): lax.ppermute(share, 'y', [(i, (i + k) % 4) for i in range(4)])  3.85 us
    ppermute x3, waiting for transfers between devices, per_device(): lax.ppermute(share, 'y', [(i, (i + k) % 4) for i in range(4)])  3.7 us
  transfers between devices with their start and end apart: 14, of which 8 were waited for; matrix products, arithmetic and copies ran while one was open for 0% of the time, Pallas kernels for 9%

profile of v6, /device:TPU:1, one launch (start us, length us, event | category | flops | bytes accessed | tf_op | source)
XLA Modules:
  0.0 118.6 jit_solution(7046346323203876221)
XLA Ops:
  0.6 0.0 copy-start.1
  0.6 0.0 copy-start
  0.7 1.9 %shard_map.59 = bf16[16,208,128]{2,1,0:T(8,128)(2,1)} custom-call(bf16[32,768]{1,0:T(8,128)(2,1)} %bitcast.18, s32[1,32]{1,0:T(1,128)} %positives_ref.1), custom_call_target="tpu_custom_call" | custom-call | flops 1000000 | bytes 65536 | tf_op jit(solution)/shard_map/pallas_call | solution.py:305
  2.6 10.1 %all-to-all-start = ((bf16[16,208,128]{2,1,0:T(8,128)(2,1)}), bf16[16,208,128]{2,1,0:T(8,128)(2,1)S(1)}, u32[]{:S(2)}, u32[]{:S(2)}) async-start(bf16[16,208,128]{2,1,0:T(8,128)(2,1)} %shard_map.59), calls=%async_computation | async-start | bytes 1703936 | tf_op jit(solution)/shard_map/all_to_all | solution.py:349
  12.7 0.1 stack.38.place_ref
  12.7 0.0 copy-done.1
  12.7 0.5 shard_map.60
  13.3 2.8 %collective-permute-start.2 = (bf16[6,8,256]{2,1,0:T(8,128)(2,1)S(1)}, bf16[6,8,256]{2,1,0:T(8,128)(2,1)S(1)}, u32[]{:S(2)}, u32[]{:S(2)}) collective-permute-start(bf16[6,8,256]{2,1,0:T(8,128)(2,1)S(1)} %shard_map.60), channel_id=1, source_target_pairs={{0,3},{1,0},{2,1},{3,2},{4,7},{5,4},{6,5},{7,6},{8,11},{9,8},{10,9... | collective-permute-start | bytes 73736 | tf_op jit(solution)/shard_map/ppermute | solution.py:346
  16.1 0.3 collective-permute-start.1
  16.5 0.7 collective-permute-start
  17.2 0.0 collective-permute-done.2
  17.2 3.2 %collective-permute-done.1 = bf16[6,8,256]{2,1,0:T(8,128)(2,1)S(1)} collective-permute-done((bf16[6,8,256]{2,1,0:T(8,128)(2,1)S(1)}, bf16[6,8,256]{2,1,0:T(8,128)(2,1)S(1)}, u32[]{:S(2)}, u32[]{:S(2)}) %collective-permute-start.1) | collective-permute-done | bytes 24608 | tf_op jit(solution)/shard_map/ppermute | solution.py:346
  20.3 0.5 collective-permute-done
  20.9 2.5 %collective-permute-start.4 = (bf16[4,6,8,256]{3,2,1,0:T(8,128)(2,1)S(1)}, bf16[4,6,8,256]{3,2,1,0:T(8,128)(2,1)S(1)}, u32[]{:S(2)}, u32[]{:S(2)}) collective-permute-start(bf16[4,6,8,256]{3,2,1,0:T(8,128)(2,1)S(1)} %pad_maximum_fusion.near_ref), channel_id=1, source_target_pairs={{0,4},{4,0},{1,5},{5,1},{2,6},{6,2},{3,7},{7,3},{8,12},{12,8},{9,1... | collective-permute-start | bytes 294920 | tf_op jit(solution)/shard_map/ppermute | solution.py:348
  23.4 2.4 %collective-permute-start.3 = (bf16[4,6,8,256]{3,2,1,0:T(8,128)(2,1)S(1)}, bf16[4,6,8,256]{3,2,1,0:T(8,128)(2,1)S(1)}, u32[]{:S(2)}, u32[]{:S(2)}) collective-permute-start(bf16[4,6,8,256]{3,2,1,0:T(8,128)(2,1)S(1)} %pad_maximum_fusion.near_ref), channel_id=1, source_target_pairs={{0,8},{8,0},{1,9},{9,1},{2,10},{10,2},{3,11},{11,3},{4,12},{12,4},... | collective-permute-start | bytes 294920 | tf_op jit(solution)/shard_map/ppermute | solution.py:353
  25.9 1.2 %collective-permute-done.4.far_ref = bf16[4,6,8,256]{3,2,1,0:T(8,128)(2,1)S(1)} collective-permute-done((bf16[4,6,8,256]{3,2,1,0:T(8,128)(2,1)S(1)}, bf16[4,6,8,256]{3,2,1,0:T(8,128)(2,1)S(1)}, u32[]{:S(2)}, u32[]{:S(2)}) %collective-permute-start.4) | collective-permute-done | bytes 98336 | tf_op jit(solution)/shard_map/ppermute | solution.py:348
  27.1 3.3 %collective-permute-start.5 = (bf16[4,6,8,256]{3,2,1,0:T(8,128)(2,1)S(1)}, bf16[4,6,8,256]{3,2,1,0:T(8,128)(2,1)S(1)}, u32[]{:S(2)}, u32[]{:S(2)}) collective-permute-start(bf16[4,6,8,256]{3,2,1,0:T(8,128)(2,1)S(1)} %collective-permute-done.4.far_ref), channel_id=1, source_target_pairs={{0,8},{8,0},{1,9},{9,1},{2,10},{10,2},{3,11},{11,3},{4,12},{12,4},... | collective-permute-start | bytes 294920 | tf_op jit(solution)/shard_map/ppermute | solution.py:353
  30.4 0.0 collective-permute-done.3.near_cross_ref
  30.4 0.9 collective-permute-done.5.far_cross_ref
  31.3 0.0 copy-done
  31.3 3.2 %shard_map.61.passages_ref = bf16[768,1024]{1,0:T(8,128)(2,1)S(1)} custom-call(s32[5]{0:T(128)S(1)} %stack.38.place_ref, s32[96,1024]{1,0:T(8,128)S(1)} %bitcast.13, bf16[4,6,8,256]{3,2,1,0:T(8,128)(2,1)S(1)} %pad_maximum_fusion.near_ref, bf16[4,6,8,256]{3,2,1,0:T(8,128)(2,1)S(1)} %collective-permute-done.3.near_cross_ref, ...), custom_call_target="tpu_custom_call" | custom-call | flops 1000000 | bytes 65536 | tf_op jit(solution)/shard_map/pallas_call | solution.py:305
  34.6 0.0 all-to-all-done.pack_ref.own_ref
  34.6 1.5 %collective-permute-start.6 = (bf16[16,208,128]{2,1,0:T(8,128)(2,1)S(1)}, bf16[16,208,128]{2,1,0:T(8,128)(2,1)S(1)}, u32[]{:S(2)}, u32[]{:S(2)}) collective-permute-start(bf16[16,208,128]{2,1,0:T(8,128)(2,1)S(1)} %all-to-all-done.pack_ref.own_ref), channel_id=1, source_target_pairs={{0,8},{8,0},{1,9},{9,1},{2,10},{10,2},{3,11},{11,3},{4,12},{12,4},... | collective-permute-start | bytes 2555912 | tf_op jit(solution)/shard_map/ppermute | solution.py:358
  36.1 1.3 %shard_map.62.own_logs_ref = f32[4,128]{1,0:T(4,128)S(1)} custom-call(bf16[16,208,128]{2,1,0:T(8,128)(2,1)S(1)} %all-to-all-done.pack_ref.own_ref, bf16[768,1024]{1,0:T(8,128)(2,1)S(1)} %shard_map.61.passages_ref), custom_call_target="tpu_custom_call" | custom-call | flops 1000000 | bytes 65536 | tf_op jit(solution)/shard_map/pallas_call | solution.py:305
  37.4 0.7 collective-permute-done.6.pack_ref.other_ref
  38.1 1.3 %shard_map.63 = f32[32,8,128]{2,1,0:T(8,128)S(1)} custom-call(bf16[16,208,128]{2,1,0:T(8,128)(2,1)S(1)} %collective-permute-done.6.pack_ref.other_ref, bf16[768,1024]{1,0:T(8,128)(2,1)S(1)} %shard_map.61.passages_ref, f32[4,128]{1,0:T(4,128)S(1)} %shard_map.62.own_logs_ref), custom_call_target="tpu_custom_call" | custom-call | flops 1000000 | bytes 65536 | tf_op jit(solution)/shard_map/pallas_call | solution.py:305
  39.4 17.4 %all_to_all.20.stats_ref = f32[32,8,128]{2,1,0:T(8,128)S(1)} all-to-all(f32[32,8,128]{2,1,0:T(8,128)S(1)} %shard_map.63), channel_id=1, replica_groups=mesh['xl'=2,'z'=8,'core'=2,'xh'=2,'y'=4] {'xl','z','core'}, dimensions={0} | all-to-all | bytes 262144 | tf_op jit(solution)/shard_map/all_to_all | solution.py:361
  56.8 9.0 %shard_map.64 = (f32[512,768]{1,0:T(8,128)S(1)}, f32[512,768]{1,0:T(8,128)S(1)}, bf16[768,1024]{1,0:T(8,128)(2,1)S(1)}) custom-call(s32[5]{0:T(128)S(1)} %stack.38.place_ref, f32[32,8,128]{2,1,0:T(8,128)S(1)} %all_to_all.20.stats_ref, bf16[16,208,128]{2,1,0:T(8,128)(2,1)S(1)} %all-to-all-done.pack_ref.own_ref, ...), custom_call_target="tpu_custom_call" | custom-call | flops 1000000 | bytes 65536 | tf_op jit(solution)/shard_map/pallas_call | solution.py:305
  65.8 1.7 %collective-permute-start.7 = (f32[512,768]{1,0:T(8,128)S(1)}, f32[512,768]{1,0:T(8,128)S(1)}, u32[]{:S(2)}, u32[]{:S(2)}) collective-permute-start(f32[512,768]{1,0:T(8,128)S(1)} %get-tuple-element.14), channel_id=1, source_target_pairs={{0,8},{8,0},{1,9},{9,1},{2,10},{10,2},{3,11},{11,3},{4,12},{12,4},... | collective-permute-start | bytes 4718600 | tf_op jit(solution)/shard_map/ppermute | solution.py:375
  67.5 2.4 %shard_map.66 = f32[8,2,3,16,128]{4,3,2,1,0:T(8,128)S(1)} custom-call(s32[5]{0:T(128)S(1)} %stack.38.place_ref, bf16[768,1024]{1,0:T(8,128)(2,1)S(1)} %get-tuple-element.15.grads_ref, s32[96,1024]{1,0:T(8,128)S(1)} %bitcast.14), custom_call_target="tpu_custom_call" | custom-call | flops 1000000 | bytes 65536 | tf_op jit(solution)/shard_map/pallas_call | solution.py:305
  69.9 0.1 collective-permute-start.8
  70.0 0.6 collective-permute-done.7.cross_ref
  70.5 2.7 %shard_map.65 = (f32[8,2,3,16,128]{4,3,2,1,0:T(8,128)S(1)}, s16[8,208,128]{2,1,0:T(8,128)(2,1)S(1)}) custom-call(s32[5]{0:T(128)S(1)} %stack.38.place_ref, bf16[768,1024]{1,0:T(8,128)(2,1)S(1)} %get-tuple-element.15.grads_ref, s32[96,1024]{1,0:T(8,128)S(1)} %bitcast.15, f32[512,768]{1,0:T(8,128)S(1)} %get-tuple-element.13.sums_ref, ...), custom_call_target="tpu_custom_call" | custom-call | flops 1000000 | bytes 65536 | tf_op jit(solution)/shard_map/pallas_call | solution.py:305
  73.2 0.0 collective-permute-done.8
  73.2 0.1 add.11
  73.3 0.5 collective-permute-start.9
  73.8 17.4 %all_to_all.21.parts_ref = f32[16,3,16,128]{3,2,1,0:T(8,128)S(1)} all-to-all(f32[16,3,16,128]{3,2,1,0:T(8,128)S(1)} %bitcast.17), channel_id=1, replica_groups=mesh['xl'=2,'z'=8,'core'=2,'xh'=2,'y'=4] {'xh','y','xl'}, dimensions={0} | all-to-all | bytes 786432 | tf_op jit(solution)/shard_map/all_to_all | solution.py:389
  91.2 0.0 collective-permute-done.9.words_ref
  91.2 1.6 %shard_map.67 = s16[8,256,128]{2,1,0:T(8,128)(2,1)S(1)} custom-call(s32[5]{0:T(128)S(1)} %stack.38.place_ref, f32[512,768]{1,0:T(8,128)S(1)} %get-tuple-element.13.sums_ref, f32[512,768]{1,0:T(8,128)S(1)} %collective-permute-done.7.cross_ref, s16[8,208,128]{2,1,0:T(8,128)(2,1)S(1)} %collective-permute-done.9.words_ref, ...), custom_call_target="tpu_custom_call" | custom-call | flops 1000000 | bytes 65536 | tf_op jit(solution)/shard_map/pallas_call | solution.py:305
  92.7 17.8 %all_to_all.22.words_ref = s16[8,256,128]{2,1,0:T(8,128)(2,1)S(1)} all-to-all(s16[8,256,128]{2,1,0:T(8,128)(2,1)S(1)} %shard_map.67), channel_id=1, replica_groups=mesh['xl'=2,'z'=8,'core'=2,'xh'=2,'y'=4] {'z'}, dimensions={0} | all-to-all | bytes 1048576 | tf_op jit(solution)/shard_map/all_to_all | solution.py:398
  110.5 0.2 shard_map.69.own_ref
  110.7 4.0 %collective-permute-start.12 = (f32[48,128]{1,0:T(8,128)S(1)}, f32[48,128]{1,0:T(8,128)S(1)}, u32[]{:S(2)}, u32[]{:S(2)}) collective-permute-start(f32[48,128]{1,0:T(8,128)S(1)} %shard_map.69.own_ref), channel_id=1, source_target_pairs={{0,136},{8,128},{128,8},{136,0},{1,137},{9,129},{129,9},{137,1},{2... | collective-permute-start | bytes 73736 | tf_op jit(solution)/shard_map/ppermute | solution.py:401
  114.7 0.0 collective-permute-start.11
  114.7 0.6 collective-permute-start.10
  115.2 0.8 shard_map.68
  116.1 0.1 collective-permute-done.12.corner_ref
  116.2 0.0 collective-permute-done.11.cross_ref
  116.2 1.2 collective-permute-done.10.beside_ref
  117.4 1.3 %shard_map.70 = f32[12,8,256]{2,1,0:T(8,128)} custom-call(s32[5]{0:T(128)S(1)} %stack.38.place_ref, f32[48,128]{1,0:T(8,128)S(1)} %shard_map.69.own_ref, f32[48,128]{1,0:T(8,128)S(1)} %collective-permute-done.10.beside_ref, f32[48,128]{1,0:T(8,128)S(1)} %collective-permute-done.11.cross_ref, f32[48,128]{1,0:T(8,128)S(1)} %collective-permute-done.12.corner_ref), custom_call_target="tpu_custom_call" | custom-call | flops 1000000 | bytes 65536 | tf_op jit(solution)/shard_map/pallas_call | solution.py:305
  (1 shorter events, 0.0 us)
Async XLA Ops:
  0.6 12.1 %copy-start.1 = (bf16[12,8,256]{2,1,0:T(8,128)(2,1)S(1)}, bf16[12,8,256]{2,1,0:T(8,128)(2,1)}, u32[]{:S(2)}) copy-start(bf16[12,8,256]{2,1,0:T(8,128)(2,1)} %book_ref.1) | copy-start | bytes 147460
  0.6 30.7 %copy-start = (s32[1,96,1024]{2,1,0:T(8,128)S(1)}, s32[1,96,1024]{2,1,0:T(8,128)}, u32[]{:S(2)}) copy-start(s32[1,96,1024]{2,1,0:T(8,128)} %param.5) | copy-start | bytes 1179652
  2.6 32.0 %all-to-all-start = ((bf16[16,208,128]{2,1,0:T(8,128)(2,1)}), bf16[16,208,128]{2,1,0:T(8,128)(2,1)S(1)}, u32[]{:S(2)}, u32[]{:S(2)}) async-start(bf16[16,208,128]{2,1,0:T(8,128)(2,1)} %shard_map.59), calls=%async_computation | async-start | bytes 1703936 | tf_op jit(solution)/shard_map/all_to_all | solution.py:349
  13.3 3.9 %collective-permute-start.2 = (bf16[6,8,256]{2,1,0:T(8,128)(2,1)S(1)}, bf16[6,8,256]{2,1,0:T(8,128)(2,1)S(1)}, u32[]{:S(2)}, u32[]{:S(2)}) collective-permute-start(bf16[6,8,256]{2,1,0:T(8,128)(2,1)S(1)} %shard_map.60), channel_id=1, source_target_pairs={{0,3},{1,0},{2,1},{3,2},{4,7},{5,4},{6,5},{7,6},{8,11},{9,8},{10,9... | collective-permute-start | bytes 73736 | tf_op jit(solution)/shard_map/ppermute | solution.py:346
  16.1 4.2 %collective-permute-start.1 = (bf16[6,8,256]{2,1,0:T(8,128)(2,1)S(1)}, bf16[6,8,256]{2,1,0:T(8,128)(2,1)S(1)}, u32[]{:S(2)}, u32[]{:S(2)}) collective-permute-start(bf16[6,8,256]{2,1,0:T(8,128)(2,1)S(1)} %shard_map.60), channel_id=1, source_target_pairs={{0,2},{1,3},{2,0},{3,1},{4,6},{5,7},{6,4},{7,5},{8,10},{9,11},{10,... | collective-permute-start | bytes 73736 | tf_op jit(solution)/shard_map/ppermute | solution.py:346
  16.5 4.4 %collective-permute-start = (bf16[6,8,256]{2,1,0:T(8,128)(2,1)S(1)}, bf16[6,8,256]{2,1,0:T(8,128)(2,1)S(1)}, u32[]{:S(2)}, u32[]{:S(2)}) collective-permute-start(bf16[6,8,256]{2,1,0:T(8,128)(2,1)S(1)} %shard_map.60), channel_id=1, source_target_pairs={{0,1},{1,2},{2,3},{3,0},{4,5},{5,6},{6,7},{7,4},{8,9},{9,10},{10,1... | collective-permute-start | bytes 73736 | tf_op jit(solution)/shard_map/ppermute | solution.py:346
  20.9 6.2 %collective-permute-start.4 = (bf16[4,6,8,256]{3,2,1,0:T(8,128)(2,1)S(1)}, bf16[4,6,8,256]{3,2,1,0:T(8,128)(2,1)S(1)}, u32[]{:S(2)}, u32[]{:S(2)}) collective-permute-start(bf16[4,6,8,256]{3,2,1,0:T(8,128)(2,1)S(1)} %pad_maximum_fusion.near_ref), channel_id=1, source_target_pairs={{0,4},{4,0},{1,5},{5,1},{2,6},{6,2},{3,7},{7,3},{8,12},{12,8},{9,1... | collective-permute-start | bytes 294920 | tf_op jit(solution)/shard_map/ppermute | solution.py:348
  23.4 7.0 %collective-permute-start.3 = (bf16[4,6,8,256]{3,2,1,0:T(8,128)(2,1)S(1)}, bf16[4,6,8,256]{3,2,1,0:T(8,128)(2,1)S(1)}, u32[]{:S(2)}, u32[]{:S(2)}) collective-permute-start(bf16[4,6,8,256]{3,2,1,0:T(8,128)(2,1)S(1)} %pad_maximum_fusion.near_ref), channel_id=1, source_target_pairs={{0,8},{8,0},{1,9},{9,1},{2,10},{10,2},{3,11},{11,3},{4,12},{12,4},... | collective-permute-start | bytes 294920 | tf_op jit(solution)/shard_map/ppermute | solution.py:353
  27.1 4.2 %collective-permute-start.5 = (bf16[4,6,8,256]{3,2,1,0:T(8,128)(2,1)S(1)}, bf16[4,6,8,256]{3,2,1,0:T(8,128)(2,1)S(1)}, u32[]{:S(2)}, u32[]{:S(2)}) collective-permute-start(bf16[4,6,8,256]{3,2,1,0:T(8,128)(2,1)S(1)} %collective-permute-done.4.far_ref), channel_id=1, source_target_pairs={{0,8},{8,0},{1,9},{9,1},{2,10},{10,2},{3,11},{11,3},{4,12},{12,4},... | collective-permute-start | bytes 294920 | tf_op jit(solution)/shard_map/ppermute | solution.py:353
  34.6 3.5 %collective-permute-start.6 = (bf16[16,208,128]{2,1,0:T(8,128)(2,1)S(1)}, bf16[16,208,128]{2,1,0:T(8,128)(2,1)S(1)}, u32[]{:S(2)}, u32[]{:S(2)}) collective-permute-start(bf16[16,208,128]{2,1,0:T(8,128)(2,1)S(1)} %all-to-all-done.pack_ref.own_ref), channel_id=1, source_target_pairs={{0,8},{8,0},{1,9},{9,1},{2,10},{10,2},{3,11},{11,3},{4,12},{12,4},... | collective-permute-start | bytes 2555912 | tf_op jit(solution)/shard_map/ppermute | solution.py:358
  65.8 4.8 %collective-permute-start.7 = (f32[512,768]{1,0:T(8,128)S(1)}, f32[512,768]{1,0:T(8,128)S(1)}, u32[]{:S(2)}, u32[]{:S(2)}) collective-permute-start(f32[512,768]{1,0:T(8,128)S(1)} %get-tuple-element.14), channel_id=1, source_target_pairs={{0,8},{8,0},{1,9},{9,1},{2,10},{10,2},{3,11},{11,3},{4,12},{12,4},... | collective-permute-start | bytes 4718600 | tf_op jit(solution)/shard_map/ppermute | solution.py:375
  69.9 3.3 %collective-permute-start.8 = (f32[8,2,3,16,128]{4,3,2,1,0:T(8,128)S(1)}, f32[8,2,3,16,128]{4,3,2,1,0:T(8,128)S(1)}, u32[]{:S(2)}, u32[]{:S(2)}) collective-permute-start(f32[8,2,3,16,128]{4,3,2,1,0:T(8,128)S(1)} %shard_map.66), channel_id=1, source_target_pairs={{0,8},{8,0},{1,9},{9,1},{2,10},{10,2},{3,11},{11,3},{4,12},{12,4},... | collective-permute-start | bytes 1179656 | tf_op jit(solution)/shard_map/ppermute | solution.py:378
  73.3 17.9 %collective-permute-start.9 = (s16[8,208,128]{2,1,0:T(8,128)(2,1)S(1)}, s16[8,208,128]{2,1,0:T(8,128)(2,1)S(1)}, u32[]{:S(2)}, u32[]{:S(2)}) collective-permute-start(s16[8,208,128]{2,1,0:T(8,128)(2,1)S(1)} %get-tuple-element.18), channel_id=1, source_target_pairs={{0,128},{128,0},{1,129},{129,1},{2,130},{130,2},{3,131},{131,3},{4... | collective-permute-start | bytes 1277960 | tf_op jit(solution)/shard_map/ppermute | solution.py:388
  110.7 5.5 %collective-permute-start.12 = (f32[48,128]{1,0:T(8,128)S(1)}, f32[48,128]{1,0:T(8,128)S(1)}, u32[]{:S(2)}, u32[]{:S(2)}) collective-permute-start(f32[48,128]{1,0:T(8,128)S(1)} %shard_map.69.own_ref), channel_id=1, source_target_pairs={{0,136},{8,128},{128,8},{136,0},{1,137},{9,129},{129,9},{137,1},{2... | collective-permute-start | bytes 73736 | tf_op jit(solution)/shard_map/ppermute | solution.py:401
  114.7 1.5 %collective-permute-start.11 = (f32[48,128]{1,0:T(8,128)S(1)}, f32[48,128]{1,0:T(8,128)S(1)}, u32[]{:S(2)}, u32[]{:S(2)}) collective-permute-start(f32[48,128]{1,0:T(8,128)S(1)} %shard_map.69.own_ref), channel_id=1, source_target_pairs={{0,8},{8,0},{1,9},{9,1},{2,10},{10,2},{3,11},{11,3},{4,12},{12,4},... | collective-permute-start | bytes 73736 | tf_op jit(solution)/shard_map/ppermute | solution.py:402
  114.7 2.7 %collective-permute-start.10 = (f32[48,128]{1,0:T(8,128)S(1)}, f32[48,128]{1,0:T(8,128)S(1)}, u32[]{:S(2)}, u32[]{:S(2)}) collective-permute-start(f32[48,128]{1,0:T(8,128)S(1)} %shard_map.69.own_ref), channel_id=1, source_target_pairs={{0,128},{128,0},{1,129},{129,1},{2,130},{130,2},{3,131},{131,3},{4... | collective-permute-start | bytes 73736 | tf_op jit(solution)/shard_map/ppermute | solution.py:400

commit v7 on v6

--- a/solution.py
+++ b/solution.py
@@ -36,14 +36,23 @@
     return jnp.clip(scaled, -32767.0, 32767.0).astype(i32).astype(i16)
 
 
-def exponent_rows(exponent):
-    column = jnp.concatenate([exponent, jnp.zeros((LANES - exponent.shape[0], 1), f32)], axis=0)
-    return jnp.transpose(jnp.broadcast_to(column, (LANES, LANES)))[:16].astype(i32).astype(i16)
-
-
-def scale_column(rows, count):
-    row = rows.astype(i32).astype(f32)[:1]
-    return jnp.exp2(jnp.transpose(jnp.broadcast_to(row, (LANES, LANES)))[:count])
+def exponent_tails(query, sums=None):
+    size = query[0].shape[0]
+    lane = lax.broadcasted_iota(i32, (size, LANES), 1)
+    block = jnp.zeros((size, LANES), f32)
+    for c, exponent in enumerate(query):
+        block = jnp.where(lane == c, exponent, block)
+    parts = [block] if sums is None else [block, jnp.broadcast_to(sums, (sums.shape[0], LANES))]
+    parts.append(jnp.zeros((LANES - sum(part.shape[0] for part in parts), LANES), f32))
+    turned = jnp.transpose(jnp.concatenate(parts, axis=0))
+    return [jnp.broadcast_to(turned[c : c + 1], (16, LANES)).astype(i32).astype(i16) for c in range(len(query))]
+
+
+def scale_columns(words_ref):
+    peers, length, _ = words_ref.shape
+    rows = [words_ref[c, length - 16 :].astype(i32).astype(f32)[:1] for c in range(peers)]
+    rows.append(jnp.zeros((LANES - peers, LANES), f32))
+    return jnp.exp2(jnp.transpose(jnp.concatenate(rows, axis=0)))
 
 
 def spread_kernel(queries_ref, positives_ref, out_ref, block_ref, sems):
@@ -230,10 +239,12 @@
     peers = out_ref.shape[0]
     half, width = sums_ref.shape
     size = half // (2 * peers)
+    query = []
     for c in range(peers):
         rows = pl.ds(pl.multiple_of((1 - place_ref[4]) * (half // 2) + c * size, size), size)
-        exponent = put_query_words(sums_ref[rows] + cross_ref[rows], out_ref, c)
-        out_ref[c, width // LANES * size :] = exponent_rows(exponent)
+        query.append(put_query_words(sums_ref[rows] + cross_ref[rows], out_ref, c))
+    for c, tail in enumerate(exponent_tails(query)):
+        out_ref[c, width // LANES * size :] = tail
     codeword_sums(place_ref[0], grads_ref, codes_ref, parts_ref)
 
 
@@ -248,20 +259,24 @@
     totals = totals.reshape(-1, LANES)
     totals_exponent = exponents(totals)
     totals = as_words(totals, totals_exponent)
+    scales = scale_columns(words_ref)
+    query = []
     for c in range(peers):
         rows = pl.ds(pl.multiple_of(place_ref[4] * (half // 2) + c * size, size), size)
-        received = take_query_words(words_ref, c, scale_column(words_ref[c, base:], size), width)
-        exponent = put_query_words(sums_ref[rows] + cross_ref[rows] + received, out_ref, c)
+        received = take_query_words(words_ref, c, scales[:size, c : c + 1], width)
+        query.append(put_query_words(sums_ref[rows] + cross_ref[rows] + received, out_ref, c))
         out_ref[c, base : base + totals.shape[0]] = totals
-        out_ref[c, base + totals.shape[0] :] = exponent_rows(jnp.concatenate([exponent, totals_exponent], axis=0))
+    for c, tail in enumerate(exponent_tails(query, totals_exponent)):
+        out_ref[c, base + totals.shape[0] :] = tail
 
 
 def unpack_query_kernel(words_ref, query_ref):
-    peers, length, _ = words_ref.shape
+    peers = words_ref.shape[0]
     size, width = query_ref.shape
+    scales = scale_columns(words_ref)
     query = 0.0
     for c in range(peers):
-        query = query + take_query_words(words_ref, c, scale_column(words_ref[c, length - 16 :], size), width)
+        query = query + take_query_words(words_ref, c, scales[:size, c : c + 1], width)
     query_ref[...] = query.astype(bf16)
 
 
@@ -269,9 +284,10 @@
     peers, length, _ = words_ref.shape
     count = sums_ref.shape[0]
     start = length - 16 - count
+    scales = scale_columns(words_ref)
     sums = 0.0
     for c in range(peers):
-        scale = scale_column(words_ref[c, length - 16 :], size + count)[size:]
+        scale = scales[size : size + count, c : c + 1]
         sums = sums + words_ref[c, start : start + count].astype(i32).astype(f32) * scale
     sums_ref[...] = sums
 

time: 119 us -> 119 us (level)
  no operation moved by 1% of the time
where the time goes in v7:
time: 119 us; the launch traced here: 118 us
  blocking collectives  52.5 us (44%)
  starting transfers between devices  30.5 us (26%)
  Pallas kernels  25.9 us (22%)
  waiting for transfers between devices  8.45 us (7%)
    pallas_call x12, Pallas kernels, call(): pl.pallas_call(kernel, out_shape=shapes, in_specs=specs, out_specs=outs i...  25.9 us
    all_to_all x1, blocking collectives, per_device(): words = lax.all_to_all(words, 'z', 0, 0)  17.8 us
    all_to_all x1, blocking collectives, per_device(): lax.all_to_all(parts.reshape(16, subspaces // 32, 16, LANES), SUB + ('xl'...  17.4 us
    all_to_all x1, blocking collectives, per_device(): stats = lax.all_to_all(stats, CHIP + ('core',), 0, 0, tiled=True)  17.4 us
    all_to_all x1, starting transfers between devices, per_device(): own = lax.all_to_all(own, CHIP, 0, 0)  10.1 us
    ppermute x1, starting transfers between devices, per_device(): corner = lax.ppermute(sums, ('xl', 'core'), [(i, 3 - i) for i in range(4)])  3.96 us
    ppermute x3, starting transfers between devices, per_device(): lax.ppermute(share, 'y', [(i, (i + k) % 4) for i in range(4)])  3.85 us
    ppermute x3, waiting for transfers between devices, per_device(): lax.ppermute(share, 'y', [(i, (i + k) % 4) for i in range(4)])  3.7 us
  transfers between devices with their start and end apart: 14, of which 8 were waited for; matrix products, arithmetic and copies ran while one was open for 0% of the time, Pallas kernels for 9%

profile of v7, /device:TPU:1, one launch (start us, length us, event | category | flops | bytes accessed | tf_op | source)
XLA Modules:
  0.0 118.3 jit_solution(1801594449881186176)
XLA Ops:
  0.6 0.0 copy-start.1
  0.6 0.0 copy-start
  0.7 1.9 %shard_map.59 = bf16[16,208,128]{2,1,0:T(8,128)(2,1)} custom-call(bf16[32,768]{1,0:T(8,128)(2,1)} %bitcast.18, s32[1,32]{1,0:T(1,128)} %positives_ref.1), custom_call_target="tpu_custom_call" | custom-call | flops 1000000 | bytes 65536 | tf_op jit(solution)/shard_map/pallas_call | solution.py:321
  2.6 10.1 %all-to-all-start = ((bf16[16,208,128]{2,1,0:T(8,128)(2,1)}), bf16[16,208,128]{2,1,0:T(8,128)(2,1)S(1)}, u32[]{:S(2)}, u32[]{:S(2)}) async-start(bf16[16,208,128]{2,1,0:T(8,128)(2,1)} %shard_map.59), calls=%async_computation | async-start | bytes 1703936 | tf_op jit(solution)/shard_map/all_to_all | solution.py:365
  12.7 0.1 stack.38.place_ref
  12.7 0.0 copy-done.1
  12.7 0.5 shard_map.60
  13.3 2.8 %collective-permute-start.2 = (bf16[6,8,256]{2,1,0:T(8,128)(2,1)S(1)}, bf16[6,8,256]{2,1,0:T(8,128)(2,1)S(1)}, u32[]{:S(2)}, u32[]{:S(2)}) collective-permute-start(bf16[6,8,256]{2,1,0:T(8,128)(2,1)S(1)} %shard_map.60), channel_id=1, source_target_pairs={{0,3},{1,0},{2,1},{3,2},{4,7},{5,4},{6,5},{7,6},{8,11},{9,8},{10,9... | collective-permute-start | bytes 73736 | tf_op jit(solution)/shard_map/ppermute | solution.py:362
  16.1 0.3 collective-permute-start.1
  16.5 0.7 collective-permute-start
  17.2 0.0 collective-permute-done.2
  17.2 3.2 %collective-permute-done.1 = bf16[6,8,256]{2,1,0:T(8,128)(2,1)S(1)} collective-permute-done((bf16[6,8,256]{2,1,0:T(8,128)(2,1)S(1)}, bf16[6,8,256]{2,1,0:T(8,128)(2,1)S(1)}, u32[]{:S(2)}, u32[]{:S(2)}) %collective-permute-start.1) | collective-permute-done | bytes 24608 | tf_op jit(solution)/shard_map/ppermute | solution.py:362
  20.3 0.5 collective-permute-done
  20.9 2.5 %collective-permute-start.4 = (bf16[4,6,8,256]{3,2,1,0:T(8,128)(2,1)S(1)}, bf16[4,6,8,256]{3,2,1,0:T(8,128)(2,1)S(1)}, u32[]{:S(2)}, u32[]{:S(2)}) collective-permute-start(bf16[4,6,8,256]{3,2,1,0:T(8,128)(2,1)S(1)} %pad_maximum_fusion.near_ref), channel_id=1, source_target_pairs={{0,4},{4,0},{1,5},{5,1},{2,6},{6,2},{3,7},{7,3},{8,12},{12,8},{9,1... | collective-permute-start | bytes 294920 | tf_op jit(solution)/shard_map/ppermute | solution.py:364
  23.4 2.4 %collective-permute-start.3 = (bf16[4,6,8,256]{3,2,1,0:T(8,128)(2,1)S(1)}, bf16[4,6,8,256]{3,2,1,0:T(8,128)(2,1)S(1)}, u32[]{:S(2)}, u32[]{:S(2)}) collective-permute-start(bf16[4,6,8,256]{3,2,1,0:T(8,128)(2,1)S(1)} %pad_maximum_fusion.near_ref), channel_id=1, source_target_pairs={{0,8},{8,0},{1,9},{9,1},{2,10},{10,2},{3,11},{11,3},{4,12},{12,4},... | collective-permute-start | bytes 294920 | tf_op jit(solution)/shard_map/ppermute | solution.py:369
  25.9 1.2 %collective-permute-done.4.far_ref = bf16[4,6,8,256]{3,2,1,0:T(8,128)(2,1)S(1)} collective-permute-done((bf16[4,6,8,256]{3,2,1,0:T(8,128)(2,1)S(1)}, bf16[4,6,8,256]{3,2,1,0:T(8,128)(2,1)S(1)}, u32[]{:S(2)}, u32[]{:S(2)}) %collective-permute-start.4) | collective-permute-done | bytes 98336 | tf_op jit(solution)/shard_map/ppermute | solution.py:364
  27.1 3.3 %collective-permute-start.5 = (bf16[4,6,8,256]{3,2,1,0:T(8,128)(2,1)S(1)}, bf16[4,6,8,256]{3,2,1,0:T(8,128)(2,1)S(1)}, u32[]{:S(2)}, u32[]{:S(2)}) collective-permute-start(bf16[4,6,8,256]{3,2,1,0:T(8,128)(2,1)S(1)} %collective-permute-done.4.far_ref), channel_id=1, source_target_pairs={{0,8},{8,0},{1,9},{9,1},{2,10},{10,2},{3,11},{11,3},{4,12},{12,4},... | collective-permute-start | bytes 294920 | tf_op jit(solution)/shard_map/ppermute | solution.py:369
  30.4 0.0 collective-permute-done.3.near_cross_ref
  30.4 0.9 collective-permute-done.5.far_cross_ref
  31.3 0.0 copy-done
  31.3 3.2 %shard_map.61.passages_ref = bf16[768,1024]{1,0:T(8,128)(2,1)S(1)} custom-call(s32[5]{0:T(128)S(1)} %stack.38.place_ref, s32[96,1024]{1,0:T(8,128)S(1)} %bitcast.13, bf16[4,6,8,256]{3,2,1,0:T(8,128)(2,1)S(1)} %pad_maximum_fusion.near_ref, bf16[4,6,8,256]{3,2,1,0:T(8,128)(2,1)S(1)} %collective-permute-done.3.near_cross_ref, ...), custom_call_target="tpu_custom_call" | custom-call | flops 1000000 | bytes 65536 | tf_op jit(solution)/shard_map/pallas_call | solution.py:321
  34.6 0.0 all-to-all-done.pack_ref.own_ref
  34.6 1.5 %collective-permute-start.6 = (bf16[16,208,128]{2,1,0:T(8,128)(2,1)S(1)}, bf16[16,208,128]{2,1,0:T(8,128)(2,1)S(1)}, u32[]{:S(2)}, u32[]{:S(2)}) collective-permute-start(bf16[16,208,128]{2,1,0:T(8,128)(2,1)S(1)} %all-to-all-done.pack_ref.own_ref), channel_id=1, source_target_pairs={{0,8},{8,0},{1,9},{9,1},{2,10},{10,2},{3,11},{11,3},{4,12},{12,4},... | collective-permute-start | bytes 2555912 | tf_op jit(solution)/shard_map/ppermute | solution.py:374
  36.1 1.3 %shard_map.62.own_logs_ref = f32[4,128]{1,0:T(4,128)S(1)} custom-call(bf16[16,208,128]{2,1,0:T(8,128)(2,1)S(1)} %all-to-all-done.pack_ref.own_ref, bf16[768,1024]{1,0:T(8,128)(2,1)S(1)} %shard_map.61.passages_ref), custom_call_target="tpu_custom_call" | custom-call | flops 1000000 | bytes 65536 | tf_op jit(solution)/shard_map/pallas_call | solution.py:321
  37.4 0.7 collective-permute-done.6.pack_ref.other_ref
  38.1 1.3 %shard_map.63 = f32[32,8,128]{2,1,0:T(8,128)S(1)} custom-call(bf16[16,208,128]{2,1,0:T(8,128)(2,1)S(1)} %collective-permute-done.6.pack_ref.other_ref, bf16[768,1024]{1,0:T(8,128)(2,1)S(1)} %shard_map.61.passages_ref, f32[4,128]{1,0:T(4,128)S(1)} %shard_map.62.own_logs_ref), custom_call_target="tpu_custom_call" | custom-call | flops 1000000 | bytes 65536 | tf_op jit(solution)/shard_map/pallas_call | solution.py:321
  39.4 17.4 %all_to_all.20.stats_ref = f32[32,8,128]{2,1,0:T(8,128)S(1)} all-to-all(f32[32,8,128]{2,1,0:T(8,128)S(1)} %shard_map.63), channel_id=1, replica_groups=mesh['xl'=2,'z'=8,'core'=2,'xh'=2,'y'=4] {'xl','z','core'}, dimensions={0} | all-to-all | bytes 262144 | tf_op jit(solution)/shard_map/all_to_all | solution.py:377
  56.8 9.0 %shard_map.64 = (f32[512,768]{1,0:T(8,128)S(1)}, f32[512,768]{1,0:T(8,128)S(1)}, bf16[768,1024]{1,0:T(8,128)(2,1)S(1)}) custom-call(s32[5]{0:T(128)S(1)} %stack.38.place_ref, f32[32,8,128]{2,1,0:T(8,128)S(1)} %all_to_all.20.stats_ref, bf16[16,208,128]{2,1,0:T(8,128)(2,1)S(1)} %all-to-all-done.pack_ref.own_ref, ...), custom_call_target="tpu_custom_call" | custom-call | flops 1000000 | bytes 65536 | tf_op jit(solution)/shard_map/pallas_call | solution.py:321
  65.8 1.7 %collective-permute-start.7 = (f32[512,768]{1,0:T(8,128)S(1)}, f32[512,768]{1,0:T(8,128)S(1)}, u32[]{:S(2)}, u32[]{:S(2)}) collective-permute-start(f32[512,768]{1,0:T(8,128)S(1)} %get-tuple-element.14), channel_id=1, source_target_pairs={{0,8},{8,0},{1,9},{9,1},{2,10},{10,2},{3,11},{11,3},{4,12},{12,4},... | collective-permute-start | bytes 4718600 | tf_op jit(solution)/shard_map/ppermute | solution.py:391
  67.5 2.4 %shard_map.66 = f32[8,2,3,16,128]{4,3,2,1,0:T(8,128)S(1)} custom-call(s32[5]{0:T(128)S(1)} %stack.38.place_ref, bf16[768,1024]{1,0:T(8,128)(2,1)S(1)} %get-tuple-element.15.grads_ref, s32[96,1024]{1,0:T(8,128)S(1)} %bitcast.14), custom_call_target="tpu_custom_call" | custom-call | flops 1000000 | bytes 65536 | tf_op jit(solution)/shard_map/pallas_call | solution.py:321
  69.9 0.1 collective-permute-start.8
  70.0 0.6 collective-permute-done.7.cross_ref
  70.5 2.7 %shard_map.65 = (f32[8,2,3,16,128]{4,3,2,1,0:T(8,128)S(1)}, s16[8,208,128]{2,1,0:T(8,128)(2,1)S(1)}) custom-call(s32[5]{0:T(128)S(1)} %stack.38.place_ref, bf16[768,1024]{1,0:T(8,128)(2,1)S(1)} %get-tuple-element.15.grads_ref, s32[96,1024]{1,0:T(8,128)S(1)} %bitcast.15, f32[512,768]{1,0:T(8,128)S(1)} %get-tuple-element.13.sums_ref, ...), custom_call_target="tpu_custom_call" | custom-call | flops 1000000 | bytes 65536 | tf_op jit(solution)/shard_map/pallas_call | solution.py:321
  73.2 0.0 collective-permute-done.8
  73.2 0.1 add.11
  73.3 0.5 collective-permute-start.9
  73.8 17.4 %all_to_all.21.parts_ref = f32[16,3,16,128]{3,2,1,0:T(8,128)S(1)} all-to-all(f32[16,3,16,128]{3,2,1,0:T(8,128)S(1)} %bitcast.17), channel_id=1, replica_groups=mesh['xl'=2,'z'=8,'core'=2,'xh'=2,'y'=4] {'xh','y','xl'}, dimensions={0} | all-to-all | bytes 786432 | tf_op jit(solution)/shard_map/all_to_all | solution.py:405
  91.2 0.0 collective-permute-done.9.words_ref
  91.2 1.2 %shard_map.67 = s16[8,256,128]{2,1,0:T(8,128)(2,1)S(1)} custom-call(s32[5]{0:T(128)S(1)} %stack.38.place_ref, f32[512,768]{1,0:T(8,128)S(1)} %get-tuple-element.13.sums_ref, f32[512,768]{1,0:T(8,128)S(1)} %collective-permute-done.7.cross_ref, s16[8,208,128]{2,1,0:T(8,128)(2,1)S(1)} %collective-permute-done.9.words_ref, ...), custom_call_target="tpu_custom_call" | custom-call | flops 1000000 | bytes 65536 | tf_op jit(solution)/shard_map/pallas_call | solution.py:321
  92.4 17.8 %all_to_all.22.words_ref = s16[8,256,128]{2,1,0:T(8,128)(2,1)S(1)} all-to-all(s16[8,256,128]{2,1,0:T(8,128)(2,1)S(1)} %shard_map.67), channel_id=1, replica_groups=mesh['xl'=2,'z'=8,'core'=2,'xh'=2,'y'=4] {'z'}, dimensions={0} | all-to-all | bytes 1048576 | tf_op jit(solution)/shard_map/all_to_all | solution.py:414
  110.1 0.2 shard_map.69.own_ref
  110.4 4.0 %collective-permute-start.12 = (f32[48,128]{1,0:T(8,128)S(1)}, f32[48,128]{1,0:T(8,128)S(1)}, u32[]{:S(2)}, u32[]{:S(2)}) collective-permute-start(f32[48,128]{1,0:T(8,128)S(1)} %shard_map.69.own_ref), channel_id=1, source_target_pairs={{0,136},{8,128},{128,8},{136,0},{1,137},{9,129},{129,9},{137,1},{2... | collective-permute-start | bytes 73736 | tf_op jit(solution)/shard_map/ppermute | solution.py:417
  114.4 0.0 collective-permute-start.11
  114.4 0.6 collective-permute-start.10
  114.9 0.8 shard_map.68
  115.8 0.1 collective-permute-done.12.corner_ref
  115.9 0.0 collective-permute-done.11.cross_ref
  115.9 1.2 collective-permute-done.10.beside_ref
  117.0 1.3 %shard_map.70 = f32[12,8,256]{2,1,0:T(8,128)} custom-call(s32[5]{0:T(128)S(1)} %stack.38.place_ref, f32[48,128]{1,0:T(8,128)S(1)} %shard_map.69.own_ref, f32[48,128]{1,0:T(8,128)S(1)} %collective-permute-done.10.beside_ref, f32[48,128]{1,0:T(8,128)S(1)} %collective-permute-done.11.cross_ref, f32[48,128]{1,0:T(8,128)S(1)} %collective-permute-done.12.corner_ref), custom_call_target="tpu_custom_call" | custom-call | flops 1000000 | bytes 65536 | tf_op jit(solution)/shard_map/pallas_call | solution.py:321
  (1 shorter events, 0.0 us)
Async XLA Ops:
  0.6 12.1 %copy-start.1 = (bf16[12,8,256]{2,1,0:T(8,128)(2,1)S(1)}, bf16[12,8,256]{2,1,0:T(8,128)(2,1)}, u32[]{:S(2)}) copy-start(bf16[12,8,256]{2,1,0:T(8,128)(2,1)} %book_ref.1) | copy-start | bytes 147460
  0.6 30.7 %copy-start = (s32[1,96,1024]{2,1,0:T(8,128)S(1)}, s32[1,96,1024]{2,1,0:T(8,128)}, u32[]{:S(2)}) copy-start(s32[1,96,1024]{2,1,0:T(8,128)} %param.5) | copy-start | bytes 1179652
  2.6 32.0 %all-to-all-start = ((bf16[16,208,128]{2,1,0:T(8,128)(2,1)}), bf16[16,208,128]{2,1,0:T(8,128)(2,1)S(1)}, u32[]{:S(2)}, u32[]{:S(2)}) async-start(bf16[16,208,128]{2,1,0:T(8,128)(2,1)} %shard_map.59), calls=%async_computation | async-start | bytes 1703936 | tf_op jit(solution)/shard_map/all_to_all | solution.py:365
  13.3 3.9 %collective-permute-start.2 = (bf16[6,8,256]{2,1,0:T(8,128)(2,1)S(1)}, bf16[6,8,256]{2,1,0:T(8,128)(2,1)S(1)}, u32[]{:S(2)}, u32[]{:S(2)}) collective-permute-start(bf16[6,8,256]{2,1,0:T(8,128)(2,1)S(1)} %shard_map.60), channel_id=1, source_target_pairs={{0,3},{1,0},{2,1},{3,2},{4,7},{5,4},{6,5},{7,6},{8,11},{9,8},{10,9... | collective-permute-start | bytes 73736 | tf_op jit(solution)/shard_map/ppermute | solution.py:362
  16.1 4.2 %collective-permute-start.1 = (bf16[6,8,256]{2,1,0:T(8,128)(2,1)S(1)}, bf16[6,8,256]{2,1,0:T(8,128)(2,1)S(1)}, u32[]{:S(2)}, u32[]{:S(2)}) collective-permute-start(bf16[6,8,256]{2,1,0:T(8,128)(2,1)S(1)} %shard_map.60), channel_id=1, source_target_pairs={{0,2},{1,3},{2,0},{3,1},{4,6},{5,7},{6,4},{7,5},{8,10},{9,11},{10,... | collective-permute-start | bytes 73736 | tf_op jit(solution)/shard_map/ppermute | solution.py:362
  16.5 4.4 %collective-permute-start = (bf16[6,8,256]{2,1,0:T(8,128)(2,1)S(1)}, bf16[6,8,256]{2,1,0:T(8,128)(2,1)S(1)}, u32[]{:S(2)}, u32[]{:S(2)}) collective-permute-start(bf16[6,8,256]{2,1,0:T(8,128)(2,1)S(1)} %shard_map.60), channel_id=1, source_target_pairs={{0,1},{1,2},{2,3},{3,0},{4,5},{5,6},{6,7},{7,4},{8,9},{9,10},{10,1... | collective-permute-start | bytes 73736 | tf_op jit(solution)/shard_map/ppermute | solution.py:362
  20.9 6.2 %collective-permute-start.4 = (bf16[4,6,8,256]{3,2,1,0:T(8,128)(2,1)S(1)}, bf16[4,6,8,256]{3,2,1,0:T(8,128)(2,1)S(1)}, u32[]{:S(2)}, u32[]{:S(2)}) collective-permute-start(bf16[4,6,8,256]{3,2,1,0:T(8,128)(2,1)S(1)} %pad_maximum_fusion.near_ref), channel_id=1, source_target_pairs={{0,4},{4,0},{1,5},{5,1},{2,6},{6,2},{3,7},{7,3},{8,12},{12,8},{9,1... | collective-permute-start | bytes 294920 | tf_op jit(solution)/shard_map/ppermute | solution.py:364
  23.4 7.0 %collective-permute-start.3 = (bf16[4,6,8,256]{3,2,1,0:T(8,128)(2,1)S(1)}, bf16[4,6,8,256]{3,2,1,0:T(8,128)(2,1)S(1)}, u32[]{:S(2)}, u32[]{:S(2)}) collective-permute-start(bf16[4,6,8,256]{3,2,1,0:T(8,128)(2,1)S(1)} %pad_maximum_fusion.near_ref), channel_id=1, source_target_pairs={{0,8},{8,0},{1,9},{9,1},{2,10},{10,2},{3,11},{11,3},{4,12},{12,4},... | collective-permute-start | bytes 294920 | tf_op jit(solution)/shard_map/ppermute | solution.py:369
  27.1 4.2 %collective-permute-start.5 = (bf16[4,6,8,256]{3,2,1,0:T(8,128)(2,1)S(1)}, bf16[4,6,8,256]{3,2,1,0:T(8,128)(2,1)S(1)}, u32[]{:S(2)}, u32[]{:S(2)}) collective-permute-start(bf16[4,6,8,256]{3,2,1,0:T(8,128)(2,1)S(1)} %collective-permute-done.4.far_ref), channel_id=1, source_target_pairs={{0,8},{8,0},{1,9},{9,1},{2,10},{10,2},{3,11},{11,3},{4,12},{12,4},... | collective-permute-start | bytes 294920 | tf_op jit(solution)/shard_map/ppermute | solution.py:369
  34.6 3.5 %collective-permute-start.6 = (bf16[16,208,128]{2,1,0:T(8,128)(2,1)S(1)}, bf16[16,208,128]{2,1,0:T(8,128)(2,1)S(1)}, u32[]{:S(2)}, u32[]{:S(2)}) collective-permute-start(bf16[16,208,128]{2,1,0:T(8,128)(2,1)S(1)} %all-to-all-done.pack_ref.own_ref), channel_id=1, source_target_pairs={{0,8},{8,0},{1,9},{9,1},{2,10},{10,2},{3,11},{11,3},{4,12},{12,4},... | collective-permute-start | bytes 2555912 | tf_op jit(solution)/shard_map/ppermute | solution.py:374
  65.8 4.8 %collective-permute-start.7 = (f32[512,768]{1,0:T(8,128)S(1)}, f32[512,768]{1,0:T(8,128)S(1)}, u32[]{:S(2)}, u32[]{:S(2)}) collective-permute-start(f32[512,768]{1,0:T(8,128)S(1)} %get-tuple-element.14), channel_id=1, source_target_pairs={{0,8},{8,0},{1,9},{9,1},{2,10},{10,2},{3,11},{11,3},{4,12},{12,4},... | collective-permute-start | bytes 4718600 | tf_op jit(solution)/shard_map/ppermute | solution.py:391
  69.9 3.3 %collective-permute-start.8 = (f32[8,2,3,16,128]{4,3,2,1,0:T(8,128)S(1)}, f32[8,2,3,16,128]{4,3,2,1,0:T(8,128)S(1)}, u32[]{:S(2)}, u32[]{:S(2)}) collective-permute-start(f32[8,2,3,16,128]{4,3,2,1,0:T(8,128)S(1)} %shard_map.66), channel_id=1, source_target_pairs={{0,8},{8,0},{1,9},{9,1},{2,10},{10,2},{3,11},{11,3},{4,12},{12,4},... | collective-permute-start | bytes 1179656 | tf_op jit(solution)/shard_map/ppermute | solution.py:394
  73.3 17.9 %collective-permute-start.9 = (s16[8,208,128]{2,1,0:T(8,128)(2,1)S(1)}, s16[8,208,128]{2,1,0:T(8,128)(2,1)S(1)}, u32[]{:S(2)}, u32[]{:S(2)}) collective-permute-start(s16[8,208,128]{2,1,0:T(8,128)(2,1)S(1)} %get-tuple-element.18), channel_id=1, source_target_pairs={{0,128},{128,0},{1,129},{129,1},{2,130},{130,2},{3,131},{131,3},{4... | collective-permute-start | bytes 1277960 | tf_op jit(solution)/shard_map/ppermute | solution.py:404
  110.4 5.5 %collective-permute-start.12 = (f32[48,128]{1,0:T(8,128)S(1)}, f32[48,128]{1,0:T(8,128)S(1)}, u32[]{:S(2)}, u32[]{:S(2)}) collective-permute-start(f32[48,128]{1,0:T(8,128)S(1)} %shard_map.69.own_ref), channel_id=1, source_target_pairs={{0,136},{8,128},{128,8},{136,0},{1,137},{9,129},{129,9},{137,1},{2... | collective-permute-start | bytes 73736 | tf_op jit(solution)/shard_map/ppermute | solution.py:417
  114.4 1.5 %collective-permute-start.11 = (f32[48,128]{1,0:T(8,128)S(1)}, f32[48,128]{1,0:T(8,128)S(1)}, u32[]{:S(2)}, u32[]{:S(2)}) collective-permute-start(f32[48,128]{1,0:T(8,128)S(1)} %shard_map.69.own_ref), channel_id=1, source_target_pairs={{0,8},{8,0},{1,9},{9,1},{2,10},{10,2},{3,11},{11,3},{4,12},{12,4},... | collective-permute-start | bytes 73736 | tf_op jit(solution)/shard_map/ppermute | solution.py:418
  114.4 2.7 %collective-permute-start.10 = (f32[48,128]{1,0:T(8,128)S(1)}, f32[48,128]{1,0:T(8,128)S(1)}, u32[]{:S(2)}, u32[]{:S(2)}) collective-permute-start(f32[48,128]{1,0:T(8,128)S(1)} %shard_map.69.own_ref), channel_id=1, source_target_pairs={{0,128},{128,0},{1,129},{129,1},{2,130},{130,2},{3,131},{131,3},{4... | collective-permute-start | bytes 73736 | tf_op jit(solution)/shard_map/ppermute | solution.py:416

commit v8 on v7

--- a/solution.py
+++ b/solution.py
@@ -16,14 +16,6 @@
 CHIP = ("xl", "z")
 SUB = ("xh", "y")
 ROWS_BY_ROWS = (((1,), (1,)), ((), ()))
-
-
-def as_column(row):
-    return jnp.transpose(jnp.broadcast_to(row, (LANES, row.shape[1])))[:, :1]
-
-
-def as_row(column):
-    return jnp.transpose(jnp.broadcast_to(column, (column.shape[0], LANES)))[:1]
 
 
 def exponents(rows):
@@ -83,12 +75,14 @@
     return jnp.concatenate([query_columns(pack_ref, t, first, count) for t in range(6)], axis=1)
 
 
-def target_columns(pack_ref):
-    chips, length, _ = pack_ref.shape
-    tail = pack_ref[:, length - 16 :, :].astype(f32)
-    target = tail[:, 0, :] * LANES + tail[:, 1, :]
-    target = jnp.concatenate([target, jnp.zeros((LANES - chips, LANES), f32)], axis=0)
-    return jnp.transpose(target)
+def target_columns(packs):
+    parts = []
+    for pack_ref in packs:
+        length = pack_ref.shape[1]
+        tail = pack_ref[:, length - 16 :, :].astype(f32)
+        parts.append(tail[:, 0, :] * LANES + tail[:, 1, :])
+    parts.append(jnp.zeros((LANES - sum(part.shape[0] for part in parts), LANES), f32))
+    return jnp.transpose(jnp.concatenate(parts, axis=0))
 
 
 def decode_kernel(place_ref, codes_ref, near_ref, near_cross_ref, far_ref, far_cross_ref, out_ref):
@@ -124,14 +118,15 @@
 
 
 def local_logs(pack_ref, passages_ref):
-    rows = []
+    lane = lax.broadcasted_iota(i32, (LANES, LANES), 1)
+    block = jnp.zeros((LANES, LANES), f32)
     for b in range(2):
         tile = jnp.dot(query_rows(pack_ref, b * 8, 8), passages_ref[...], preferred_element_type=f32)
         peak = jnp.max(tile, axis=1, keepdims=True)
-        total = jnp.sum(jnp.exp(tile - peak), axis=1, keepdims=True)
-        row = as_row(peak + jnp.log(total))
-        rows += [row[:, j * LANES : (j + 1) * LANES] for j in range(2)]
-    return jnp.concatenate(rows, axis=0)
+        logs = peak + jnp.log(jnp.sum(jnp.exp(tile - peak), axis=1, keepdims=True))
+        for j in range(2):
+            block = jnp.where(lane == 2 * b + j, logs[j * LANES : (j + 1) * LANES], block)
+    return jnp.transpose(block)[:4]
 
 
 def own_scores_kernel(pack_ref, passages_ref, logs_ref):
@@ -163,19 +158,21 @@
     size = half // own_ref.shape[0]
     passages = passages_ref[...]
     spot = lax.broadcasted_iota(i32, (size, passage_count), 1) + offset
+    targets = target_columns((own_ref, other_ref))[:size].astype(i32)
+    logs = log_totals(core, stats_ref, 0) + log_totals(core, stats_ref, 1)
+    all_totals = jnp.transpose(jnp.concatenate([*logs, jnp.zeros((LANES - 8, LANES), f32)], axis=0))
     for h, pack_ref, sums_ref in ((1, other_ref, other_sums_ref), (0, own_ref, own_sums_ref)):
         for t in range(turned_ref.shape[0] // LANES):
             columns = query_columns(pack_ref, t, 0, pack_ref.shape[0])
             turned_ref[t * LANES : (t + 1) * LANES, h * half : (h + 1) * half] = jnp.transpose(columns)
-        totals = [as_column(row) for row in log_totals(core, stats_ref, h)]
-        targets = target_columns(pack_ref)[:size].astype(i32)
+        totals = [all_totals[:, 4 * h + j : 4 * h + j + 1] for j in range(4)]
         for b in range(half // BLOCK):
             tile = jnp.dot(query_rows(pack_ref, b * 8, 8), passages, preferred_element_type=f32)
             tile = jnp.exp(tile - jnp.concatenate(totals[2 * b : 2 * b + 2], axis=0))
             rows = slice(h * half + b * BLOCK, h * half + (b + 1) * BLOCK)
             pieces = []
             for c in range(BLOCK // size):
-                place = b * BLOCK // size + c
+                place = (h * half + b * BLOCK) // size + c
                 hits = jnp.where(targets[:, place : place + 1] == spot, 1.0, 0.0)
                 pieces.append(tile[c * size : (c + 1) * size] - hits)
             weight = jnp.concatenate(pieces, axis=0)

time: 119 us -> 118 us (level)
  no operation moved by 1% of the time
where the time goes in v8:
time: 118 us
  blocking collectives  52.5 us (44%)
  starting transfers between devices  30.3 us (26%)
  Pallas kernels  26 us (22%)
  waiting for transfers between devices  8.45 us (7%)
    pallas_call x12, Pallas kernels, call(): pl.pallas_call(kernel, out_shape=shapes, in_specs=specs, out_specs=outs i...  26 us
    all_to_all x1, blocking collectives, per_device(): words = lax.all_to_all(words, 'z', 0, 0)  17.8 us
    all_to_all x1, blocking collectives, per_device(): lax.all_to_all(parts.reshape(16, subspaces // 32, 16, LANES), SUB + ('xl'...  17.4 us
    all_to_all x1, blocking collectives, per_device(): stats = lax.all_to_all(stats, CHIP + ('core',), 0, 0, tiled=True)  17.4 us
    all_to_all x1, starting transfers between devices, per_device(): own = lax.all_to_all(own, CHIP, 0, 0)  10.1 us
    ppermute x1, starting transfers between devices, per_device(): corner = lax.ppermute(sums, ('xl', 'core'), [(i, 3 - i) for i in range(4)])  3.96 us
    ppermute x3, starting transfers between devices, per_device(): lax.ppermute(share, 'y', [(i, (i + k) % 4) for i in range(4)])  3.85 us
    ppermute x3, waiting for transfers between devices, per_device(): lax.ppermute(share, 'y', [(i, (i + k) % 4) for i in range(4)])  3.7 us
  transfers between devices with their start and end apart: 14, of which 8 were waited for; matrix products, arithmetic and copies ran while one was open for 0% of the time, Pallas kernels for 9%

profile of v8, /device:TPU:1, one launch (start us, length us, event | category | flops | bytes accessed | tf_op | source)
XLA Modules:
  0.0 118.2 jit_solution(10261357826201893092)
XLA Ops:
  0.6 0.0 copy-start.1
  0.6 0.0 copy-start
  0.7 1.9 %shard_map.59 = bf16[16,208,128]{2,1,0:T(8,128)(2,1)} custom-call(bf16[32,768]{1,0:T(8,128)(2,1)} %bitcast.18, s32[1,32]{1,0:T(1,128)} %positives_ref.1), custom_call_target="tpu_custom_call" | custom-call | flops 1000000 | bytes 65536 | tf_op jit(solution)/shard_map/pallas_call | solution.py:318
  2.6 10.1 %all-to-all-start = ((bf16[16,208,128]{2,1,0:T(8,128)(2,1)}), bf16[16,208,128]{2,1,0:T(8,128)(2,1)S(1)}, u32[]{:S(2)}, u32[]{:S(2)}) async-start(bf16[16,208,128]{2,1,0:T(8,128)(2,1)} %shard_map.59), calls=%async_computation | async-start | bytes 1703936 | tf_op jit(solution)/shard_map/all_to_all | solution.py:362
  12.7 0.1 stack.38.place_ref
  12.7 0.0 copy-done.1
  12.7 0.5 shard_map.60
  13.3 2.8 %collective-permute-start.2 = (bf16[6,8,256]{2,1,0:T(8,128)(2,1)S(1)}, bf16[6,8,256]{2,1,0:T(8,128)(2,1)S(1)}, u32[]{:S(2)}, u32[]{:S(2)}) collective-permute-start(bf16[6,8,256]{2,1,0:T(8,128)(2,1)S(1)} %shard_map.60), channel_id=1, source_target_pairs={{0,3},{1,0},{2,1},{3,2},{4,7},{5,4},{6,5},{7,6},{8,11},{9,8},{10,9... | collective-permute-start | bytes 73736 | tf_op jit(solution)/shard_map/ppermute | solution.py:359
  16.1 0.3 collective-permute-start.1
  16.5 0.7 collective-permute-start
  17.2 0.0 collective-permute-done.2
  17.2 3.2 %collective-permute-done.1 = bf16[6,8,256]{2,1,0:T(8,128)(2,1)S(1)} collective-permute-done((bf16[6,8,256]{2,1,0:T(8,128)(2,1)S(1)}, bf16[6,8,256]{2,1,0:T(8,128)(2,1)S(1)}, u32[]{:S(2)}, u32[]{:S(2)}) %collective-permute-start.1) | collective-permute-done | bytes 24608 | tf_op jit(solution)/shard_map/ppermute | solution.py:359
  20.3 0.5 collective-permute-done
  20.9 2.5 %collective-permute-start.4 = (bf16[4,6,8,256]{3,2,1,0:T(8,128)(2,1)S(1)}, bf16[4,6,8,256]{3,2,1,0:T(8,128)(2,1)S(1)}, u32[]{:S(2)}, u32[]{:S(2)}) collective-permute-start(bf16[4,6,8,256]{3,2,1,0:T(8,128)(2,1)S(1)} %pad_maximum_fusion.near_ref), channel_id=1, source_target_pairs={{0,4},{4,0},{1,5},{5,1},{2,6},{6,2},{3,7},{7,3},{8,12},{12,8},{9,1... | collective-permute-start | bytes 294920 | tf_op jit(solution)/shard_map/ppermute | solution.py:361
  23.4 2.4 %collective-permute-start.3 = (bf16[4,6,8,256]{3,2,1,0:T(8,128)(2,1)S(1)}, bf16[4,6,8,256]{3,2,1,0:T(8,128)(2,1)S(1)}, u32[]{:S(2)}, u32[]{:S(2)}) collective-permute-start(bf16[4,6,8,256]{3,2,1,0:T(8,128)(2,1)S(1)} %pad_maximum_fusion.near_ref), channel_id=1, source_target_pairs={{0,8},{8,0},{1,9},{9,1},{2,10},{10,2},{3,11},{11,3},{4,12},{12,4},... | collective-permute-start | bytes 294920 | tf_op jit(solution)/shard_map/ppermute | solution.py:366
  25.9 1.2 %collective-permute-done.4.far_ref = bf16[4,6,8,256]{3,2,1,0:T(8,128)(2,1)S(1)} collective-permute-done((bf16[4,6,8,256]{3,2,1,0:T(8,128)(2,1)S(1)}, bf16[4,6,8,256]{3,2,1,0:T(8,128)(2,1)S(1)}, u32[]{:S(2)}, u32[]{:S(2)}) %collective-permute-start.4) | collective-permute-done | bytes 98336 | tf_op jit(solution)/shard_map/ppermute | solution.py:361
  27.1 3.3 %collective-permute-start.5 = (bf16[4,6,8,256]{3,2,1,0:T(8,128)(2,1)S(1)}, bf16[4,6,8,256]{3,2,1,0:T(8,128)(2,1)S(1)}, u32[]{:S(2)}, u32[]{:S(2)}) collective-permute-start(bf16[4,6,8,256]{3,2,1,0:T(8,128)(2,1)S(1)} %collective-permute-done.4.far_ref), channel_id=1, source_target_pairs={{0,8},{8,0},{1,9},{9,1},{2,10},{10,2},{3,11},{11,3},{4,12},{12,4},... | collective-permute-start | bytes 294920 | tf_op jit(solution)/shard_map/ppermute | solution.py:366
  30.4 0.0 collective-permute-done.3.near_cross_ref
  30.4 0.9 collective-permute-done.5.far_cross_ref
  31.3 0.0 copy-done
  31.3 3.2 %shard_map.61.passages_ref = bf16[768,1024]{1,0:T(8,128)(2,1)S(1)} custom-call(s32[5]{0:T(128)S(1)} %stack.38.place_ref, s32[96,1024]{1,0:T(8,128)S(1)} %bitcast.13, bf16[4,6,8,256]{3,2,1,0:T(8,128)(2,1)S(1)} %pad_maximum_fusion.near_ref, bf16[4,6,8,256]{3,2,1,0:T(8,128)(2,1)S(1)} %collective-permute-done.3.near_cross_ref, ...), custom_call_target="tpu_custom_call" | custom-call | flops 1000000 | bytes 65536 | tf_op jit(solution)/shard_map/pallas_call | solution.py:318
  34.6 0.0 all-to-all-done.pack_ref.own_ref
  34.6 1.5 %collective-permute-start.6 = (bf16[16,208,128]{2,1,0:T(8,128)(2,1)S(1)}, bf16[16,208,128]{2,1,0:T(8,128)(2,1)S(1)}, u32[]{:S(2)}, u32[]{:S(2)}) collective-permute-start(bf16[16,208,128]{2,1,0:T(8,128)(2,1)S(1)} %all-to-all-done.pack_ref.own_ref), channel_id=1, source_target_pairs={{0,8},{8,0},{1,9},{9,1},{2,10},{10,2},{3,11},{11,3},{4,12},{12,4},... | collective-permute-start | bytes 2555912 | tf_op jit(solution)/shard_map/ppermute | solution.py:371
  36.1 1.3 %shard_map.62.own_logs_ref = f32[4,128]{1,0:T(4,128)S(1)} custom-call(bf16[16,208,128]{2,1,0:T(8,128)(2,1)S(1)} %all-to-all-done.pack_ref.own_ref, bf16[768,1024]{1,0:T(8,128)(2,1)S(1)} %shard_map.61.passages_ref), custom_call_target="tpu_custom_call" | custom-call | flops 1000000 | bytes 65536 | tf_op jit(solution)/shard_map/pallas_call | solution.py:318
  37.4 0.7 collective-permute-done.6.pack_ref.other_ref
  38.1 1.3 %shard_map.63 = f32[32,8,128]{2,1,0:T(8,128)S(1)} custom-call(bf16[16,208,128]{2,1,0:T(8,128)(2,1)S(1)} %collective-permute-done.6.pack_ref.other_ref, bf16[768,1024]{1,0:T(8,128)(2,1)S(1)} %shard_map.61.passages_ref, f32[4,128]{1,0:T(4,128)S(1)} %shard_map.62.own_logs_ref), custom_call_target="tpu_custom_call" | custom-call | flops 1000000 | bytes 65536 | tf_op jit(solution)/shard_map/pallas_call | solution.py:318
  39.4 17.4 %all_to_all.20.stats_ref = f32[32,8,128]{2,1,0:T(8,128)S(1)} all-to-all(f32[32,8,128]{2,1,0:T(8,128)S(1)} %shard_map.63), channel_id=1, replica_groups=mesh['xl'=2,'z'=8,'core'=2,'xh'=2,'y'=4] {'xl','z','core'}, dimensions={0} | all-to-all | bytes 262144 | tf_op jit(solution)/shard_map/all_to_all | solution.py:374
  56.8 9.1 %shard_map.64 = (f32[512,768]{1,0:T(8,128)S(1)}, f32[512,768]{1,0:T(8,128)S(1)}, bf16[768,1024]{1,0:T(8,128)(2,1)S(1)}) custom-call(s32[5]{0:T(128)S(1)} %stack.38.place_ref, f32[32,8,128]{2,1,0:T(8,128)S(1)} %all_to_all.20.stats_ref, bf16[16,208,128]{2,1,0:T(8,128)(2,1)S(1)} %all-to-all-done.pack_ref.own_ref, ...), custom_call_target="tpu_custom_call" | custom-call | flops 1000000 | bytes 65536 | tf_op jit(solution)/shard_map/pallas_call | solution.py:318
  65.9 1.7 %collective-permute-start.7 = (f32[512,768]{1,0:T(8,128)S(1)}, f32[512,768]{1,0:T(8,128)S(1)}, u32[]{:S(2)}, u32[]{:S(2)}) collective-permute-start(f32[512,768]{1,0:T(8,128)S(1)} %get-tuple-element.14), channel_id=1, source_target_pairs={{0,8},{8,0},{1,9},{9,1},{2,10},{10,2},{3,11},{11,3},{4,12},{12,4},... | collective-permute-start | bytes 4718600 | tf_op jit(solution)/shard_map/ppermute | solution.py:388
  67.6 2.4 %shard_map.66 = f32[8,2,3,16,128]{4,3,2,1,0:T(8,128)S(1)} custom-call(s32[5]{0:T(128)S(1)} %stack.38.place_ref, bf16[768,1024]{1,0:T(8,128)(2,1)S(1)} %get-tuple-element.15.grads_ref, s32[96,1024]{1,0:T(8,128)S(1)} %bitcast.14), custom_call_target="tpu_custom_call" | custom-call | flops 1000000 | bytes 65536 | tf_op jit(solution)/shard_map/pallas_call | solution.py:318
  70.0 0.1 collective-permute-start.8
  70.0 0.6 collective-permute-done.7.cross_ref
  70.6 2.7 %shard_map.65 = (f32[8,2,3,16,128]{4,3,2,1,0:T(8,128)S(1)}, s16[8,208,128]{2,1,0:T(8,128)(2,1)S(1)}) custom-call(s32[5]{0:T(128)S(1)} %stack.38.place_ref, bf16[768,1024]{1,0:T(8,128)(2,1)S(1)} %get-tuple-element.15.grads_ref, s32[96,1024]{1,0:T(8,128)S(1)} %bitcast.15, f32[512,768]{1,0:T(8,128)S(1)} %get-tuple-element.13.sums_ref, ...), custom_call_target="tpu_custom_call" | custom-call | flops 1000000 | bytes 65536 | tf_op jit(solution)/shard_map/pallas_call | solution.py:318
  73.3 0.0 collective-permute-done.8
  73.3 0.1 add.11
  73.4 0.3 collective-permute-start.9
  73.6 17.4 %all_to_all.21.parts_ref = f32[16,3,16,128]{3,2,1,0:T(8,128)S(1)} all-to-all(f32[16,3,16,128]{3,2,1,0:T(8,128)S(1)} %bitcast.17), channel_id=1, replica_groups=mesh['xl'=2,'z'=8,'core'=2,'xh'=2,'y'=4] {'xh','y','xl'}, dimensions={0} | all-to-all | bytes 786432 | tf_op jit(solution)/shard_map/all_to_all | solution.py:402
  91.0 0.0 collective-permute-done.9.words_ref
  91.1 1.2 %shard_map.67 = s16[8,256,128]{2,1,0:T(8,128)(2,1)S(1)} custom-call(s32[5]{0:T(128)S(1)} %stack.38.place_ref, f32[512,768]{1,0:T(8,128)S(1)} %get-tuple-element.13.sums_ref, f32[512,768]{1,0:T(8,128)S(1)} %collective-permute-done.7.cross_ref, s16[8,208,128]{2,1,0:T(8,128)(2,1)S(1)} %collective-permute-done.9.words_ref, ...), custom_call_target="tpu_custom_call" | custom-call | flops 1000000 | bytes 65536 | tf_op jit(solution)/shard_map/pallas_call | solution.py:318
  92.3 17.8 %all_to_all.22.words_ref = s16[8,256,128]{2,1,0:T(8,128)(2,1)S(1)} all-to-all(s16[8,256,128]{2,1,0:T(8,128)(2,1)S(1)} %shard_map.67), channel_id=1, replica_groups=mesh['xl'=2,'z'=8,'core'=2,'xh'=2,'y'=4] {'z'}, dimensions={0} | all-to-all | bytes 1048576 | tf_op jit(solution)/shard_map/all_to_all | solution.py:411
  110.0 0.2 shard_map.69.own_ref
  110.3 4.0 %collective-permute-start.12 = (f32[48,128]{1,0:T(8,128)S(1)}, f32[48,128]{1,0:T(8,128)S(1)}, u32[]{:S(2)}, u32[]{:S(2)}) collective-permute-start(f32[48,128]{1,0:T(8,128)S(1)} %shard_map.69.own_ref), channel_id=1, source_target_pairs={{0,136},{8,128},{128,8},{136,0},{1,137},{9,129},{129,9},{137,1},{2... | collective-permute-start | bytes 73736 | tf_op jit(solution)/shard_map/ppermute | solution.py:414
  114.2 0.0 collective-permute-start.11
  114.2 0.6 collective-permute-start.10
  114.8 0.8 shard_map.68
  115.7 0.1 collective-permute-done.12.corner_ref
  115.7 0.0 collective-permute-done.11.cross_ref
  115.7 1.2 collective-permute-done.10.beside_ref
  116.9 1.3 %shard_map.70 = f32[12,8,256]{2,1,0:T(8,128)} custom-call(s32[5]{0:T(128)S(1)} %stack.38.place_ref, f32[48,128]{1,0:T(8,128)S(1)} %shard_map.69.own_ref, f32[48,128]{1,0:T(8,128)S(1)} %collective-permute-done.10.beside_ref, f32[48,128]{1,0:T(8,128)S(1)} %collective-permute-done.11.cross_ref, f32[48,128]{1,0:T(8,128)S(1)} %collective-permute-done.12.corner_ref), custom_call_target="tpu_custom_call" | custom-call | flops 1000000 | bytes 65536 | tf_op jit(solution)/shard_map/pallas_call | solution.py:318
  (1 shorter events, 0.0 us)
Async XLA Ops:
  0.6 12.1 %copy-start.1 = (bf16[12,8,256]{2,1,0:T(8,128)(2,1)S(1)}, bf16[12,8,256]{2,1,0:T(8,128)(2,1)}, u32[]{:S(2)}) copy-start(bf16[12,8,256]{2,1,0:T(8,128)(2,1)} %book_ref.1) | copy-start | bytes 147460
  0.6 30.7 %copy-start = (s32[1,96,1024]{2,1,0:T(8,128)S(1)}, s32[1,96,1024]{2,1,0:T(8,128)}, u32[]{:S(2)}) copy-start(s32[1,96,1024]{2,1,0:T(8,128)} %param.5) | copy-start | bytes 1179652
  2.6 32.0 %all-to-all-start = ((bf16[16,208,128]{2,1,0:T(8,128)(2,1)}), bf16[16,208,128]{2,1,0:T(8,128)(2,1)S(1)}, u32[]{:S(2)}, u32[]{:S(2)}) async-start(bf16[16,208,128]{2,1,0:T(8,128)(2,1)} %shard_map.59), calls=%async_computation | async-start | bytes 1703936 | tf_op jit(solution)/shard_map/all_to_all | solution.py:362
  13.3 3.9 %collective-permute-start.2 = (bf16[6,8,256]{2,1,0:T(8,128)(2,1)S(1)}, bf16[6,8,256]{2,1,0:T(8,128)(2,1)S(1)}, u32[]{:S(2)}, u32[]{:S(2)}) collective-permute-start(bf16[6,8,256]{2,1,0:T(8,128)(2,1)S(1)} %shard_map.60), channel_id=1, source_target_pairs={{0,3},{1,0},{2,1},{3,2},{4,7},{5,4},{6,5},{7,6},{8,11},{9,8},{10,9... | collective-permute-start | bytes 73736 | tf_op jit(solution)/shard_map/ppermute | solution.py:359
  16.1 4.2 %collective-permute-start.1 = (bf16[6,8,256]{2,1,0:T(8,128)(2,1)S(1)}, bf16[6,8,256]{2,1,0:T(8,128)(2,1)S(1)}, u32[]{:S(2)}, u32[]{:S(2)}) collective-permute-start(bf16[6,8,256]{2,1,0:T(8,128)(2,1)S(1)} %shard_map.60), channel_id=1, source_target_pairs={{0,2},{1,3},{2,0},{3,1},{4,6},{5,7},{6,4},{7,5},{8,10},{9,11},{10,... | collective-permute-start | bytes 73736 | tf_op jit(solution)/shard_map/ppermute | solution.py:359
  16.5 4.4 %collective-permute-start = (bf16[6,8,256]{2,1,0:T(8,128)(2,1)S(1)}, bf16[6,8,256]{2,1,0:T(8,128)(2,1)S(1)}, u32[]{:S(2)}, u32[]{:S(2)}) collective-permute-start(bf16[6,8,256]{2,1,0:T(8,128)(2,1)S(1)} %shard_map.60), channel_id=1, source_target_pairs={{0,1},{1,2},{2,3},{3,0},{4,5},{5,6},{6,7},{7,4},{8,9},{9,10},{10,1... | collective-permute-start | bytes 73736 | tf_op jit(solution)/shard_map/ppermute | solution.py:359
  20.9 6.2 %collective-permute-start.4 = (bf16[4,6,8,256]{3,2,1,0:T(8,128)(2,1)S(1)}, bf16[4,6,8,256]{3,2,1,0:T(8,128)(2,1)S(1)}, u32[]{:S(2)}, u32[]{:S(2)}) collective-permute-start(bf16[4,6,8,256]{3,2,1,0:T(8,128)(2,1)S(1)} %pad_maximum_fusion.near_ref), channel_id=1, source_target_pairs={{0,4},{4,0},{1,5},{5,1},{2,6},{6,2},{3,7},{7,3},{8,12},{12,8},{9,1... | collective-permute-start | bytes 294920 | tf_op jit(solution)/shard_map/ppermute | solution.py:361
  23.4 7.0 %collective-permute-start.3 = (bf16[4,6,8,256]{3,2,1,0:T(8,128)(2,1)S(1)}, bf16[4,6,8,256]{3,2,1,0:T(8,128)(2,1)S(1)}, u32[]{:S(2)}, u32[]{:S(2)}) collective-permute-start(bf16[4,6,8,256]{3,2,1,0:T(8,128)(2,1)S(1)} %pad_maximum_fusion.near_ref), channel_id=1, source_target_pairs={{0,8},{8,0},{1,9},{9,1},{2,10},{10,2},{3,11},{11,3},{4,12},{12,4},... | collective-permute-start | bytes 294920 | tf_op jit(solution)/shard_map/ppermute | solution.py:366
  27.1 4.2 %collective-permute-start.5 = (bf16[4,6,8,256]{3,2,1,0:T(8,128)(2,1)S(1)}, bf16[4,6,8,256]{3,2,1,0:T(8,128)(2,1)S(1)}, u32[]{:S(2)}, u32[]{:S(2)}) collective-permute-start(bf16[4,6,8,256]{3,2,1,0:T(8,128)(2,1)S(1)} %collective-permute-done.4.far_ref), channel_id=1, source_target_pairs={{0,8},{8,0},{1,9},{9,1},{2,10},{10,2},{3,11},{11,3},{4,12},{12,4},... | collective-permute-start | bytes 294920 | tf_op jit(solution)/shard_map/ppermute | solution.py:366
  34.6 3.5 %collective-permute-start.6 = (bf16[16,208,128]{2,1,0:T(8,128)(2,1)S(1)}, bf16[16,208,128]{2,1,0:T(8,128)(2,1)S(1)}, u32[]{:S(2)}, u32[]{:S(2)}) collective-permute-start(bf16[16,208,128]{2,1,0:T(8,128)(2,1)S(1)} %all-to-all-done.pack_ref.own_ref), channel_id=1, source_target_pairs={{0,8},{8,0},{1,9},{9,1},{2,10},{10,2},{3,11},{11,3},{4,12},{12,4},... | collective-permute-start | bytes 2555912 | tf_op jit(solution)/shard_map/ppermute | solution.py:371
  65.9 4.8 %collective-permute-start.7 = (f32[512,768]{1,0:T(8,128)S(1)}, f32[512,768]{1,0:T(8,128)S(1)}, u32[]{:S(2)}, u32[]{:S(2)}) collective-permute-start(f32[512,768]{1,0:T(8,128)S(1)} %get-tuple-element.14), channel_id=1, source_target_pairs={{0,8},{8,0},{1,9},{9,1},{2,10},{10,2},{3,11},{11,3},{4,12},{12,4},... | collective-permute-start | bytes 4718600 | tf_op jit(solution)/shard_map/ppermute | solution.py:388
  70.0 3.3 %collective-permute-start.8 = (f32[8,2,3,16,128]{4,3,2,1,0:T(8,128)S(1)}, f32[8,2,3,16,128]{4,3,2,1,0:T(8,128)S(1)}, u32[]{:S(2)}, u32[]{:S(2)}) collective-permute-start(f32[8,2,3,16,128]{4,3,2,1,0:T(8,128)S(1)} %shard_map.66), channel_id=1, source_target_pairs={{0,8},{8,0},{1,9},{9,1},{2,10},{10,2},{3,11},{11,3},{4,12},{12,4},... | collective-permute-start | bytes 1179656 | tf_op jit(solution)/shard_map/ppermute | solution.py:391
  73.4 17.7 %collective-permute-start.9 = (s16[8,208,128]{2,1,0:T(8,128)(2,1)S(1)}, s16[8,208,128]{2,1,0:T(8,128)(2,1)S(1)}, u32[]{:S(2)}, u32[]{:S(2)}) collective-permute-start(s16[8,208,128]{2,1,0:T(8,128)(2,1)S(1)} %get-tuple-element.18), channel_id=1, source_target_pairs={{0,128},{128,0},{1,129},{129,1},{2,130},{130,2},{3,131},{131,3},{4... | collective-permute-start | bytes 1277960 | tf_op jit(solution)/shard_map/ppermute | solution.py:401
  110.3 5.5 %collective-permute-start.12 = (f32[48,128]{1,0:T(8,128)S(1)}, f32[48,128]{1,0:T(8,128)S(1)}, u32[]{:S(2)}, u32[]{:S(2)}) collective-permute-start(f32[48,128]{1,0:T(8,128)S(1)} %shard_map.69.own_ref), channel_id=1, source_target_pairs={{0,136},{8,128},{128,8},{136,0},{1,137},{9,129},{129,9},{137,1},{2... | collective-permute-start | bytes 73736 | tf_op jit(solution)/shard_map/ppermute | solution.py:414
  114.2 1.5 %collective-permute-start.11 = (f32[48,128]{1,0:T(8,128)S(1)}, f32[48,128]{1,0:T(8,128)S(1)}, u32[]{:S(2)}, u32[]{:S(2)}) collective-permute-start(f32[48,128]{1,0:T(8,128)S(1)} %shard_map.69.own_ref), channel_id=1, source_target_pairs={{0,8},{8,0},{1,9},{9,1},{2,10},{10,2},{3,11},{11,3},{4,12},{12,4},... | collective-permute-start | bytes 73736 | tf_op jit(solution)/shard_map/ppermute | solution.py:415
  114.2 2.7 %collective-permute-start.10 = (f32[48,128]{1,0:T(8,128)S(1)}, f32[48,128]{1,0:T(8,128)S(1)}, u32[]{:S(2)}, u32[]{:S(2)}) collective-permute-start(f32[48,128]{1,0:T(8,128)S(1)} %shard_map.69.own_ref), channel_id=1, source_target_pairs={{0,128},{128,0},{1,129},{129,1},{2,130},{130,2},{3,131},{131,3},{4... | collective-permute-start | bytes 73736 | tf_op jit(solution)/shard_map/ppermute | solution.py:413

commit v9 on v8

--- a/solution.py
+++ b/solution.py
@@ -347,7 +347,7 @@
         10**6,
         scratch=[pltpu.VMEM((length, LANES), bf16), pltpu.SemaphoreType.DMA((chips,))],
         out_special={0: ANYWHERE},
-        vmem=60,
+        vmem=12,
     )
     share = call(
         share_kernel,

time: 118 us -> 119 us (level)
  local copies, waits for them, and re-layouts: 0.09 us -> 1.59 us
    unnamed x4 -> x8, local copies, waits for them, and re-layouts: 0.01 us -> 1.5 us
where the time goes in v9:
time: 119 us
  blocking collectives  52.5 us (44%)
  starting transfers between devices  30.3 us (25%)
  Pallas kernels  25 us (21%)
  waiting for transfers between devices  8.46 us (7%)
  local copies, waits for them, and re-layouts  1.59 us (1%)
    pallas_call x12, Pallas kernels, call(): pl.pallas_call(kernel, out_shape=shapes, in_specs=specs, out_specs=outs i...  25 us
    all_to_all x1, blocking collectives, per_device(): words = lax.all_to_all(words, 'z', 0, 0)  17.8 us
    all_to_all x1, blocking collectives, per_device(): lax.all_to_all(parts.reshape(16, subspaces // 32, 16, LANES), SUB + ('xl'...  17.4 us
    all_to_all x1, blocking collectives, per_device(): stats = lax.all_to_all(stats, CHIP + ('core',), 0, 0, tiled=True)  17.4 us
    all_to_all x1, starting transfers between devices, per_device(): own = lax.all_to_all(own, CHIP, 0, 0)  10.1 us
    ppermute x1, starting transfers between devices, per_device(): corner = lax.ppermute(sums, ('xl', 'core'), [(i, 3 - i) for i in range(4)])  3.96 us
    ppermute x3, starting transfers between devices, per_device(): lax.ppermute(share, 'y', [(i, (i + k) % 4) for i in range(4)])  3.85 us
    ppermute x3, waiting for transfers between devices, per_device(): lax.ppermute(share, 'y', [(i, (i + k) % 4) for i in range(4)])  3.7 us
  transfers between devices with their start and end apart: 14, of which 8 were waited for; matrix products, arithmetic and copies ran while one was open for 0% of the time, Pallas kernels for 9%

profile of v9, /device:TPU:1, one launch (start us, length us, event | category | flops | bytes accessed | tf_op | source)
XLA Modules:
  0.0 118.7 jit_solution(10951610277712053108)
XLA Ops:
  0.6 0.0 copy-start
  0.6 0.0 copy-start.1
  0.7 0.8 copy-done.1
  1.5 0.0 copy-start.3
  1.5 0.7 copy-done.3
  2.1 0.0 copy-start.2
  2.1 1.1 shard_map.59
  3.2 10.1 %all-to-all-start = ((bf16[16,208,128]{2,1,0:T(8,128)(2,1)}), bf16[16,208,128]{2,1,0:T(8,128)(2,1)S(1)}, u32[]{:S(2)}, u32[]{:S(2)}) async-start(bf16[16,208,128]{2,1,0:T(8,128)(2,1)} %shard_map.59), calls=%async_computation | async-start | bytes 1703936 | tf_op jit(solution)/shard_map/all_to_all | solution.py:362
  13.3 0.1 stack.38.place_ref
  13.4 0.0 copy-done.2
  13.4 0.5 shard_map.60
  13.9 2.8 %collective-permute-start.2 = (bf16[6,8,256]{2,1,0:T(8,128)(2,1)S(1)}, bf16[6,8,256]{2,1,0:T(8,128)(2,1)S(1)}, u32[]{:S(2)}, u32[]{:S(2)}) collective-permute-start(bf16[6,8,256]{2,1,0:T(8,128)(2,1)S(1)} %shard_map.60), channel_id=1, source_target_pairs={{0,3},{1,0},{2,1},{3,2},{4,7},{5,4},{6,5},{7,6},{8,11},{9,8},{10,9... | collective-permute-start | bytes 73736 | tf_op jit(solution)/shard_map/ppermute | solution.py:359
  16.8 0.3 collective-permute-start.1
  17.1 0.7 collective-permute-start
  17.8 0.0 collective-permute-done.2
  17.8 3.2 %collective-permute-done.1 = bf16[6,8,256]{2,1,0:T(8,128)(2,1)S(1)} collective-permute-done((bf16[6,8,256]{2,1,0:T(8,128)(2,1)S(1)}, bf16[6,8,256]{2,1,0:T(8,128)(2,1)S(1)}, u32[]{:S(2)}, u32[]{:S(2)}) %collective-permute-start.1) | collective-permute-done | bytes 24608 | tf_op jit(solution)/shard_map/ppermute | solution.py:359
  20.9 0.5 collective-permute-done
  21.5 2.5 %collective-permute-start.4 = (bf16[4,6,8,256]{3,2,1,0:T(8,128)(2,1)S(1)}, bf16[4,6,8,256]{3,2,1,0:T(8,128)(2,1)S(1)}, u32[]{:S(2)}, u32[]{:S(2)}) collective-permute-start(bf16[4,6,8,256]{3,2,1,0:T(8,128)(2,1)S(1)} %pad_maximum_fusion.near_ref), channel_id=1, source_target_pairs={{0,4},{4,0},{1,5},{5,1},{2,6},{6,2},{3,7},{7,3},{8,12},{12,8},{9,1... | collective-permute-start | bytes 294920 | tf_op jit(solution)/shard_map/ppermute | solution.py:361
  24.0 2.4 %collective-permute-start.3 = (bf16[4,6,8,256]{3,2,1,0:T(8,128)(2,1)S(1)}, bf16[4,6,8,256]{3,2,1,0:T(8,128)(2,1)S(1)}, u32[]{:S(2)}, u32[]{:S(2)}) collective-permute-start(bf16[4,6,8,256]{3,2,1,0:T(8,128)(2,1)S(1)} %pad_maximum_fusion.near_ref), channel_id=1, source_target_pairs={{0,8},{8,0},{1,9},{9,1},{2,10},{10,2},{3,11},{11,3},{4,12},{12,4},... | collective-permute-start | bytes 294920 | tf_op jit(solution)/shard_map/ppermute | solution.py:366
  26.5 1.2 %collective-permute-done.4.far_ref = bf16[4,6,8,256]{3,2,1,0:T(8,128)(2,1)S(1)} collective-permute-done((bf16[4,6,8,256]{3,2,1,0:T(8,128)(2,1)S(1)}, bf16[4,6,8,256]{3,2,1,0:T(8,128)(2,1)S(1)}, u32[]{:S(2)}, u32[]{:S(2)}) %collective-permute-start.4) | collective-permute-done | bytes 98336 | tf_op jit(solution)/shard_map/ppermute | solution.py:361
  27.7 3.3 %collective-permute-start.5 = (bf16[4,6,8,256]{3,2,1,0:T(8,128)(2,1)S(1)}, bf16[4,6,8,256]{3,2,1,0:T(8,128)(2,1)S(1)}, u32[]{:S(2)}, u32[]{:S(2)}) collective-permute-start(bf16[4,6,8,256]{3,2,1,0:T(8,128)(2,1)S(1)} %collective-permute-done.4.far_ref), channel_id=1, source_target_pairs={{0,8},{8,0},{1,9},{9,1},{2,10},{10,2},{3,11},{11,3},{4,12},{12,4},... | collective-permute-start | bytes 294920 | tf_op jit(solution)/shard_map/ppermute | solution.py:366
  31.0 0.0 collective-permute-done.3.near_cross_ref
  31.0 0.9 collective-permute-done.5.far_cross_ref
  32.0 0.0 copy-done
  32.0 3.2 %shard_map.61.passages_ref = bf16[768,1024]{1,0:T(8,128)(2,1)S(1)} custom-call(s32[5]{0:T(128)S(1)} %stack.38.place_ref, s32[96,1024]{1,0:T(8,128)S(1)} %bitcast.13, bf16[4,6,8,256]{3,2,1,0:T(8,128)(2,1)S(1)} %pad_maximum_fusion.near_ref, bf16[4,6,8,256]{3,2,1,0:T(8,128)(2,1)S(1)} %collective-permute-done.3.near_cross_ref, ...), custom_call_target="tpu_custom_call" | custom-call | flops 1000000 | bytes 65536 | tf_op jit(solution)/shard_map/pallas_call | solution.py:318
  35.2 0.0 all-to-all-done.pack_ref.own_ref
  35.2 1.5 %collective-permute-start.6 = (bf16[16,208,128]{2,1,0:T(8,128)(2,1)S(1)}, bf16[16,208,128]{2,1,0:T(8,128)(2,1)S(1)}, u32[]{:S(2)}, u32[]{:S(2)}) collective-permute-start(bf16[16,208,128]{2,1,0:T(8,128)(2,1)S(1)} %all-to-all-done.pack_ref.own_ref), channel_id=1, source_target_pairs={{0,8},{8,0},{1,9},{9,1},{2,10},{10,2},{3,11},{11,3},{4,12},{12,4},... | collective-permute-start | bytes 2555912 | tf_op jit(solution)/shard_map/ppermute | solution.py:371
  36.7 1.3 %shard_map.62.own_logs_ref = f32[4,128]{1,0:T(4,128)S(1)} custom-call(bf16[16,208,128]{2,1,0:T(8,128)(2,1)S(1)} %all-to-all-done.pack_ref.own_ref, bf16[768,1024]{1,0:T(8,128)(2,1)S(1)} %shard_map.61.passages_ref), custom_call_target="tpu_custom_call" | custom-call | flops 1000000 | bytes 65536 | tf_op jit(solution)/shard_map/pallas_call | solution.py:318
  38.0 0.7 collective-permute-done.6.pack_ref.other_ref
  38.7 1.3 %shard_map.63 = f32[32,8,128]{2,1,0:T(8,128)S(1)} custom-call(bf16[16,208,128]{2,1,0:T(8,128)(2,1)S(1)} %collective-permute-done.6.pack_ref.other_ref, bf16[768,1024]{1,0:T(8,128)(2,1)S(1)} %shard_map.61.passages_ref, f32[4,128]{1,0:T(4,128)S(1)} %shard_map.62.own_logs_ref), custom_call_target="tpu_custom_call" | custom-call | flops 1000000 | bytes 65536 | tf_op jit(solution)/shard_map/pallas_call | solution.py:318
  40.0 17.4 %all_to_all.20.stats_ref = f32[32,8,128]{2,1,0:T(8,128)S(1)} all-to-all(f32[32,8,128]{2,1,0:T(8,128)S(1)} %shard_map.63), channel_id=1, replica_groups=mesh['xl'=2,'z'=8,'core'=2,'xh'=2,'y'=4] {'xl','z','core'}, dimensions={0} | all-to-all | bytes 262144 | tf_op jit(solution)/shard_map/all_to_all | solution.py:374
  57.4 9.0 %shard_map.64 = (f32[512,768]{1,0:T(8,128)S(1)}, f32[512,768]{1,0:T(8,128)S(1)}, bf16[768,1024]{1,0:T(8,128)(2,1)S(1)}) custom-call(s32[5]{0:T(128)S(1)} %stack.38.place_ref, f32[32,8,128]{2,1,0:T(8,128)S(1)} %all_to_all.20.stats_ref, bf16[16,208,128]{2,1,0:T(8,128)(2,1)S(1)} %all-to-all-done.pack_ref.own_ref, ...), custom_call_target="tpu_custom_call" | custom-call | flops 1000000 | bytes 65536 | tf_op jit(solution)/shard_map/pallas_call | solution.py:318
  66.4 1.7 %collective-permute-start.7 = (f32[512,768]{1,0:T(8,128)S(1)}, f32[512,768]{1,0:T(8,128)S(1)}, u32[]{:S(2)}, u32[]{:S(2)}) collective-permute-start(f32[512,768]{1,0:T(8,128)S(1)} %get-tuple-element.14), channel_id=1, source_target_pairs={{0,8},{8,0},{1,9},{9,1},{2,10},{10,2},{3,11},{11,3},{4,12},{12,4},... | collective-permute-start | bytes 4718600 | tf_op jit(solution)/shard_map/ppermute | solution.py:388
  68.2 2.4 %shard_map.66 = f32[8,2,3,16,128]{4,3,2,1,0:T(8,128)S(1)} custom-call(s32[5]{0:T(128)S(1)} %stack.38.place_ref, bf16[768,1024]{1,0:T(8,128)(2,1)S(1)} %get-tuple-element.15.grads_ref, s32[96,1024]{1,0:T(8,128)S(1)} %bitcast.14), custom_call_target="tpu_custom_call" | custom-call | flops 1000000 | bytes 65536 | tf_op jit(solution)/shard_map/pallas_call | solution.py:318
  70.6 0.1 collective-permute-start.8
  70.6 0.6 collective-permute-done.7.cross_ref
  71.2 2.6 %shard_map.65 = (f32[8,2,3,16,128]{4,3,2,1,0:T(8,128)S(1)}, s16[8,208,128]{2,1,0:T(8,128)(2,1)S(1)}) custom-call(s32[5]{0:T(128)S(1)} %stack.38.place_ref, bf16[768,1024]{1,0:T(8,128)(2,1)S(1)} %get-tuple-element.15.grads_ref, s32[96,1024]{1,0:T(8,128)S(1)} %bitcast.15, f32[512,768]{1,0:T(8,128)S(1)} %get-tuple-element.13.sums_ref, ...), custom_call_target="tpu_custom_call" | custom-call | flops 1000000 | bytes 65536 | tf_op jit(solution)/shard_map/pallas_call | solution.py:318
  73.8 0.0 collective-permute-done.8
  73.9 0.1 add.11
  73.9 0.3 collective-permute-start.9
  74.2 17.4 %all_to_all.21.parts_ref = f32[16,3,16,128]{3,2,1,0:T(8,128)S(1)} all-to-all(f32[16,3,16,128]{3,2,1,0:T(8,128)S(1)} %bitcast.18), channel_id=1, replica_groups=mesh['xl'=2,'z'=8,'core'=2,'xh'=2,'y'=4] {'xh','y','xl'}, dimensions={0} | all-to-all | bytes 786432 | tf_op jit(solution)/shard_map/all_to_all | solution.py:402
  91.6 0.0 collective-permute-done.9.words_ref
  91.6 1.2 shard_map.67
  92.8 17.8 %all_to_all.22.words_ref = s16[8,256,128]{2,1,0:T(8,128)(2,1)S(1)} all-to-all(s16[8,256,128]{2,1,0:T(8,128)(2,1)S(1)} %shard_map.67), channel_id=1, replica_groups=mesh['xl'=2,'z'=8,'core'=2,'xh'=2,'y'=4] {'z'}, dimensions={0} | all-to-all | bytes 1048576 | tf_op jit(solution)/shard_map/all_to_all | solution.py:411
  110.6 0.2 shard_map.69.own_ref
  110.8 4.0 %collective-permute-start.12 = (f32[48,128]{1,0:T(8,128)S(1)}, f32[48,128]{1,0:T(8,128)S(1)}, u32[]{:S(2)}, u32[]{:S(2)}) collective-permute-start(f32[48,128]{1,0:T(8,128)S(1)} %shard_map.69.own_ref), channel_id=1, source_target_pairs={{0,136},{8,128},{128,8},{136,0},{1,137},{9,129},{129,9},{137,1},{2... | collective-permute-start | bytes 73736 | tf_op jit(solution)/shard_map/ppermute | solution.py:414
  114.8 0.0 collective-permute-start.11
  114.8 0.6 collective-permute-start.10
  115.3 0.8 shard_map.68
  116.2 0.1 collective-permute-done.12.corner_ref
  116.3 0.0 collective-permute-done.11.cross_ref
  116.3 1.2 collective-permute-done.10.beside_ref
  117.4 1.3 %shard_map.70 = f32[12,8,256]{2,1,0:T(8,128)} custom-call(s32[5]{0:T(128)S(1)} %stack.38.place_ref, f32[48,128]{1,0:T(8,128)S(1)} %shard_map.69.own_ref, f32[48,128]{1,0:T(8,128)S(1)} %collective-permute-done.10.beside_ref, f32[48,128]{1,0:T(8,128)S(1)} %collective-permute-done.11.cross_ref, f32[48,128]{1,0:T(8,128)S(1)} %collective-permute-done.12.corner_ref), custom_call_target="tpu_custom_call" | custom-call | flops 1000000 | bytes 65536 | tf_op jit(solution)/shard_map/pallas_call | solution.py:318
  (1 shorter events, 0.0 us)
Async XLA Ops:
  0.6 31.3 %copy-start = (s32[1,96,1024]{2,1,0:T(8,128)S(1)}, s32[1,96,1024]{2,1,0:T(8,128)}, u32[]{:S(2)}) copy-start(s32[1,96,1024]{2,1,0:T(8,128)} %param.5) | copy-start | bytes 1179652
  0.6 0.8 copy-start.1
  1.5 0.7 copy-start.3
  2.1 11.2 %copy-start.2 = (bf16[12,8,256]{2,1,0:T(8,128)(2,1)S(1)}, bf16[12,8,256]{2,1,0:T(8,128)(2,1)}, u32[]{:S(2)}) copy-start(bf16[12,8,256]{2,1,0:T(8,128)(2,1)} %book_ref.1) | copy-start | bytes 147460
  3.2 32.0 %all-to-all-start = ((bf16[16,208,128]{2,1,0:T(8,128)(2,1)}), bf16[16,208,128]{2,1,0:T(8,128)(2,1)S(1)}, u32[]{:S(2)}, u32[]{:S(2)}) async-start(bf16[16,208,128]{2,1,0:T(8,128)(2,1)} %shard_map.59), calls=%async_computation | async-start | bytes 1703936 | tf_op jit(solution)/shard_map/all_to_all | solution.py:362
  13.9 3.9 %collective-permute-start.2 = (bf16[6,8,256]{2,1,0:T(8,128)(2,1)S(1)}, bf16[6,8,256]{2,1,0:T(8,128)(2,1)S(1)}, u32[]{:S(2)}, u32[]{:S(2)}) collective-permute-start(bf16[6,8,256]{2,1,0:T(8,128)(2,1)S(1)} %shard_map.60), channel_id=1, source_target_pairs={{0,3},{1,0},{2,1},{3,2},{4,7},{5,4},{6,5},{7,6},{8,11},{9,8},{10,9... | collective-permute-start | bytes 73736 | tf_op jit(solution)/shard_map/ppermute | solution.py:359
  16.8 4.2 %collective-permute-start.1 = (bf16[6,8,256]{2,1,0:T(8,128)(2,1)S(1)}, bf16[6,8,256]{2,1,0:T(8,128)(2,1)S(1)}, u32[]{:S(2)}, u32[]{:S(2)}) collective-permute-start(bf16[6,8,256]{2,1,0:T(8,128)(2,1)S(1)} %shard_map.60), channel_id=1, source_target_pairs={{0,2},{1,3},{2,0},{3,1},{4,6},{5,7},{6,4},{7,5},{8,10},{9,11},{10,... | collective-permute-start | bytes 73736 | tf_op jit(solution)/shard_map/ppermute | solution.py:359
  17.1 4.4 %collective-permute-start = (bf16[6,8,256]{2,1,0:T(8,128)(2,1)S(1)}, bf16[6,8,256]{2,1,0:T(8,128)(2,1)S(1)}, u32[]{:S(2)}, u32[]{:S(2)}) collective-permute-start(bf16[6,8,256]{2,1,0:T(8,128)(2,1)S(1)} %shard_map.60), channel_id=1, source_target_pairs={{0,1},{1,2},{2,3},{3,0},{4,5},{5,6},{6,7},{7,4},{8,9},{9,10},{10,1... | collective-permute-start | bytes 73736 | tf_op jit(solution)/shard_map/ppermute | solution.py:359
  21.5 6.2 %collective-permute-start.4 = (bf16[4,6,8,256]{3,2,1,0:T(8,128)(2,1)S(1)}, bf16[4,6,8,256]{3,2,1,0:T(8,128)(2,1)S(1)}, u32[]{:S(2)}, u32[]{:S(2)}) collective-permute-start(bf16[4,6,8,256]{3,2,1,0:T(8,128)(2,1)S(1)} %pad_maximum_fusion.near_ref), channel_id=1, source_target_pairs={{0,4},{4,0},{1,5},{5,1},{2,6},{6,2},{3,7},{7,3},{8,12},{12,8},{9,1... | collective-permute-start | bytes 294920 | tf_op jit(solution)/shard_map/ppermute | solution.py:361
  24.0 7.0 %collective-permute-start.3 = (bf16[4,6,8,256]{3,2,1,0:T(8,128)(2,1)S(1)}, bf16[4,6,8,256]{3,2,1,0:T(8,128)(2,1)S(1)}, u32[]{:S(2)}, u32[]{:S(2)}) collective-permute-start(bf16[4,6,8,256]{3,2,1,0:T(8,128)(2,1)S(1)} %pad_maximum_fusion.near_ref), channel_id=1, source_target_pairs={{0,8},{8,0},{1,9},{9,1},{2,10},{10,2},{3,11},{11,3},{4,12},{12,4},... | collective-permute-start | bytes 294920 | tf_op jit(solution)/shard_map/ppermute | solution.py:366
  27.7 4.2 %collective-permute-start.5 = (bf16[4,6,8,256]{3,2,1,0:T(8,128)(2,1)S(1)}, bf16[4,6,8,256]{3,2,1,0:T(8,128)(2,1)S(1)}, u32[]{:S(2)}, u32[]{:S(2)}) collective-permute-start(bf16[4,6,8,256]{3,2,1,0:T(8,128)(2,1)S(1)} %collective-permute-done.4.far_ref), channel_id=1, source_target_pairs={{0,8},{8,0},{1,9},{9,1},{2,10},{10,2},{3,11},{11,3},{4,12},{12,4},... | collective-permute-start | bytes 294920 | tf_op jit(solution)/shard_map/ppermute | solution.py:366
  35.2 3.5 %collective-permute-start.6 = (bf16[16,208,128]{2,1,0:T(8,128)(2,1)S(1)}, bf16[16,208,128]{2,1,0:T(8,128)(2,1)S(1)}, u32[]{:S(2)}, u32[]{:S(2)}) collective-permute-start(bf16[16,208,128]{2,1,0:T(8,128)(2,1)S(1)} %all-to-all-done.pack_ref.own_ref), channel_id=1, source_target_pairs={{0,8},{8,0},{1,9},{9,1},{2,10},{10,2},{3,11},{11,3},{4,12},{12,4},... | collective-permute-start | bytes 2555912 | tf_op jit(solution)/shard_map/ppermute | solution.py:371
  66.4 4.8 %collective-permute-start.7 = (f32[512,768]{1,0:T(8,128)S(1)}, f32[512,768]{1,0:T(8,128)S(1)}, u32[]{:S(2)}, u32[]{:S(2)}) collective-permute-start(f32[512,768]{1,0:T(8,128)S(1)} %get-tuple-element.14), channel_id=1, source_target_pairs={{0,8},{8,0},{1,9},{9,1},{2,10},{10,2},{3,11},{11,3},{4,12},{12,4},... | collective-permute-start | bytes 4718600 | tf_op jit(solution)/shard_map/ppermute | solution.py:388
  70.6 3.3 %collective-permute-start.8 = (f32[8,2,3,16,128]{4,3,2,1,0:T(8,128)S(1)}, f32[8,2,3,16,128]{4,3,2,1,0:T(8,128)S(1)}, u32[]{:S(2)}, u32[]{:S(2)}) collective-permute-start(f32[8,2,3,16,128]{4,3,2,1,0:T(8,128)S(1)} %shard_map.66), channel_id=1, source_target_pairs={{0,8},{8,0},{1,9},{9,1},{2,10},{10,2},{3,11},{11,3},{4,12},{12,4},... | collective-permute-start | bytes 1179656 | tf_op jit(solution)/shard_map/ppermute | solution.py:391
  73.9 17.7 %collective-permute-start.9 = (s16[8,208,128]{2,1,0:T(8,128)(2,1)S(1)}, s16[8,208,128]{2,1,0:T(8,128)(2,1)S(1)}, u32[]{:S(2)}, u32[]{:S(2)}) collective-permute-start(s16[8,208,128]{2,1,0:T(8,128)(2,1)S(1)} %get-tuple-element.18), channel_id=1, source_target_pairs={{0,128},{128,0},{1,129},{129,1},{2,130},{130,2},{3,131},{131,3},{4... | collective-permute-start | bytes 1277960 | tf_op jit(solution)/shard_map/ppermute | solution.py:401
  110.8 5.5 %collective-permute-start.12 = (f32[48,128]{1,0:T(8,128)S(1)}, f32[48,128]{1,0:T(8,128)S(1)}, u32[]{:S(2)}, u32[]{:S(2)}) collective-permute-start(f32[48,128]{1,0:T(8,128)S(1)} %shard_map.69.own_ref), channel_id=1, source_target_pairs={{0,136},{8,128},{128,8},{136,0},{1,137},{9,129},{129,9},{137,1},{2... | collective-permute-start | bytes 73736 | tf_op jit(solution)/shard_map/ppermute | solution.py:414
  114.8 1.5 %collective-permute-start.11 = (f32[48,128]{1,0:T(8,128)S(1)}, f32[48,128]{1,0:T(8,128)S(1)}, u32[]{:S(2)}, u32[]{:S(2)}) collective-permute-start(f32[48,128]{1,0:T(8,128)S(1)} %shard_map.69.own_ref), channel_id=1, source_target_pairs={{0,8},{8,0},{1,9},{9,1},{2,10},{10,2},{3,11},{11,3},{4,12},{12,4},... | collective-permute-start | bytes 73736 | tf_op jit(solution)/shard_map/ppermute | solution.py:415
  114.8 2.7 %collective-permute-start.10 = (f32[48,128]{1,0:T(8,128)S(1)}, f32[48,128]{1,0:T(8,128)S(1)}, u32[]{:S(2)}, u32[]{:S(2)}) collective-permute-start(f32[48,128]{1,0:T(8,128)S(1)} %shard_map.69.own_ref), channel_id=1, source_target_pairs={{0,128},{128,0},{1,129},{129,1},{2,130},{130,2},{3,131},{131,3},{4... | collective-permute-start | bytes 73736 | tf_op jit(solution)/shard_map/ppermute | solution.py:413
